TPU v7x, 512 devices: a whole 4x4x16 slice. The times are simulated.
512 devices in a mesh: dp: 32 (over z, core), expert: 16 (over y, x).
Axes of the slice: x: 4, y: 4, z: 16, core: 2. Of those that a mesh axis runs over, the one named last changes fastest.
Arguments:
- tokens: bfloat16 [65536, 2048], P(('dp', 'expert')), may hold values from -6 to 6
- routes: int32 [65536, 2], P(('dp', 'expert')), may hold values from 0 to 15, all different within a row; in each aligned block of 128 rows (0 to 127, 128 to 255, ...) at most 18 rows name the same one
- gates: float32 [65536, 2], P(('dp', 'expert')), may hold values from 0.2 to 1
- cotangent: bfloat16 [65536, 2048], P(('dp', 'expert')), may hold values from -6 to 6
- up_weight: bfloat16 [16, 2048, 384], P('expert', 'dp'), may hold values from -0.125 to 0.125
- down_weight: bfloat16 [16, 2048, 384], P('expert', 'dp'), may hold values from -0.3125 to 0.3125
Outputs:
- mixed: bfloat16 [65536, 2048], P(('dp', 'expert'))
- input_grad: bfloat16 [65536, 2048], P(('dp', 'expert'))
- up_grad: bfloat16 [16, 2048, 384], P('expert', 'dp')
- down_grad: bfloat16 [16, 2048, 384], P('expert', 'dp')
Inputs may be any that keep to these rules, and one draw needn't show every extreme that they name: `routes`: each row names two different experts; in each device's block of 128 rows no expert is named by more than 18 rows, a bound that some block reaches.
All inputs are finite; a program needn't handle non-finite values.
Results may differ from a plain program's by a relative error of at most 0.03.
Values may be sent and summed in bfloat16 or wider, within the bound.
No kernel may reach another device: no remote copies, remote signals or barrier semaphores. Data moves between devices by JAX's collectives and lax.ppermute only.
A program may use at most 64 MiB of HBM per device.

v0:
```python
import jax
import jax.numpy as jnp
from jax import lax
from jax.sharding import PartitionSpec as P


def contract_rows(left, right):
    return lax.dot_general(
        left, right, (((0,), (0,)), ((), ())), preferred_element_type=jnp.float32
    )


def contract_last(left, right):
    return lax.dot_general(
        left, right, (((1,), (1,)), ((), ())), preferred_element_type=jnp.float32
    )


def local(tokens, routes, gates, cotangent, up_weight, down_weight):
    tok_rows = tokens.shape[0]
    width = tokens.shape[1]
    hidden = up_weight.shape[2]
    experts = lax.axis_size("expert")
    capacity = 9 * tok_rows // (4 * experts)
    slot_rows = experts * capacity
    flat = routes.reshape(-1)
    onehot = (flat[:, None] == jnp.arange(experts, dtype=jnp.int32)[None, :]).astype(jnp.int32)
    earlier = jnp.cumsum(onehot, axis=0) - onehot
    slot = jnp.sum(earlier * onehot, axis=1)
    target = flat * capacity + slot
    dispatch_table = (jnp.arange(slot_rows, dtype=jnp.int32)[:, None] == target[None, :]).astype(
        jnp.bfloat16
    )
    pair_tokens = jnp.broadcast_to(tokens[:, None, :], (tok_rows, 2, width)).reshape(
        2 * tok_rows, width
    )
    pair_grads = (
        (gates[:, :, None] * cotangent[:, None, :].astype(jnp.float32))
        .astype(jnp.bfloat16)
        .reshape(2 * tok_rows, width)
    )
    send_tokens = (
        jnp.dot(dispatch_table, pair_tokens, preferred_element_type=jnp.float32)
        .astype(jnp.bfloat16)
        .reshape(experts, capacity, width)
    )
    send_grads = (
        jnp.dot(dispatch_table, pair_grads, preferred_element_type=jnp.float32)
        .astype(jnp.bfloat16)
        .reshape(experts, capacity, width)
    )
    recv_tokens = lax.all_to_all(send_tokens, "expert", split_axis=0, concat_axis=0, tiled=True)
    token_slots = recv_tokens.reshape(slot_rows, width)
    columns = token_slots
    hpre = jnp.dot(
        columns,
        lax.all_gather(up_weight, "dp", axis=1, tiled=True)[0],
        preferred_element_type=jnp.float32,
    )
    act = jax.nn.silu(hpre).astype(jnp.bfloat16)
    out_slots = contract_last(act, lax.all_gather(down_weight, "dp", axis=1, tiled=True)[0])
    out_slots = out_slots.astype(jnp.bfloat16).reshape(experts, capacity, width)
    back_out = lax.all_to_all(out_slots, "expert", split_axis=0, concat_axis=0, tiled=True)
    pair_out = contract_rows(dispatch_table, back_out.reshape(slot_rows, width)).reshape(
        tok_rows, 2, width
    )
    mixed = jnp.sum(gates[:, :, None] * pair_out, axis=1).astype(jnp.bfloat16)
    recv_grads = lax.all_to_all(send_grads, "expert", split_axis=0, concat_axis=0, tiled=True)
    grad_slots = recv_grads.reshape(slot_rows, width)
    columns = grad_slots
    dact = jnp.dot(
        columns,
        lax.all_gather(down_weight, "dp", axis=1, tiled=True)[0],
        preferred_element_type=jnp.float32,
    )
    sigma = jax.nn.sigmoid(hpre)
    dh = (dact * sigma * (1.0 + hpre * (1.0 - sigma))).astype(jnp.bfloat16)
    dx_slots = contract_last(dh, lax.all_gather(up_weight, "dp", axis=1, tiled=True)[0])
    dx_slots = dx_slots.astype(jnp.bfloat16).reshape(experts, capacity, width)
    back_dx = lax.all_to_all(dx_slots, "expert", split_axis=0, concat_axis=0, tiled=True)
    pair_dx = contract_rows(dispatch_table, back_dx.reshape(slot_rows, width)).reshape(
        tok_rows, 2, width
    )
    input_grad = jnp.sum(pair_dx, axis=1).astype(jnp.bfloat16)
    summed = lax.psum_scatter(
        jnp.concatenate(
            [contract_rows(token_slots, dh), contract_rows(grad_slots, act)], axis=1
        ).astype(jnp.bfloat16),
        "dp",
        scatter_dimension=0,
        tiled=True,
    ).astype(jnp.float32)
    up_grad = summed[:, :hidden].astype(jnp.bfloat16)[None]
    down_grad = summed[:, hidden:].astype(jnp.bfloat16)[None]
    return (mixed, input_grad, up_grad, down_grad)


def solution(mesh):
    return jax.shard_map(
        local,
        mesh=mesh,
        in_specs=(
            P(("dp", "expert"), None),
            P(("dp", "expert"), None),
            P(("dp", "expert"), None),
            P(("dp", "expert"), None),
            P("expert", "dp", None),
            P("expert", "dp", None),
        ),
        out_specs=(
            P(("dp", "expert"), None),
            P(("dp", "expert"), None),
            P("expert", "dp", None),
            P("expert", "dp", None),
        ),
        check_vma=False,
    )
```

profile of v0, /device:TPU:1, one launch (start us, length us, event | category | flops | bytes accessed | tf_op | source)
XLA Modules:
  0.0 280.1 jit_solution(13232220424088196125)
XLA Ops:
  10.6 1.7 broadcast_in_dim.6
  13.3 1.4 reshape.113
  14.6 7.8 %all-to-all-start = ((bf16[16,18,2048]{2,1,0:T(8,128)(2,1)}), bf16[16,18,2048]{2,1,0:T(8,128)(2,1)}, u32[]{:S(2)}, u32[]{:S(2)}) async-start(bf16[16,18,2048]{2,1,0:T(8,128)(2,1)} %reshape.113), calls=%async_computation | async-start | bytes 3145728 | tf_op jit(solution)/shard_map/all_to_all | solution.py:52
  22.4 1.0 mul.60
  23.5 2.5 mul.61
  26.2 2.2 convolution_convert_fusion.3
  28.4 1.3 reshape.117
  29.7 12.4 %all-to-all-done = bf16[16,18,2048]{2,1,0:T(8,128)(2,1)} async-done(((bf16[16,18,2048]{2,1,0:T(8,128)(2,1)}), bf16[16,18,2048]{2,1,0:T(8,128)(2,1)}, u32[]{:S(2)}, u32[]{:S(2)}) %all-to-all-start) | async-done | bytes 1179680 | tf_op jit(solution)/shard_map/all_to_all | solution.py:52
  42.1 5.5 %all-to-all-start.2 = ((bf16[16,18,2048]{2,1,0:T(8,128)(2,1)}), bf16[16,18,2048]{2,1,0:T(8,128)(2,1)S(1)}, u32[]{:S(2)}, u32[]{:S(2)}) async-start(bf16[16,18,2048]{2,1,0:T(8,128)(2,1)} %reshape.117), calls=%async_computation.2 | async-start | bytes 3145728 | tf_op jit(solution)/shard_map/all_to_all | solution.py:68
  47.6 1.6 reshape.114
  49.2 18.0 %all-to-all-done.2 = bf16[16,18,2048]{2,1,0:T(8,128)(2,1)S(1)} async-done(((bf16[16,18,2048]{2,1,0:T(8,128)(2,1)}), bf16[16,18,2048]{2,1,0:T(8,128)(2,1)S(1)}, u32[]{:S(2)}, u32[]{:S(2)}) %all-to-all-start.2) | async-done | bytes 1179680 | tf_op jit(solution)/shard_map/all_to_all | solution.py:68
  67.2 1.2 reshape.118
  68.4 18.8 %all-gather.3.cloned.1.call-done = bf16[1,2048,384]{2,1,0:T(8,128)(2,1)} async-done(((bf16[1,64,384]{2,1,0:T(8,128)(2,1)}), bf16[1,2048,384]{2,1,0:T(8,128)(2,1)}) %all-gather.3.cloned.1.call-update) | async-done | bytes 1572880 | tf_op jit(solution)/shard_map/all_gather | solution.py:57
  87.2 2.2 fusion.4
  89.4 2.2 convolution_convert_fusion
  91.6 66.1 %all-gather.5.cloned.1.call-done = bf16[1,2048,384]{2,1,0:T(8,128)(2,1)} async-done(((bf16[1,64,384]{2,1,0:T(8,128)(2,1)}), bf16[1,2048,384]{2,1,0:T(8,128)(2,1)}) %all-gather.5.cloned.1.call-update) | async-done | bytes 1572880 | tf_op jit(solution)/shard_map/all_gather | solution.py:61
  157.7 2.2 fusion.13
  159.9 1.0 convolution_convert_fusion.1
  161.6 2.8 %copy.28 = bf16[2048,768]{1,0:T(8,128)(2,1)} copy(bf16[2048,768]{0,1:T(8,128)(2,1)S(1)} %pad_maximum_fusion) | data formatting | bytes 6291456
  164.4 1.4 copy-done.5
  166.7 1.3 reshape.115
  168.0 6.5 %all-to-all-start.1 = ((bf16[16,18,2048]{2,1,0:T(8,128)(2,1)}), bf16[16,18,2048]{2,1,0:T(8,128)(2,1)S(1)}, u32[]{:S(2)}, u32[]{:S(2)}) async-start(bf16[16,18,2048]{2,1,0:T(8,128)(2,1)} %reshape.115), calls=%async_computation.1 | async-start | bytes 3145728 | tf_op jit(solution)/shard_map/all_to_all | solution.py:63
  174.6 2.2 convolution_convert_fusion.2
  176.8 1.4 reshape.119
  178.1 21.0 %all-to-all-done.1 = bf16[16,18,2048]{2,1,0:T(8,128)(2,1)S(1)} async-done(((bf16[16,18,2048]{2,1,0:T(8,128)(2,1)}), bf16[16,18,2048]{2,1,0:T(8,128)(2,1)S(1)}, u32[]{:S(2)}, u32[]{:S(2)}) %all-to-all-start.1) | async-done | bytes 1179680 | tf_op jit(solution)/shard_map/all_to_all | solution.py:63
  199.1 3.8 %all-to-all-start.3 = ((bf16[16,18,2048]{2,1,0:T(8,128)(2,1)}), bf16[16,18,2048]{2,1,0:T(8,128)(2,1)S(1)}, u32[]{:S(2)}, u32[]{:S(2)}) async-start(bf16[16,18,2048]{2,1,0:T(8,128)(2,1)} %reshape.119), calls=%async_computation.3 | async-start | bytes 3145728 | tf_op jit(solution)/shard_map/all_to_all | solution.py:80
  203.4 1.2 reshape.121
  204.6 20.0 %all-to-all-done.3 = bf16[16,18,2048]{2,1,0:T(8,128)(2,1)S(1)} async-done(((bf16[16,18,2048]{2,1,0:T(8,128)(2,1)}), bf16[16,18,2048]{2,1,0:T(8,128)(2,1)S(1)}, u32[]{:S(2)}, u32[]{:S(2)}) %all-to-all-start.3) | async-done | bytes 1179680 | tf_op jit(solution)/shard_map/all_to_all | solution.py:80
  225.0 1.6 convolution_reduce_fusion
  226.6 1.6 fusion.6
  228.1 42.9 %reduce-scatter.4.cloned.1.call-done = bf16[64,768]{1,0:T(8,128)(2,1)} async-done(((bf16[2048,768]{1,0:T(8,128)(2,1)}), bf16[64,768]{1,0:T(8,128)(2,1)}) %reduce-scatter.4.cloned.1.call-update) | async-done | bytes 98320
  271.0 0.8 fusion.23
  (45 shorter events, 8.7 us)
Async XLA Ops:
  7.2 80.0 %all-gather.3.cloned.1.call-start = ((), (), s32[]{:S(2)}) async-start(), calls=%async_computation.5 | async-start | bytes 1622016 | tf_op jit(solution)/shard_map/all_gather | solution.py:57
  7.9 149.8 %all-gather.5.cloned.1.call-start = ((), (), s32[]{:S(2)}) async-start(), calls=%async_computation.6 | async-start | bytes 1622016 | tf_op jit(solution)/shard_map/all_gather | solution.py:61
  14.6 7.8 %copy-start.3 = (bf16[128,2048]{1,0:T(8,128)(2,1)S(1)}, bf16[128,2048]{1,0:T(8,128)(2,1)}, u32[]{:S(2)}) copy-start(bf16[128,2048]{1,0:T(8,128)(2,1)} %param.9) | copy-start | bytes 1572868
  14.6 27.4 %all-to-all-start = ((bf16[16,18,2048]{2,1,0:T(8,128)(2,1)}), bf16[16,18,2048]{2,1,0:T(8,128)(2,1)}, u32[]{:S(2)}, u32[]{:S(2)}) async-start(bf16[16,18,2048]{2,1,0:T(8,128)(2,1)} %reshape.113), calls=%async_computation | async-start | bytes 3145728 | tf_op jit(solution)/shard_map/all_to_all | solution.py:52
  23.4 2.5 copy-start.4
  42.1 25.1 %all-to-all-start.2 = ((bf16[16,18,2048]{2,1,0:T(8,128)(2,1)}), bf16[16,18,2048]{2,1,0:T(8,128)(2,1)S(1)}, u32[]{:S(2)}, u32[]{:S(2)}) async-start(bf16[16,18,2048]{2,1,0:T(8,128)(2,1)} %reshape.117), calls=%async_computation.2 | async-start | bytes 3145728 | tf_op jit(solution)/shard_map/all_to_all | solution.py:68
  47.5 223.5 %reduce-scatter.4.cloned.1.call-start = ((), (), s32[]{:S(2)}) async-start(), calls=%async_computation.7 | async-start | bytes 3244032
  68.4 21.0 %copy-start.2 = (bf16[288,2048]{1,0:T(8,128)(2,1)S(1)}, bf16[288,2048]{1,0:T(8,128)(2,1)}, u32[]{:S(2)}) copy-start(bf16[288,2048]{1,0:T(8,128)(2,1)} %reshape.118) | copy-start | bytes 3538948
  89.4 68.3 %copy-start.6 = (f32[288,384]{1,0:T(8,128)}, f32[288,384]{1,0:T(8,128)S(1)}, u32[]{:S(2)}) copy-start(f32[288,384]{1,0:T(8,128)S(1)} %fusion.4) | copy-start | bytes 1327108
  159.9 1.4 copy-start
  164.4 1.4 copy-start.5
  164.4 1.5 copy-start.7
  168.0 31.1 %all-to-all-start.1 = ((bf16[16,18,2048]{2,1,0:T(8,128)(2,1)}), bf16[16,18,2048]{2,1,0:T(8,128)(2,1)S(1)}, u32[]{:S(2)}, u32[]{:S(2)}) async-start(bf16[16,18,2048]{2,1,0:T(8,128)(2,1)} %reshape.115), calls=%async_computation.1 | async-start | bytes 3145728 | tf_op jit(solution)/shard_map/all_to_all | solution.py:63
  199.1 25.5 %all-to-all-start.3 = ((bf16[16,18,2048]{2,1,0:T(8,128)(2,1)}), bf16[16,18,2048]{2,1,0:T(8,128)(2,1)S(1)}, u32[]{:S(2)}, u32[]{:S(2)}) async-start(bf16[16,18,2048]{2,1,0:T(8,128)(2,1)} %reshape.119), calls=%async_computation.3 | async-start | bytes 3145728 | tf_op jit(solution)/shard_map/all_to_all | solution.py:80
  225.0 1.6 copy-start.1
Sparse Core Ops, SparseCore 0:
  10.1 77.0 all-gather.2
  89.3 68.3 all-gather.4
  164.5 106.4 reduce-scatter.3
where the time goes:
time: 283 us; the launch traced here: 280 us
  waiting for transfers between devices  200 us (71%)
  local copies, waits for them, and re-layouts  24.5 us (9%)
  starting transfers between devices  23.6 us (8%)
  matrix products  16.5 us (6%)
  between operations  14 us (5%)
    all_gather x1, waiting for transfers between devices, local(): lax.all_gather(down_weight, 'dp', axis=1, tiled=True)[0]  66.1 us
    unnamed x4, waiting for transfers between devices  44.3 us
    all_to_all x1, waiting for transfers between devices, local(): lax.all_to_all(out_slots, 'expert', split_axis=0, concat_axis=0, tiled=True)  21 us
    all_to_all x1, waiting for transfers between devices, local(): lax.all_to_all(dx_slots, 'expert', split_axis=0, concat_axis=0, tiled=True)  20 us
    all_gather x1, waiting for transfers between devices, local(): lax.all_gather(up_weight, 'dp', axis=1, tiled=True)[0]  18.8 us
    all_to_all x1, waiting for transfers between devices, local(): lax.all_to_all(send_grads, 'expert', split_axis=0, concat_axis=0, tiled=T...  18 us
    all_to_all x1, waiting for transfers between devices, local(): lax.all_to_all(send_tokens, 'expert', split_axis=0, concat_axis=0, tiled=...  12.4 us
    all_to_all x1, starting transfers between devices, local(): lax.all_to_all(send_tokens, 'expert', split_axis=0, concat_axis=0, tiled=...  7.75 us
  transfers between devices with their start and end apart: 7, of which 7 were waited for; matrix products, arithmetic and copies ran while one was open for 11% of the time, Pallas kernels for 0%

commit v1 on v0

v1 whole, which is shorter than its diff:
```python
import functools

import jax
import jax.numpy as jnp
from jax import lax
from jax.experimental import pallas as pl
from jax.experimental.pallas import tpu as pltpu
from jax.sharding import PartitionSpec as P

F32 = jnp.float32
BF16 = jnp.bfloat16
EXPERTS = 16
CAP = 18
BODY = 16
REST = CAP - BODY
BLOCK = 40
CORES = 2
VMEM = 56 * 1024 * 1024


def dot(left, right):
    return lax.dot_general(left, right, (((1,), (0,)), ((), ())), preferred_element_type=F32)


def contract_rows(left, right):
    return lax.dot_general(left, right, (((0,), (0,)), ((), ())), preferred_element_type=F32)


def contract_last(left, right):
    return lax.dot_general(left, right, (((1,), (1,)), ((), ())), preferred_element_type=F32)


def named_and_earlier(routes):
    tokens = routes.shape[1]
    expert = lax.broadcasted_iota(jnp.int32, (EXPERTS, tokens), 0)
    first, second = expert == routes[0:1], expert == routes[1:2]
    earlier = lax.broadcasted_iota(jnp.int32, (tokens, tokens), 0) < lax.broadcasted_iota(
        jnp.int32, (tokens, tokens), 1
    )
    named = jnp.where(first | second, 1.0, 0.0).astype(BF16)
    count = dot(named, jnp.where(earlier, 1.0, 0.0).astype(BF16))
    return first, second, count.astype(jnp.int32)


def slots_of_rows(rows, lanes):
    row = lax.broadcasted_iota(jnp.int32, (1, rows, lanes), 1)
    one = jnp.where(row < BODY, row, -1)
    one = jnp.where((row >= 2 * BODY) & (row < 2 * BODY + REST), row - BODY, one)
    two = jnp.where((row >= BODY) & (row < 2 * BODY), row - BODY, -1)
    two = jnp.where((row >= 2 * BODY + REST) & (row < 2 * BODY + 2 * REST), row - BODY - REST, two)
    return one, two


def dispatch_kernel(routes, gates, tokens, cotangent, send, table, scale):
    @pl.when(pl.program_id(0) == 0)
    def _():
        first, second, count = named_and_earlier(routes[...])
        number = count.shape[1]
        held = jnp.where(first | second, count, -2)[:, None, :]
        one, two = slots_of_rows(BLOCK, number)
        gate = jnp.where(first, gates[0:1], 0.0) + jnp.where(second, gates[1:2], 0.0)
        in_one, in_two = held == one, held == two
        table[:, :number] = jnp.where(in_one, 1.0, 0.0).reshape(EXPERTS * BLOCK, number).astype(BF16)
        table[:, number:] = jnp.where(in_two, 1.0, 0.0).reshape(EXPERTS * BLOCK, number).astype(BF16)
        factor = jnp.where(in_two, gate[:, None, :], 0.0) + jnp.where(in_one, 1.0, 0.0)
        scale[...] = jnp.sum(factor.reshape(EXPERTS * BLOCK, number), axis=1, keepdims=True)

    both = jnp.concatenate([tokens[...], cotangent[...]], axis=0)
    rows = dot(table[...], both) * scale[...]
    send[...] = rows.astype(BF16).reshape(send.shape)


def dispatch(routes, gates, tokens, cotangent):
    number, width = tokens.shape
    step = 512
    whole = lambda i: (0, 0)
    column = lambda i: (0, i)
    return pl.pallas_call(
        dispatch_kernel,
        grid=(width // step,),
        in_specs=[
            pl.BlockSpec((2, number), whole),
            pl.BlockSpec((2, number), whole),
            pl.BlockSpec((number, step), column),
            pl.BlockSpec((number, step), column),
        ],
        out_specs=pl.BlockSpec((EXPERTS, BLOCK, step), lambda i: (0, 0, i)),
        out_shape=jax.ShapeDtypeStruct((EXPERTS, BLOCK, width), BF16),
        scratch_shapes=[
            pltpu.VMEM((EXPERTS * BLOCK, 2 * number), BF16),
            pltpu.VMEM((EXPERTS * BLOCK, 1), F32),
        ],
        compiler_params=pltpu.CompilerParams(vmem_limit_bytes=VMEM),
        name="dispatch",
    )(routes, gates, tokens, cotangent)


def expert_kernel(core, received, weights, act_out, dh_out, keep, give, part):
    width = received.shape[2]
    hidden = weights.shape[1] // 2
    body = EXPERTS * BODY
    x = received[:, :BODY, :].reshape(body, width)
    g = received[:, BODY : 2 * BODY, :].reshape(body, width)
    over = received[:, 2 * BODY :, :].reshape(EXPERTS * (BLOCK - 2 * BODY), width)
    rest = over.shape[0]
    up, down = weights[:, :hidden], weights[:, hidden:]
    valid = lax.broadcasted_iota(jnp.int32, (rest, hidden), 0) % (BLOCK - 2 * BODY) < REST

    def hidden_part(hpre, dact):
        s = 1.0 / (1.0 + jnp.exp(-hpre))
        return hpre * s, dact * s * (1.0 + hpre * (1.0 - s))

    act, dh = hidden_part(dot(x, up), dot(g, down))
    act, dh = act.astype(BF16), dh.astype(BF16)
    dact_over = pltpu.roll(dot(over, down), rest - REST, 0)
    act_over, dh_over = hidden_part(dot(over, up), dact_over)
    act_over = jnp.where(valid, act_over, 0.0)
    dh_over = jnp.where(valid, dh_over, 0.0).astype(BF16)
    act_moved = pltpu.roll(act_over, REST, 0).astype(BF16)
    act_out[:body] = act
    act_out[body:] = act_over.astype(BF16)
    dh_out[:body] = dh
    dh_out[body:] = dh_over
    part[:, :hidden] = (contract_rows(x, dh) + contract_rows(over, dh_over)).astype(BF16)
    part[:, hidden:] = (contract_rows(g, act) + contract_rows(over, act_moved)).astype(BF16)
    share = keep.shape[1]
    mine = core[0]
    for z in range(keep.shape[0]):
        at = z * CORES * share
        keep[z] = part[pl.ds(pl.multiple_of(at + mine * share, share), share), :]
        give[z] = part[pl.ds(pl.multiple_of(at + (1 - mine) * share, share), share), :]


def expert(core, received, weights, share):
    width = received.shape[2]
    wide = weights.shape[1]
    rows = EXPERTS * (BLOCK - BODY)
    whole = pl.BlockSpec(memory_space=pltpu.VMEM)
    chips = width // share // CORES
    return pl.pallas_call(
        expert_kernel,
        in_specs=[pl.BlockSpec(memory_space=pltpu.SMEM), whole, whole],
        out_specs=[whole] * 4,
        out_shape=[
            jax.ShapeDtypeStruct((rows, wide // 2), BF16),
            jax.ShapeDtypeStruct((rows, wide // 2), BF16),
            jax.ShapeDtypeStruct((chips, share, wide), BF16),
            jax.ShapeDtypeStruct((chips, share, wide), BF16),
        ],
        scratch_shapes=[pltpu.VMEM((width, wide), BF16)],
        compiler_params=pltpu.CompilerParams(vmem_limit_bytes=VMEM),
        name="expert",
    )(core, received, weights)


def return_kernel(act, dh, weights, back):
    hidden = weights.shape[1] // 2
    width = weights.shape[0]
    body = EXPERTS * BODY
    up, down = weights[:, :hidden], weights[:, hidden:]
    back[:, :BODY, :] = contract_last(act[:body], down).astype(BF16).reshape(EXPERTS, BODY, width)
    back[:, BODY : 2 * BODY, :] = (
        contract_last(dh[:body], up).astype(BF16).reshape(EXPERTS, BODY, width)
    )
    over = contract_last(act[body:], down) + pltpu.roll(contract_last(dh[body:], up), REST, 0)
    back[:, 2 * BODY :, :] = over.astype(BF16).reshape(EXPERTS, BLOCK - 2 * BODY, width)


def returns(act, dh, weights):
    whole = pl.BlockSpec(memory_space=pltpu.VMEM)
    return pl.pallas_call(
        return_kernel,
        in_specs=[whole] * 3,
        out_specs=whole,
        out_shape=jax.ShapeDtypeStruct((EXPERTS, BLOCK, weights.shape[0]), BF16),
        compiler_params=pltpu.CompilerParams(vmem_limit_bytes=VMEM),
        name="returns",
    )(act, dh, weights)


def combine_kernel(routes, gates, back, mixed, input_grad, table, scale):
    number = routes.shape[1]

    @pl.when(pl.program_id(0) == 0)
    def _():
        first, second, count = named_and_earlier(routes[...])
        one, two = slots_of_rows(BLOCK, number)

        def picked(chosen, slots):
            held = jnp.where(chosen, count, -2)[:, None, :]
            return jnp.where(held == slots, 1.0, 0.0).reshape(EXPERTS * BLOCK, number).astype(BF16)

        table[:, :number] = picked(first, one)
        table[:, number : 2 * number] = picked(second, one)
        table[:, 2 * number :] = picked(first | second, two)
        here = lax.broadcasted_iota(jnp.int32, (number, number), 0) == lax.broadcasted_iota(
            jnp.int32, (number, number), 1
        )
        for k in range(2):
            scale[k] = jnp.sum(jnp.where(here, gates[k : k + 1], 0.0), axis=1, keepdims=True)

    rows = back[...].reshape(EXPERTS * BLOCK, back.shape[2])
    pairs = contract_rows(table[...], rows)
    mixed[...] = (scale[0] * pairs[:number] + scale[1] * pairs[number : 2 * number]).astype(BF16)
    input_grad[...] = pairs[2 * number :].astype(BF16)


def combine(routes, gates, back):
    number = routes.shape[1]
    width = back.shape[2]
    step = 512
    whole = lambda i: (0, 0)
    column = pl.BlockSpec((number, step), lambda i: (0, i))
    return pl.pallas_call(
        combine_kernel,
        grid=(width // step,),
        in_specs=[
            pl.BlockSpec((2, number), whole),
            pl.BlockSpec((2, number), whole),
            pl.BlockSpec((EXPERTS, BLOCK, step), lambda i: (0, 0, i)),
        ],
        out_specs=[column, column],
        out_shape=[jax.ShapeDtypeStruct((number, width), BF16)] * 2,
        scratch_shapes=[
            pltpu.VMEM((EXPERTS * BLOCK, 3 * number), BF16),
            pltpu.VMEM((2, number, 1), F32),
        ],
        compiler_params=pltpu.CompilerParams(vmem_limit_bytes=VMEM),
        name="combine",
    )(routes, gates, back)


def local(chips, tokens, routes, gates, cotangent, up_weight, down_weight):
    hidden = up_weight.shape[2]
    share = up_weight.shape[1]
    at = lambda z, core: z * CORES + core
    across = [(at(z, c), at(z, 1 - c)) for z in range(chips) for c in range(CORES)]
    along_z = [[at(z, c) for z in range(chips)] for c in range(CORES)]
    weights = lax.all_gather(
        jnp.concatenate([up_weight[0], down_weight[0]], axis=1), "dp", axis=0, tiled=True
    )
    routes, gates = routes.T, gates.T
    send = dispatch(routes, gates, tokens, cotangent)
    received = lax.all_to_all(send, "expert", split_axis=0, concat_axis=0, tiled=True)
    core = (lax.axis_index("dp") % CORES).astype(jnp.int32).reshape(1)
    act, dh, keep, give = expert(core, received, weights, share)
    got = lax.ppermute(give, "dp", across)
    chip_sum = (keep.astype(F32) + got.astype(F32)).astype(BF16)
    summed = lax.psum_scatter(
        chip_sum, "dp", scatter_dimension=0, tiled=True, axis_index_groups=along_z
    )
    back = returns(act, dh, weights)
    back = lax.all_to_all(back, "expert", split_axis=0, concat_axis=0, tiled=True)
    mixed, input_grad = combine(routes, gates, back)
    return mixed, input_grad, summed[:, :, :hidden], summed[:, :, hidden:]


def solution(mesh):
    token = P(("dp", "expert"), None)
    weight = P("expert", "dp", None)
    return jax.shard_map(
        functools.partial(local, mesh.shape["dp"] // CORES),
        mesh=mesh,
        in_specs=(token, token, token, token, weight, weight),
        out_specs=(token, token, weight, weight),
        check_vma=False,
    )
```

time: 283 us -> 183 us (0.65)
  the two profiles are of different devices: /device:TPU:1 before, /device:TPU:12 now
where the time goes in v1:
time: 183 us; the launch traced here: 182 us
  waiting for transfers between devices  88.7 us (48%)
  blocking collectives  38.1 us (21%)
  Pallas kernels  23.8 us (13%)
  between operations  14.1 us (8%)
  starting transfers between devices  11.5 us (6%)
  other arithmetic  4.54 us (2%)
    all_to_all x1, blocking collectives, local(): lax.all_to_all(back, 'expert', split_axis=0, concat_axis=0, tiled=True)  38.1 us
    all_gather x1, waiting for transfers between devices, local(): lax.all_gather(jnp.concatenate([up_weight[0], down_weight[0]], axis=1), '...  33.6 us
    all_to_all x1, waiting for transfers between devices, local(): lax.all_to_all(send, 'expert', split_axis=0, concat_axis=0, tiled=True)  31.7 us
    reduce_scatter x1, waiting for transfers between devices, local(): lax.psum_scatter(chip_sum, 'dp', scatter_dimension=0, tiled=True, axis_in...  20.1 us
    all_to_all x1, starting transfers between devices, local(): lax.all_to_all(send, 'expert', split_axis=0, concat_axis=0, tiled=True)  9.32 us
    pallas_call x1, Pallas kernels, expert(): pl.pallas_call(expert_kernel, in_specs=[pl.BlockSpec(memory_space=pltpu.S...  8.36 us
    pallas_call x1, Pallas kernels, returns(): pl.pallas_call(return_kernel, in_specs=[whole] * 3, out_specs=whole, out_...  5.8 us
    pallas_call x1, Pallas kernels, combine(): pl.pallas_call(combine_kernel, grid=(width // step,), in_specs=[pl.BlockS...  4.82 us
  transfers between devices with their start and end apart: 4, of which 4 were waited for; matrix products, arithmetic and copies ran while one was open for 0% of the time, Pallas kernels for 8%

profile of v1, /device:TPU:12, one launch (start us, length us, event | category | flops | bytes accessed | tf_op | source)
XLA Modules:
  0.0 182.2 jit_solution(7315694621441647868)
XLA Ops:
  7.2 0.0 all-gather.2.cloned.1.call-start
  7.2 1.5 pad_maximum_fusion
  8.7 0.0 all-gather.2.cloned.1.call-update
  8.7 4.8 %dispatch.1 = bf16[16,40,2048]{2,1,0:T(8,128)(2,1)} custom-call(s32[2,128]{1,0:T(2,128)} %bitcast.7, f32[2,128]{1,0:T(2,128)} %bitcast.9, bf16[128,2048]{1,0:T(8,128)(2,1)} %tokens.1, bf16[128,2048]{1,0:T(8,128)(2,1)} %cotangent.1), custom_call_target="tpu_custom_call" | custom-call | tf_op jit(solution)/shard_map/dispatch/pallas_call | solution.py:78
  13.5 9.3 %all-to-all-start = ((bf16[16,40,2048]{2,1,0:T(8,128)(2,1)}), bf16[16,40,2048]{2,1,0:T(8,128)(2,1)S(1)}, u32[]{:S(2)}, u32[]{:S(2)}) async-start(bf16[16,40,2048]{2,1,0:T(8,128)(2,1)} %dispatch.1), calls=%async_computation | async-start | bytes 5242880 | tf_op jit(solution)/shard_map/all_to_all | solution.py:244
  22.8 0.0 reduce-scatter.2.cloned.1.call-start
  22.9 31.7 %all-to-all-done.received = bf16[16,40,2048]{2,1,0:T(8,128)(2,1)S(1)} async-done(((bf16[16,40,2048]{2,1,0:T(8,128)(2,1)}), bf16[16,40,2048]{2,1,0:T(8,128)(2,1)S(1)}, u32[]{:S(2)}, u32[]{:S(2)}) %all-to-all-start) | async-done | bytes 2621472 | tf_op jit(solution)/shard_map/all_to_all | solution.py:244
  54.5 0.0 copy-start
  54.5 33.6 %all-gather.2.cloned.1.call-done.weights = bf16[2048,768]{1,0:T(8,128)(2,1)} async-done(((bf16[64,768]{1,0:T(8,128)(2,1)}), bf16[2048,768]{1,0:T(8,128)(2,1)}) %all-gather.2.cloned.1.call-update) | async-done | bytes 3145744 | tf_op jit(solution)/shard_map/all_gather | solution.py:239
  88.1 0.0 copy-done
  88.1 8.4 %expert.1 = (bf16[384,384]{1,0:T(8,128)(2,1)}, bf16[384,384]{1,0:T(8,128)(2,1)}, bf16[16,64,768]{2,1,0:T(8,128)(2,1)}, bf16[16,64,768]{2,1,0:T(8,128)(2,1)}) custom-call(s32[1]{0:T(128)} %bitcast.2.core, bf16[16,40,2048]{2,1,0:T(8,128)(2,1)} %copy-done, bf16[2048,768]{1,0:T(8,128)(2,1)} %all-gather.2.cloned.1.call-done.weights), custom_call_target="tpu_custom_call" | custom-call | tf_op jit(solution)/shard_map/expert/pallas_call | solution.py:140
  96.5 2.1 %collective-permute-start = (bf16[16,64,768]{2,1,0:T(8,128)(2,1)}, bf16[16,64,768]{2,1,0:T(8,128)(2,1)S(1)}, u32[]{:S(2)}, u32[]{:S(2)}) collective-permute-start(bf16[16,64,768]{2,1,0:T(8,128)(2,1)} %get-tuple-element.15), channel_id=1, source_target_pairs={{0,16},{16,0},{32,48},{48,32},{64,80},{80,64},{96,112},{112,96},{1... | collective-permute-start | bytes 4718600 | tf_op jit(solution)/shard_map/ppermute | solution.py:247
  98.6 3.3 %collective-permute-done = bf16[16,64,768]{2,1,0:T(8,128)(2,1)S(1)} collective-permute-done((bf16[16,64,768]{2,1,0:T(8,128)(2,1)}, bf16[16,64,768]{2,1,0:T(8,128)(2,1)S(1)}, u32[]{:S(2)}, u32[]{:S(2)}) %collective-permute-start) | collective-permute-done | bytes 1572896 | tf_op jit(solution)/shard_map/ppermute | solution.py:247
  102.0 3.1 %add_convert_fusion = bf16[16,64,768]{2,1,0:T(8,128)(2,1)} fusion(bf16[16,64,768]{2,1,0:T(8,128)(2,1)S(1)} %collective-permute-done, bf16[16,64,768]{2,1,0:T(8,128)(2,1)} %get-tuple-element.14), kind=kLoop, calls=%fused_computation | loop fusion | flops 3145728 | bytes 4718592 | tf_op jit(solution)/shard_map/convert_element_type | solution.py:248
  105.0 0.0 reduce-scatter.2.cloned.1.call-update
  105.0 5.8 %returns.1 = bf16[16,40,2048]{2,1,0:T(8,128)(2,1)} custom-call(bf16[384,384]{1,0:T(8,128)(2,1)} %get-tuple-element.10.act, bf16[384,384]{1,0:T(8,128)(2,1)} %get-tuple-element.11.dh, bf16[2048,768]{1,0:T(8,128)(2,1)} %all-gather.2.cloned.1.call-done.weights), custom_call_target="tpu_custom_call" | custom-call | tf_op jit(solution)/shard_map/returns/pallas_call | solution.py:171
  110.9 38.1 %all_to_all.10.back = bf16[16,40,2048]{2,1,0:T(8,128)(2,1)} all-to-all(bf16[16,40,2048]{2,1,0:T(8,128)(2,1)} %returns.1), channel_id=1, replica_groups=mesh['dp'=32,'expert'=16] {'expert'}, dimensions={0} | all-to-all | bytes 5242880 | tf_op jit(solution)/shard_map/all_to_all | solution.py:253
  149.0 4.8 %combine.1 = (bf16[128,2048]{1,0:T(8,128)(2,1)}, bf16[128,2048]{1,0:T(8,128)(2,1)}) custom-call(s32[2,128]{1,0:T(2,128)} %bitcast.8, f32[2,128]{1,0:T(2,128)} %bitcast.10, bf16[16,40,2048]{2,1,0:T(8,128)(2,1)} %all_to_all.10.back), custom_call_target="tpu_custom_call" | custom-call | tf_op jit(solution)/shard_map/combine/pallas_call | solution.py:214
  153.8 20.1 %reduce-scatter.2.cloned.1.call-done = bf16[1,64,768]{2,1,0:T(8,128)(2,1)} async-done(((bf16[16,64,768]{2,1,0:T(8,128)(2,1)}), bf16[1,64,768]{2,1,0:T(8,128)(2,1)}) %reduce-scatter.2.cloned.1.call-update) | async-done | bytes 98320 | tf_op jit(solution)/shard_map/reduce_scatter | solution.py:249
  173.9 1.5 fusion
Async XLA Ops:
  7.2 80.9 %all-gather.2.cloned.1.call-start = ((), (), s32[]{:S(2)}) async-start(), calls=%async_computation.3 | async-start | bytes 3244032 | tf_op jit(solution)/shard_map/all_gather | solution.py:239
  13.5 41.0 %all-to-all-start = ((bf16[16,40,2048]{2,1,0:T(8,128)(2,1)}), bf16[16,40,2048]{2,1,0:T(8,128)(2,1)S(1)}, u32[]{:S(2)}, u32[]{:S(2)}) async-start(bf16[16,40,2048]{2,1,0:T(8,128)(2,1)} %dispatch.1), calls=%async_computation | async-start | bytes 5242880 | tf_op jit(solution)/shard_map/all_to_all | solution.py:244
  22.8 151.1 %reduce-scatter.2.cloned.1.call-start = ((), (), s32[]{:S(2)}) async-start(), calls=%async_computation.4 | async-start | bytes 1671168 | tf_op jit(solution)/shard_map/reduce_scatter | solution.py:249
  54.5 33.6 %copy-start = (bf16[16,40,2048]{2,1,0:T(8,128)(2,1)}, bf16[16,40,2048]{2,1,0:T(8,128)(2,1)S(1)}, u32[]{:S(2)}) copy-start(bf16[16,40,2048]{2,1,0:T(8,128)(2,1)S(1)} %all-to-all-done.received) | copy-start | bytes 7864324
  96.5 5.5 %collective-permute-start = (bf16[16,64,768]{2,1,0:T(8,128)(2,1)}, bf16[16,64,768]{2,1,0:T(8,128)(2,1)S(1)}, u32[]{:S(2)}, u32[]{:S(2)}) collective-permute-start(bf16[16,64,768]{2,1,0:T(8,128)(2,1)} %get-tuple-element.15), channel_id=1, source_target_pairs={{0,16},{16,0},{32,48},{48,32},{64,80},{80,64},{96,112},{112,96},{1... | collective-permute-start | bytes 4718600 | tf_op jit(solution)/shard_map/ppermute | solution.py:247
Sparse Core Ops, SparseCore 0:
  10.7 77.3 all-gather.1
  105.2 68.6 reduce-scatter.1

commit v2 on v1

--- a/solution.py
+++ b/solution.py
@@ -15,7 +15,10 @@
 REST = CAP - BODY
 BLOCK = 40
 CORES = 2
-VMEM = 56 * 1024 * 1024
+NOTE = 8
+SMALL = 16 * 1024 * 1024
+LARGE = 40 * 1024 * 1024
+WHOLE = 60 * 1024 * 1024
 
 
 def dot(left, right):
@@ -51,9 +54,21 @@
     return one, two
 
 
-def dispatch_kernel(routes, gates, tokens, cotangent, send, table, scale):
+def coded(weight):
+    rows = weight.astype(F32)
+    peak = jnp.max(jnp.max(jnp.abs(rows), axis=1, keepdims=True), axis=0, keepdims=True)
+    power = jnp.floor(jnp.log2(16384.0 / jnp.maximum(peak, 2.0**-100)))
+    factor = jnp.exp2(power).astype(BF16).astype(F32)
+    code = (rows * factor).astype(BF16)
+    return jnp.concatenate([code, jnp.broadcast_to(power, (NOTE, rows.shape[1])).astype(BF16)], axis=0)
+
+
+def dispatch_kernel(routes, gates, tokens, cotangent, up, down, send, codes, table, scale):
     @pl.when(pl.program_id(0) == 0)
     def _():
+        hidden = up.shape[2]
+        codes[:, :hidden] = coded(up[0])
+        codes[:, hidden:] = coded(down[0])
         first, second, count = named_and_earlier(routes[...])
         number = count.shape[1]
         held = jnp.where(first | second, count, -2)[:, None, :]
@@ -70,8 +85,9 @@
     send[...] = rows.astype(BF16).reshape(send.shape)
 
 
-def dispatch(routes, gates, tokens, cotangent):
+def dispatch(routes, gates, tokens, cotangent, up_weight, down_weight):
     number, width = tokens.shape
+    share, hidden = up_weight.shape[1:]
     step = 512
     whole = lambda i: (0, 0)
     column = lambda i: (0, i)
@@ -83,21 +99,36 @@
             pl.BlockSpec((2, number), whole),
             pl.BlockSpec((number, step), column),
             pl.BlockSpec((number, step), column),
-        ],
-        out_specs=pl.BlockSpec((EXPERTS, BLOCK, step), lambda i: (0, 0, i)),
-        out_shape=jax.ShapeDtypeStruct((EXPERTS, BLOCK, width), BF16),
+            pl.BlockSpec((1, share, hidden), lambda i: (0, 0, 0)),
+            pl.BlockSpec((1, share, hidden), lambda i: (0, 0, 0)),
+        ],
+        out_specs=[
+            pl.BlockSpec((EXPERTS, BLOCK, step), lambda i: (0, 0, i)),
+            pl.BlockSpec((share + NOTE, 2 * hidden), whole),
+        ],
+        out_shape=[
+            jax.ShapeDtypeStruct((EXPERTS, BLOCK, width), BF16),
+            jax.ShapeDtypeStruct((share + NOTE, 2 * hidden), BF16),
+        ],
         scratch_shapes=[
             pltpu.VMEM((EXPERTS * BLOCK, 2 * number), BF16),
             pltpu.VMEM((EXPERTS * BLOCK, 1), F32),
         ],
-        compiler_params=pltpu.CompilerParams(vmem_limit_bytes=VMEM),
+        compiler_params=pltpu.CompilerParams(vmem_limit_bytes=WHOLE),
         name="dispatch",
-    )(routes, gates, tokens, cotangent)
-
-
-def expert_kernel(core, received, weights, act_out, dh_out, keep, give, part):
+    )(routes, gates, tokens, cotangent, up_weight, down_weight)
+
+
+def offset_of(r, core):
+    return (0, 1, 2 - 4 * core, -1)[r]
+
+
+def expert_kernel(place, received, codes, act_out, dh_out, weights, keep, give, part):
     width = received.shape[2]
-    hidden = weights.shape[1] // 2
+    hidden = codes.shape[2] // 2
+    rows = codes.shape[1] - NOTE
+    factor = jnp.exp2(-codes[:, rows:, :].astype(F32)).astype(BF16)[:, :1, :]
+    weights[...] = (codes[:, :rows, :] * factor).reshape(weights.shape)
     body = EXPERTS * BODY
     x = received[:, :BODY, :].reshape(body, width)
     g = received[:, BODY : 2 * BODY, :].reshape(body, width)
@@ -123,34 +154,39 @@
     dh_out[body:] = dh_over
     part[:, :hidden] = (contract_rows(x, dh) + contract_rows(over, dh_over)).astype(BF16)
     part[:, hidden:] = (contract_rows(g, act) + contract_rows(over, act_moved)).astype(BF16)
-    share = keep.shape[1]
-    mine = core[0]
-    for z in range(keep.shape[0]):
-        at = z * CORES * share
-        keep[z] = part[pl.ds(pl.multiple_of(at + mine * share, share), share), :]
-        give[z] = part[pl.ds(pl.multiple_of(at + (1 - mine) * share, share), share), :]
-
-
-def expert(core, received, weights, share):
+    near, far, share = keep.shape[:3]
+    z, mine = place[0], place[1]
+    for out, owner in ((keep, mine), (give, 1 - mine)):
+        for r in range(near):
+            for j in range(far):
+                chip = lax.rem(z + offset_of(r, owner) + near * j + near * far, near * far)
+                at = (chip * CORES + owner) * share
+                out[r, j] = part[pl.ds(pl.multiple_of(at, share), share), :]
+
+
+def expert(place, received, codes):
     width = received.shape[2]
-    wide = weights.shape[1]
+    wide = codes.shape[2]
+    share = codes.shape[1] - NOTE
     rows = EXPERTS * (BLOCK - BODY)
     whole = pl.BlockSpec(memory_space=pltpu.VMEM)
-    chips = width // share // CORES
+    near = 4
+    far = width // share // CORES // near
     return pl.pallas_call(
         expert_kernel,
         in_specs=[pl.BlockSpec(memory_space=pltpu.SMEM), whole, whole],
-        out_specs=[whole] * 4,
+        out_specs=[whole] * 5,
         out_shape=[
             jax.ShapeDtypeStruct((rows, wide // 2), BF16),
             jax.ShapeDtypeStruct((rows, wide // 2), BF16),
-            jax.ShapeDtypeStruct((chips, share, wide), BF16),
-            jax.ShapeDtypeStruct((chips, share, wide), BF16),
+            jax.ShapeDtypeStruct((width, wide), BF16),
+            jax.ShapeDtypeStruct((near, far, share, wide), BF16),
+            jax.ShapeDtypeStruct((near, far, share, wide), BF16),
         ],
         scratch_shapes=[pltpu.VMEM((width, wide), BF16)],
-        compiler_params=pltpu.CompilerParams(vmem_limit_bytes=VMEM),
+        compiler_params=pltpu.CompilerParams(vmem_limit_bytes=LARGE),
         name="expert",
-    )(core, received, weights)
+    )(place, received, codes)
 
 
 def return_kernel(act, dh, weights, back):
@@ -173,85 +209,109 @@
         in_specs=[whole] * 3,
         out_specs=whole,
         out_shape=jax.ShapeDtypeStruct((EXPERTS, BLOCK, weights.shape[0]), BF16),
-        compiler_params=pltpu.CompilerParams(vmem_limit_bytes=VMEM),
+        compiler_params=pltpu.CompilerParams(vmem_limit_bytes=LARGE),
         name="returns",
     )(act, dh, weights)
 
 
-def combine_kernel(routes, gates, back, mixed, input_grad, table, scale):
+def table_kernel(routes, gates, table, scale):
     number = routes.shape[1]
-
-    @pl.when(pl.program_id(0) == 0)
-    def _():
-        first, second, count = named_and_earlier(routes[...])
-        one, two = slots_of_rows(BLOCK, number)
-
-        def picked(chosen, slots):
-            held = jnp.where(chosen, count, -2)[:, None, :]
-            return jnp.where(held == slots, 1.0, 0.0).reshape(EXPERTS * BLOCK, number).astype(BF16)
-
-        table[:, :number] = picked(first, one)
-        table[:, number : 2 * number] = picked(second, one)
-        table[:, 2 * number :] = picked(first | second, two)
-        here = lax.broadcasted_iota(jnp.int32, (number, number), 0) == lax.broadcasted_iota(
-            jnp.int32, (number, number), 1
-        )
-        for k in range(2):
-            scale[k] = jnp.sum(jnp.where(here, gates[k : k + 1], 0.0), axis=1, keepdims=True)
-
+    first, second, count = named_and_earlier(routes[...])
+    one, two = slots_of_rows(BLOCK, number)
+
+    def picked(chosen, slots):
+        held = jnp.where(chosen, count, -2)[:, None, :]
+        return jnp.where(held == slots, 1.0, 0.0).reshape(EXPERTS * BLOCK, number).T.astype(BF16)
+
+    table[:number] = picked(first, one)
+    table[number : 2 * number] = picked(second, one)
+    table[2 * number :] = picked(first | second, two)
+    here = lax.broadcasted_iota(jnp.int32, (number, number), 0) == lax.broadcasted_iota(
+        jnp.int32, (number, number), 1
+    )
+    for k in range(2):
+        scale[k] = jnp.sum(jnp.where(here, gates[k : k + 1], 0.0), axis=1, keepdims=True)
+
+
+def tables(routes, gates):
+    number = routes.shape[1]
+    return pl.pallas_call(
+        table_kernel,
+        out_shape=[
+            jax.ShapeDtypeStruct((3 * number, EXPERTS * BLOCK), BF16),
+            jax.ShapeDtypeStruct((2, number, 1), F32),
+        ],
+        compiler_params=pltpu.CompilerParams(vmem_limit_bytes=SMALL),
+        name="tables",
+    )(routes, gates)
+
+
+def combine_kernel(table, scale, back, mixed, input_grad):
+    number = mixed.shape[0]
     rows = back[...].reshape(EXPERTS * BLOCK, back.shape[2])
-    pairs = contract_rows(table[...], rows)
+    pairs = dot(table[...], rows)
     mixed[...] = (scale[0] * pairs[:number] + scale[1] * pairs[number : 2 * number]).astype(BF16)
     input_grad[...] = pairs[2 * number :].astype(BF16)
 
 
-def combine(routes, gates, back):
-    number = routes.shape[1]
+def combine(table, scale, back):
+    number = scale.shape[1]
     width = back.shape[2]
     step = 512
-    whole = lambda i: (0, 0)
     column = pl.BlockSpec((number, step), lambda i: (0, i))
     return pl.pallas_call(
         combine_kernel,
         grid=(width // step,),
         in_specs=[
-            pl.BlockSpec((2, number), whole),
-            pl.BlockSpec((2, number), whole),
+            pl.BlockSpec(table.shape, lambda i: (0, 0)),
+            pl.BlockSpec(scale.shape, lambda i: (0, 0, 0)),
             pl.BlockSpec((EXPERTS, BLOCK, step), lambda i: (0, 0, i)),
         ],
         out_specs=[column, column],
         out_shape=[jax.ShapeDtypeStruct((number, width), BF16)] * 2,
-        scratch_shapes=[
-            pltpu.VMEM((EXPERTS * BLOCK, 3 * number), BF16),
-            pltpu.VMEM((2, number, 1), F32),
-        ],
-        compiler_params=pltpu.CompilerParams(vmem_limit_bytes=VMEM),
+        compiler_params=pltpu.CompilerParams(vmem_limit_bytes=SMALL),
         name="combine",
-    )(routes, gates, back)
+    )(table, scale, back)
 
 
 def local(chips, tokens, routes, gates, cotangent, up_weight, down_weight):
     hidden = up_weight.shape[2]
-    share = up_weight.shape[1]
-    at = lambda z, core: z * CORES + core
-    across = [(at(z, c), at(z, 1 - c)) for z in range(chips) for c in range(CORES)]
-    along_z = [[at(z, c) for z in range(chips)] for c in range(CORES)]
-    weights = lax.all_gather(
-        jnp.concatenate([up_weight[0], down_weight[0]], axis=1), "dp", axis=0, tiled=True
-    )
+    near = 4
+    far = chips // near
+
+    def moved(array, hops):
+        pairs = []
+        for z in range(chips):
+            for core in range(CORES):
+                to = z * CORES + 1 - core if hops is None else (z + hops(core)) % chips * CORES + core
+                pairs.append((z * CORES + core, to))
+        return lax.ppermute(array, "dp", pairs)
+
     routes, gates = routes.T, gates.T
-    send = dispatch(routes, gates, tokens, cotangent)
+    send, codes = dispatch(routes, gates, tokens, cotangent, up_weight, down_weight)
+    codes = lax.all_gather(codes.astype(jnp.float16), "dp").astype(BF16)
     received = lax.all_to_all(send, "expert", split_axis=0, concat_axis=0, tiled=True)
-    core = (lax.axis_index("dp") % CORES).astype(jnp.int32).reshape(1)
-    act, dh, keep, give = expert(core, received, weights, share)
-    got = lax.ppermute(give, "dp", across)
-    chip_sum = (keep.astype(F32) + got.astype(F32)).astype(BF16)
-    summed = lax.psum_scatter(
-        chip_sum, "dp", scatter_dimension=0, tiled=True, axis_index_groups=along_z
-    )
+    me = lax.axis_index("dp").astype(jnp.int32)
+    place = jnp.stack([me // CORES, me % CORES])
+    act, dh, weights, keep, give = expert(place, received, codes)
+    got = moved(give, None)
+
+    def total(*arrays):
+        return sum(a.astype(F32) for a in arrays)
+
+    quarter = total(keep[0], got[0])
+    for r in range(1, near):
+        chip_sum = total(keep[r], got[r]).astype(BF16)
+        arrived = moved(chip_sum, lambda core: offset_of(r, core))
+        quarter = quarter + arrived.astype(F32)
+    quarter = quarter.astype(BF16)
+    arrived = [moved(quarter[j], lambda core: near * j) for j in range(1, far)]
+    table, scale = tables(routes, gates)
     back = returns(act, dh, weights)
     back = lax.all_to_all(back, "expert", split_axis=0, concat_axis=0, tiled=True)
-    mixed, input_grad = combine(routes, gates, back)
+    mixed, input_grad = combine(table, scale, back)
+    mixed, input_grad, arrived = lax.optimization_barrier((mixed, input_grad, arrived))
+    summed = total(quarter[0], *arrived).astype(BF16)[None]
     return mixed, input_grad, summed[:, :, :hidden], summed[:, :, hidden:]
 
 

time: 183 us -> 145 us (0.79)
  the two profiles are of different devices: /device:TPU:12 before, /device:TPU:1 now
where the time goes in v2:
time: 145 us
  blocking collectives  48 us (33%)
  starting transfers between devices  41.7 us (29%)
  waiting for transfers between devices  28.3 us (20%)
  Pallas kernels  17.4 us (12%)
  other arithmetic  5.05 us (3%)
  local copies, waits for them, and re-layouts  3.34 us (2%)
    all_gather x1, blocking collectives, local(): codes = lax.all_gather(codes.astype(jnp.float16), 'dp').astype(BF16)  48 us
    ppermute x7, waiting for transfers between devices, moved(): return lax.ppermute(array, 'dp', pairs)  28.3 us
    ppermute x7, starting transfers between devices, moved(): return lax.ppermute(array, 'dp', pairs)  27 us
    all_to_all x1, starting transfers between devices, local(): lax.all_to_all(send, 'expert', split_axis=0, concat_axis=0, tiled=True)  7.76 us
    pallas_call x1, Pallas kernels, expert(): pl.pallas_call(expert_kernel, in_specs=[pl.BlockSpec(memory_space=pltpu.S...  7.12 us
    all_to_all x1, starting transfers between devices, local(): lax.all_to_all(back, 'expert', split_axis=0, concat_axis=0, tiled=True)  6.87 us
    pallas_call x1, Pallas kernels, dispatch(): pl.pallas_call(dispatch_kernel, grid=(width // step,), in_specs=[pl.Block...  4.77 us
    pallas_call x1, Pallas kernels, combine(): pl.pallas_call(combine_kernel, grid=(width // step,), in_specs=[pl.BlockS...  2.94 us
  transfers between devices with their start and end apart: 9, of which 5 were waited for; matrix products, arithmetic and copies ran while one was open for 3% of the time, Pallas kernels for 4%

profile of v2, /device:TPU:1, one launch (start us, length us, event | category | flops | bytes accessed | tf_op | source)
XLA Modules:
  0.0 144.6 jit_solution(9956661023707155399)
XLA Ops:
  0.6 4.8 %dispatch.1 = (bf16[16,40,2048]{2,1,0:T(8,128)(2,1)}, bf16[72,768]{1,0:T(8,128)(2,1)}) custom-call(s32[2,128]{1,0:T(2,128)} %bitcast.33, f32[2,128]{1,0:T(2,128)} %bitcast.35, bf16[128,2048]{1,0:T(8,128)(2,1)} %tokens.1, bf16[128,2048]{1,0:T(8,128)(2,1)} %cotangent.1, bf16[1,64,384]{2,1,0:T(8,128)(2,1)} %up.1, bf16[1,64,384]{2,1,0:T(8,128)(2,1)} %down.1), custom_call_target="tpu_custom_call" | custom-call | tf_op jit(solution)/shard_map/dispatch/pallas_call | solution.py:94
  5.4 7.8 %all-to-all-start = ((bf16[16,40,2048]{2,1,0:T(8,128)(2,1)}), bf16[16,40,2048]{2,1,0:T(8,128)(2,1)}, u32[]{:S(2)}, u32[]{:S(2)}) async-start(bf16[16,40,2048]{2,1,0:T(8,128)(2,1)} %get-tuple-element.22), calls=%async_computation | async-start | bytes 5242880 | tf_op jit(solution)/shard_map/all_to_all | solution.py:293
  13.2 48.0 %all-gather.2 = f16[2304,768]{1,0:T(8,128)(2,1)S(1)} all-gather(f16[72,768]{1,0:T(8,128)(2,1)S(1)} %convert_element_type.86), channel_id=2, replica_groups=mesh['dp'=32,'expert'=16] {'dp'}, dimensions={0}, use_global_device_ids=true | all-gather | bytes 3649536 | tf_op jit(solution)/shard_map/all_gather | solution.py:292
  61.2 0.6 convert_element_type.113
  61.8 0.1 pad_add_fusion.place
  61.9 0.0 all-to-all-done.received
  61.9 7.1 %expert.1 = (bf16[384,384]{1,0:T(8,128)(2,1)S(1)}, bf16[384,384]{1,0:T(8,128)(2,1)S(1)}, bf16[2048,768]{1,0:T(8,128)(2,1)S(1)}, bf16[4,4,64,768]{3,2,1,0:T(8,128)(2,1)S(1)}, bf16[4,4,64,768]{3,2,1,0:T(8,128)(2,1)}) custom-call(s32[2]{0:T(128)S(1)} %pad_add_fusion.place, bf16[16,40,2048]{2,1,0:T(8,128)(2,1)} %all-to-all-done.received, ...), custom_call_target="tpu_custom_call" | custom-call | tf_op jit(solution)/shard_map/expert/pallas_call | solution.py:175
  69.0 1.2 copy-done.1
  70.2 2.0 %collective-permute-start = (bf16[4,4,64,768]{3,2,1,0:T(8,128)(2,1)}, bf16[4,4,64,768]{3,2,1,0:T(8,128)(2,1)}, u32[]{:S(2)}, u32[]{:S(2)}) collective-permute-start(bf16[4,4,64,768]{3,2,1,0:T(8,128)(2,1)} %get-tuple-element.30), channel_id=1, source_target_pairs={{0,16},{16,0},{32,48},{48,32},{64,80},{80,64},{96,112},{112,96},{1... | collective-permute-start | bytes 4718600 | tf_op jit(solution)/shard_map/ppermute | solution.py:288
  72.2 2.2 %returns.1 = bf16[16,40,2048]{2,1,0:T(8,128)(2,1)S(1)} custom-call(bf16[384,384]{1,0:T(8,128)(2,1)S(1)} %get-tuple-element.24.act, bf16[384,384]{1,0:T(8,128)(2,1)S(1)} %get-tuple-element.25.dh, bf16[2048,768]{1,0:T(8,128)(2,1)S(1)} %get-tuple-element.26.weights), custom_call_target="tpu_custom_call" | custom-call | tf_op jit(solution)/shard_map/returns/pallas_call | solution.py:207
  74.5 1.5 %copy-done = bf16[16,40,2048]{2,1,0:T(8,128)(2,1)} copy-done((bf16[16,40,2048]{2,1,0:T(8,128)(2,1)}, bf16[16,40,2048]{2,1,0:T(8,128)(2,1)S(1)}, u32[]{:S(2)}) %copy-start) | copy-done | bytes 2621464
  75.9 6.9 %all-to-all-start.1 = ((bf16[16,40,2048]{2,1,0:T(8,128)(2,1)}), bf16[16,40,2048]{2,1,0:T(8,128)(2,1)S(1)}, u32[]{:S(2)}, u32[]{:S(2)}) async-start(bf16[16,40,2048]{2,1,0:T(8,128)(2,1)} %copy-done), calls=%async_computation.1 | async-start | bytes 5242880 | tf_op jit(solution)/shard_map/all_to_all | solution.py:311
  82.8 0.0 copy-start.2
  82.8 0.0 copy-start.3
  82.9 1.9 %fusion.3 = (bf16[4,64,768]{2,1,0:T(8,128)(2,1)S(1)}, bf16[4,64,768]{2,1,0:T(8,128)(2,1)S(1)}, bf16[4,64,768]{2,1,0:T(8,128)(2,1)S(1)}) fusion(bf16[4,4,64,768]{3,2,1,0:T(8,128)(2,1)} %collective-permute-done, bf16[4,4,64,768]{3,2,1,0:T(8,128)(2,1)} %copy-done.1), kind=kLoop, calls=%fused_computation.7 | loop fusion | flops 2359296 | bytes 3538944 | tf_op jit(solution)/shard_map/convert_element_type | solution.py:304
  84.8 1.9 %collective-permute-start.1 = (bf16[4,64,768]{2,1,0:T(8,128)(2,1)S(1)}, bf16[4,64,768]{2,1,0:T(8,128)(2,1)S(1)}, u32[]{:S(2)}, u32[]{:S(2)}) collective-permute-start(bf16[4,64,768]{2,1,0:T(8,128)(2,1)S(1)} %get-tuple-element.36), channel_id=1, source_target_pairs={{0,32},{16,48},{32,64},{48,80},{64,96},{80,112},{96,128},{112,144}... | collective-permute-start | bytes 1179656 | tf_op jit(solution)/shard_map/ppermute | solution.py:288
  86.7 3.5 %collective-permute-start.2 = (bf16[4,64,768]{2,1,0:T(8,128)(2,1)S(1)}, bf16[4,64,768]{2,1,0:T(8,128)(2,1)S(1)}, u32[]{:S(2)}, u32[]{:S(2)}) collective-permute-start(bf16[4,64,768]{2,1,0:T(8,128)(2,1)S(1)} %get-tuple-element.38), channel_id=1, source_target_pairs={{0,64},{16,464},{32,96},{48,496},{64,128},{80,16},{96,160},{112,48... | collective-permute-start | bytes 1179656 | tf_op jit(solution)/shard_map/ppermute | solution.py:288
  90.2 3.4 %collective-permute-start.3 = (bf16[4,64,768]{2,1,0:T(8,128)(2,1)S(1)}, bf16[4,64,768]{2,1,0:T(8,128)(2,1)S(1)}, u32[]{:S(2)}, u32[]{:S(2)}) collective-permute-start(bf16[4,64,768]{2,1,0:T(8,128)(2,1)S(1)} %get-tuple-element.37), channel_id=1, source_target_pairs={{0,480},{16,496},{32,0},{48,16},{64,32},{80,48},{96,64},{112,80},{... | collective-permute-start | bytes 1179656 | tf_op jit(solution)/shard_map/ppermute | solution.py:288
  93.6 4.3 %collective-permute-done.1 = bf16[4,64,768]{2,1,0:T(8,128)(2,1)S(1)} collective-permute-done((bf16[4,64,768]{2,1,0:T(8,128)(2,1)S(1)}, bf16[4,64,768]{2,1,0:T(8,128)(2,1)S(1)}, u32[]{:S(2)}, u32[]{:S(2)}) %collective-permute-start.1) | collective-permute-done | bytes 393248 | tf_op jit(solution)/shard_map/ppermute | solution.py:288
  97.9 5.2 %collective-permute-done.2 = bf16[4,64,768]{2,1,0:T(8,128)(2,1)S(1)} collective-permute-done((bf16[4,64,768]{2,1,0:T(8,128)(2,1)S(1)}, bf16[4,64,768]{2,1,0:T(8,128)(2,1)S(1)}, u32[]{:S(2)}, u32[]{:S(2)}) %collective-permute-start.2) | collective-permute-done | bytes 393248 | tf_op jit(solution)/shard_map/ppermute | solution.py:288
  103.0 7.0 %collective-permute-done.3 = bf16[4,64,768]{2,1,0:T(8,128)(2,1)S(1)} collective-permute-done((bf16[4,64,768]{2,1,0:T(8,128)(2,1)S(1)}, bf16[4,64,768]{2,1,0:T(8,128)(2,1)S(1)}, u32[]{:S(2)}, u32[]{:S(2)}) %collective-permute-start.3) | collective-permute-done | bytes 393248 | tf_op jit(solution)/shard_map/ppermute | solution.py:288
  110.0 1.4 fusion.2
  111.4 3.1 %collective-permute-start.4 = (bf16[64,768]{1,0:T(8,128)(2,1)S(1)}, bf16[64,768]{1,0:T(8,128)(2,1)}, u32[]{:S(2)}, u32[]{:S(2)}) collective-permute-start(bf16[64,768]{1,0:T(8,128)(2,1)S(1)} %get-tuple-element.41), channel_id=1, source_target_pairs={{0,128},{16,144},{32,160},{48,176},{64,192},{80,208},{96,224},{112... | collective-permute-start | bytes 294920 | tf_op jit(solution)/shard_map/ppermute | solution.py:288
  114.5 9.1 %collective-permute-start.5 = (bf16[64,768]{1,0:T(8,128)(2,1)S(1)}, bf16[64,768]{1,0:T(8,128)(2,1)}, u32[]{:S(2)}, u32[]{:S(2)}) collective-permute-start(bf16[64,768]{1,0:T(8,128)(2,1)S(1)} %get-tuple-element.40), channel_id=1, source_target_pairs={{0,256},{16,272},{32,288},{48,304},{64,320},{80,336},{96,352},{112... | collective-permute-start | bytes 294920 | tf_op jit(solution)/shard_map/ppermute | solution.py:288
  123.7 4.0 %collective-permute-start.6 = (bf16[64,768]{1,0:T(8,128)(2,1)S(1)}, bf16[64,768]{1,0:T(8,128)(2,1)}, u32[]{:S(2)}, u32[]{:S(2)}) collective-permute-start(bf16[64,768]{1,0:T(8,128)(2,1)S(1)} %get-tuple-element.39), channel_id=1, source_target_pairs={{0,384},{16,400},{32,416},{48,432},{64,448},{80,464},{96,480},{112... | collective-permute-start | bytes 294920 | tf_op jit(solution)/shard_map/ppermute | solution.py:288
  127.7 0.4 tables.1
  128.1 2.9 %combine.1 = (bf16[128,2048]{1,0:T(8,128)(2,1)}, bf16[128,2048]{1,0:T(8,128)(2,1)}) custom-call(bf16[384,640]{1,0:T(8,128)(2,1)S(1)} %get-tuple-element.20.table, f32[2,128,1]{2,1,0:T(8,128)S(1)} %get-tuple-element.21.scale, bf16[16,40,2048]{2,1,0:T(8,128)(2,1)S(1)} %all-to-all-done.1.back), custom_call_target="tpu_custom_call" | custom-call | tf_op jit(solution)/shard_map/combine/pallas_call | solution.py:262
  131.0 0.0 collective-permute-done.4
  131.1 6.1 %collective-permute-done.5 = bf16[64,768]{1,0:T(8,128)(2,1)} collective-permute-done((bf16[64,768]{1,0:T(8,128)(2,1)S(1)}, bf16[64,768]{1,0:T(8,128)(2,1)}, u32[]{:S(2)}, u32[]{:S(2)}) %collective-permute-start.5) | collective-permute-done | bytes 98336 | tf_op jit(solution)/shard_map/ppermute | solution.py:288
  137.1 5.7 %collective-permute-done.6 = bf16[64,768]{1,0:T(8,128)(2,1)} collective-permute-done((bf16[64,768]{1,0:T(8,128)(2,1)S(1)}, bf16[64,768]{1,0:T(8,128)(2,1)}, u32[]{:S(2)}, u32[]{:S(2)}) %collective-permute-start.6) | collective-permute-done | bytes 98336 | tf_op jit(solution)/shard_map/ppermute | solution.py:288
  142.9 1.1 fusion.9
  144.0 0.6 fusion.10
  (12 shorter events, 0.1 us)
Async XLA Ops:
  5.4 7.8 %copy-start.5 = (bf16[72,768]{1,0:T(8,128)(2,1)S(1)}, bf16[72,768]{1,0:T(8,128)(2,1)}, u32[]{:S(2)}) copy-start(bf16[72,768]{1,0:T(8,128)(2,1)} %get-tuple-element.23) | copy-start | bytes 331780
  5.4 56.5 %all-to-all-start = ((bf16[16,40,2048]{2,1,0:T(8,128)(2,1)}), bf16[16,40,2048]{2,1,0:T(8,128)(2,1)}, u32[]{:S(2)}, u32[]{:S(2)}) async-start(bf16[16,40,2048]{2,1,0:T(8,128)(2,1)} %get-tuple-element.22), calls=%async_computation | async-start | bytes 5242880 | tf_op jit(solution)/shard_map/all_to_all | solution.py:293
  69.0 1.2 copy-start.1
  70.2 12.6 %collective-permute-start = (bf16[4,4,64,768]{3,2,1,0:T(8,128)(2,1)}, bf16[4,4,64,768]{3,2,1,0:T(8,128)(2,1)}, u32[]{:S(2)}, u32[]{:S(2)}) collective-permute-start(bf16[4,4,64,768]{3,2,1,0:T(8,128)(2,1)} %get-tuple-element.30), channel_id=1, source_target_pairs={{0,16},{16,0},{32,48},{48,32},{64,80},{80,64},{96,112},{112,96},{1... | collective-permute-start | bytes 4718600 | tf_op jit(solution)/shard_map/ppermute | solution.py:288
  74.4 1.5 %copy-start = (bf16[16,40,2048]{2,1,0:T(8,128)(2,1)}, bf16[16,40,2048]{2,1,0:T(8,128)(2,1)S(1)}, u32[]{:S(2)}) copy-start(bf16[16,40,2048]{2,1,0:T(8,128)(2,1)S(1)} %returns.1) | copy-start | bytes 7864324
  75.9 52.2 %all-to-all-start.1 = ((bf16[16,40,2048]{2,1,0:T(8,128)(2,1)}), bf16[16,40,2048]{2,1,0:T(8,128)(2,1)S(1)}, u32[]{:S(2)}, u32[]{:S(2)}) async-start(bf16[16,40,2048]{2,1,0:T(8,128)(2,1)} %copy-done), calls=%async_computation.1 | async-start | bytes 5242880 | tf_op jit(solution)/shard_map/all_to_all | solution.py:311
  82.8 44.9 %copy-start.2 = (s32[128,2]{0,1:T(2,128)S(1)}, s32[128,2]{0,1:T(2,128)}, u32[]{:S(2)}) copy-start(s32[128,2]{0,1:T(2,128)} %param.7) | copy-start | bytes 3076
  82.8 44.9 %copy-start.3 = (f32[128,2]{0,1:T(2,128)S(1)}, f32[128,2]{0,1:T(2,128)}, u32[]{:S(2)}) copy-start(f32[128,2]{0,1:T(2,128)} %param.8) | copy-start | bytes 3076
  84.8 13.1 %collective-permute-start.1 = (bf16[4,64,768]{2,1,0:T(8,128)(2,1)S(1)}, bf16[4,64,768]{2,1,0:T(8,128)(2,1)S(1)}, u32[]{:S(2)}, u32[]{:S(2)}) collective-permute-start(bf16[4,64,768]{2,1,0:T(8,128)(2,1)S(1)} %get-tuple-element.36), channel_id=1, source_target_pairs={{0,32},{16,48},{32,64},{48,80},{64,96},{80,112},{96,128},{112,144}... | collective-permute-start | bytes 1179656 | tf_op jit(solution)/shard_map/ppermute | solution.py:288
  86.7 16.4 %collective-permute-start.2 = (bf16[4,64,768]{2,1,0:T(8,128)(2,1)S(1)}, bf16[4,64,768]{2,1,0:T(8,128)(2,1)S(1)}, u32[]{:S(2)}, u32[]{:S(2)}) collective-permute-start(bf16[4,64,768]{2,1,0:T(8,128)(2,1)S(1)} %get-tuple-element.38), channel_id=1, source_target_pairs={{0,64},{16,464},{32,96},{48,496},{64,128},{80,16},{96,160},{112,48... | collective-permute-start | bytes 1179656 | tf_op jit(solution)/shard_map/ppermute | solution.py:288
  90.2 19.8 %collective-permute-start.3 = (bf16[4,64,768]{2,1,0:T(8,128)(2,1)S(1)}, bf16[4,64,768]{2,1,0:T(8,128)(2,1)S(1)}, u32[]{:S(2)}, u32[]{:S(2)}) collective-permute-start(bf16[4,64,768]{2,1,0:T(8,128)(2,1)S(1)} %get-tuple-element.37), channel_id=1, source_target_pairs={{0,480},{16,496},{32,0},{48,16},{64,32},{80,48},{96,64},{112,80},{... | collective-permute-start | bytes 1179656 | tf_op jit(solution)/shard_map/ppermute | solution.py:288
  111.4 12.3 %copy-start.4 = (bf16[4,64,768]{2,1,0:T(8,128)(2,1)}, bf16[4,64,768]{2,1,0:T(8,128)(2,1)S(1)}, u32[]{:S(2)}) copy-start(bf16[4,64,768]{2,1,0:T(8,128)(2,1)S(1)} %fusion.2) | copy-start | bytes 1179652
  111.4 19.6 %collective-permute-start.4 = (bf16[64,768]{1,0:T(8,128)(2,1)S(1)}, bf16[64,768]{1,0:T(8,128)(2,1)}, u32[]{:S(2)}, u32[]{:S(2)}) collective-permute-start(bf16[64,768]{1,0:T(8,128)(2,1)S(1)} %get-tuple-element.41), channel_id=1, source_target_pairs={{0,128},{16,144},{32,160},{48,176},{64,192},{80,208},{96,224},{112... | collective-permute-start | bytes 294920 | tf_op jit(solution)/shard_map/ppermute | solution.py:288
  114.5 22.6 %collective-permute-start.5 = (bf16[64,768]{1,0:T(8,128)(2,1)S(1)}, bf16[64,768]{1,0:T(8,128)(2,1)}, u32[]{:S(2)}, u32[]{:S(2)}) collective-permute-start(bf16[64,768]{1,0:T(8,128)(2,1)S(1)} %get-tuple-element.40), channel_id=1, source_target_pairs={{0,256},{16,272},{32,288},{48,304},{64,320},{80,336},{96,352},{112... | collective-permute-start | bytes 294920 | tf_op jit(solution)/shard_map/ppermute | solution.py:288
  123.7 19.2 %collective-permute-start.6 = (bf16[64,768]{1,0:T(8,128)(2,1)S(1)}, bf16[64,768]{1,0:T(8,128)(2,1)}, u32[]{:S(2)}, u32[]{:S(2)}) collective-permute-start(bf16[64,768]{1,0:T(8,128)(2,1)S(1)} %get-tuple-element.39), channel_id=1, source_target_pairs={{0,384},{16,400},{32,416},{48,432},{64,448},{80,464},{96,480},{112... | collective-permute-start | bytes 294920 | tf_op jit(solution)/shard_map/ppermute | solution.py:288

commit v3 on v2

--- a/solution.py
+++ b/solution.py
@@ -19,6 +19,7 @@
 SMALL = 16 * 1024 * 1024
 LARGE = 40 * 1024 * 1024
 WHOLE = 60 * 1024 * 1024
+LONG = pl.CostEstimate(flops=50_000_000_000, bytes_accessed=1_000_000, transcendentals=0)
 
 
 def dot(left, right):
@@ -63,60 +64,67 @@
     return jnp.concatenate([code, jnp.broadcast_to(power, (NOTE, rows.shape[1])).astype(BF16)], axis=0)
 
 
-def dispatch_kernel(routes, gates, tokens, cotangent, up, down, send, codes, table, scale):
-    @pl.when(pl.program_id(0) == 0)
-    def _():
-        hidden = up.shape[2]
-        codes[:, :hidden] = coded(up[0])
-        codes[:, hidden:] = coded(down[0])
-        first, second, count = named_and_earlier(routes[...])
-        number = count.shape[1]
-        held = jnp.where(first | second, count, -2)[:, None, :]
-        one, two = slots_of_rows(BLOCK, number)
-        gate = jnp.where(first, gates[0:1], 0.0) + jnp.where(second, gates[1:2], 0.0)
-        in_one, in_two = held == one, held == two
-        table[:, :number] = jnp.where(in_one, 1.0, 0.0).reshape(EXPERTS * BLOCK, number).astype(BF16)
-        table[:, number:] = jnp.where(in_two, 1.0, 0.0).reshape(EXPERTS * BLOCK, number).astype(BF16)
-        factor = jnp.where(in_two, gate[:, None, :], 0.0) + jnp.where(in_one, 1.0, 0.0)
-        scale[...] = jnp.sum(factor.reshape(EXPERTS * BLOCK, number), axis=1, keepdims=True)
-
-    both = jnp.concatenate([tokens[...], cotangent[...]], axis=0)
-    rows = dot(table[...], both) * scale[...]
-    send[...] = rows.astype(BF16).reshape(send.shape)
+def dispatch_kernel(
+    routes, gates, up, down, tokens, cotangent, send, codes, both, table, rows, in_sems, out_sems
+):
+    number, width = tokens.shape
+    step = rows.shape[3]
+    loads = [
+        pltpu.make_async_copy(source, both.at[pl.ds(k * number, number)], in_sems.at[k])
+        for k, source in enumerate((tokens, cotangent))
+    ]
+    for load in loads:
+        load.start()
+    hidden = up.shape[2]
+    codes[:, :hidden] = coded(up[0])
+    codes[:, hidden:] = coded(down[0])
+    first, second, count = named_and_earlier(routes[...])
+    held = jnp.where(first | second, count, -2)[:, None, :]
+    one, two = slots_of_rows(BLOCK, number)
+    gate = jnp.where(first, gates[0:1], 0.0) + jnp.where(second, gates[1:2], 0.0)
+    in_one, in_two = held == one, held == two
+    table[:, :number] = jnp.where(in_one, 1.0, 0.0).reshape(EXPERTS * BLOCK, number).astype(BF16)
+    table[:, number:] = jnp.where(in_two, 1.0, 0.0).reshape(EXPERTS * BLOCK, number).astype(BF16)
+    scale = jnp.where(in_two, gate[:, None, :], 0.0) + jnp.where(in_one, 1.0, 0.0)
+    scale = jnp.sum(scale.reshape(EXPERTS * BLOCK, number), axis=1, keepdims=True)
+    for load in loads:
+        load.wait()
+    stores = []
+    for k in range(width // step):
+        columns = pl.ds(k * step, step)
+        block = dot(table[...], both[:, columns]) * scale
+        rows[k] = block.astype(BF16).reshape(EXPERTS, BLOCK, step)
+        stores.append(pltpu.make_async_copy(rows.at[k], send.at[:, :, columns], out_sems.at[k]))
+        stores[-1].start()
+    for store in stores:
+        store.wait()
 
 
 def dispatch(routes, gates, tokens, cotangent, up_weight, down_weight):
     number, width = tokens.shape
     share, hidden = up_weight.shape[1:]
     step = 512
-    whole = lambda i: (0, 0)
-    column = lambda i: (0, i)
+    steps = width // step
+    vmem = pl.BlockSpec(memory_space=pltpu.VMEM)
+    anywhere = pl.BlockSpec(memory_space=pl.ANY)
     return pl.pallas_call(
         dispatch_kernel,
-        grid=(width // step,),
-        in_specs=[
-            pl.BlockSpec((2, number), whole),
-            pl.BlockSpec((2, number), whole),
-            pl.BlockSpec((number, step), column),
-            pl.BlockSpec((number, step), column),
-            pl.BlockSpec((1, share, hidden), lambda i: (0, 0, 0)),
-            pl.BlockSpec((1, share, hidden), lambda i: (0, 0, 0)),
-        ],
-        out_specs=[
-            pl.BlockSpec((EXPERTS, BLOCK, step), lambda i: (0, 0, i)),
-            pl.BlockSpec((share + NOTE, 2 * hidden), whole),
-        ],
+        in_specs=[vmem] * 4 + [anywhere] * 2,
+        out_specs=[anywhere, vmem],
         out_shape=[
             jax.ShapeDtypeStruct((EXPERTS, BLOCK, width), BF16),
             jax.ShapeDtypeStruct((share + NOTE, 2 * hidden), BF16),
         ],
         scratch_shapes=[
+            pltpu.VMEM((2 * number, width), BF16),
             pltpu.VMEM((EXPERTS * BLOCK, 2 * number), BF16),
-            pltpu.VMEM((EXPERTS * BLOCK, 1), F32),
+            pltpu.VMEM((steps, EXPERTS, BLOCK, step), BF16),
+            pltpu.SemaphoreType.DMA((2,)),
+            pltpu.SemaphoreType.DMA((steps,)),
         ],
         compiler_params=pltpu.CompilerParams(vmem_limit_bytes=WHOLE),
         name="dispatch",
-    )(routes, gates, tokens, cotangent, up_weight, down_weight)
+    )(routes, gates, up_weight, down_weight, tokens, cotangent)
 
 
 def offset_of(r, core):
@@ -191,15 +199,19 @@
 
 def return_kernel(act, dh, weights, back):
     hidden = weights.shape[1] // 2
-    width = weights.shape[0]
+    half = weights.shape[0] // 2
     body = EXPERTS * BODY
-    up, down = weights[:, :hidden], weights[:, hidden:]
-    back[:, :BODY, :] = contract_last(act[:body], down).astype(BF16).reshape(EXPERTS, BODY, width)
-    back[:, BODY : 2 * BODY, :] = (
-        contract_last(dh[:body], up).astype(BF16).reshape(EXPERTS, BODY, width)
-    )
-    over = contract_last(act[body:], down) + pltpu.roll(contract_last(dh[body:], up), REST, 0)
-    back[:, 2 * BODY :, :] = over.astype(BF16).reshape(EXPERTS, BLOCK - 2 * BODY, width)
+    over = jnp.zeros((act.shape[0] - body, half), F32)
+    for kind, value in enumerate((act, dh)):
+        for side in range(2):
+            place = 2 * kind + side
+            weight = weights[side * half : (side + 1) * half, (1 - kind) * hidden : (2 - kind) * hidden]
+            back[:, place * BODY : (place + 1) * BODY, :] = (
+                contract_last(value[:body], weight).astype(BF16).reshape(EXPERTS, BODY, half)
+            )
+            rest = contract_last(value[body:], weight)
+            over = over + (pltpu.roll(rest, REST * place, 0) if place else rest)
+    back[:, 4 * BODY :, :] = over.astype(BF16).reshape(EXPERTS, 4 * REST, half)
 
 
 def returns(act, dh, weights):
@@ -208,8 +220,9 @@
         return_kernel,
         in_specs=[whole] * 3,
         out_specs=whole,
-        out_shape=jax.ShapeDtypeStruct((EXPERTS, BLOCK, weights.shape[0]), BF16),
+        out_shape=jax.ShapeDtypeStruct((EXPERTS, 4 * CAP, weights.shape[0] // 2), BF16),
         compiler_params=pltpu.CompilerParams(vmem_limit_bytes=LARGE),
+        cost_estimate=LONG,
         name="returns",
     )(act, dh, weights)
 
@@ -217,15 +230,18 @@
 def table_kernel(routes, gates, table, scale):
     number = routes.shape[1]
     first, second, count = named_and_earlier(routes[...])
-    one, two = slots_of_rows(BLOCK, number)
-
-    def picked(chosen, slots):
+    slot = lax.broadcasted_iota(jnp.int32, (1, BODY, number), 1)
+    place = lax.broadcasted_iota(jnp.int32, (1, 4 * REST, number), 1)
+    for k, chosen in enumerate((first, second, first | second)):
         held = jnp.where(chosen, count, -2)[:, None, :]
-        return jnp.where(held == slots, 1.0, 0.0).reshape(EXPERTS * BLOCK, number).T.astype(BF16)
-
-    table[:number] = picked(first, one)
-    table[number : 2 * number] = picked(second, one)
-    table[2 * number :] = picked(first | second, two)
+        body = jnp.where(held == slot, 1.0, 0.0).reshape(EXPERTS * BODY, number).T
+        for side in range(2):
+            start = REST * (2 * (k // 2) + side)
+            mine = (place >= start) & (place < start + REST)
+            over = jnp.where(mine & (held == place - start + BODY), 1.0, 0.0)
+            over = over.reshape(EXPERTS * 4 * REST, number).T
+            at = slice(k * number, (k + 1) * number)
+            table[side, at] = jnp.concatenate([body, over], axis=1).astype(BF16)
     here = lax.broadcasted_iota(jnp.int32, (number, number), 0) == lax.broadcasted_iota(
         jnp.int32, (number, number), 1
     )
@@ -238,44 +254,57 @@
     return pl.pallas_call(
         table_kernel,
         out_shape=[
-            jax.ShapeDtypeStruct((3 * number, EXPERTS * BLOCK), BF16),
+            jax.ShapeDtypeStruct((2, 3 * number, EXPERTS * (BODY + 4 * REST)), BF16),
             jax.ShapeDtypeStruct((2, number, 1), F32),
         ],
         compiler_params=pltpu.CompilerParams(vmem_limit_bytes=SMALL),
+        cost_estimate=LONG,
         name="tables",
     )(routes, gates)
 
 
 def combine_kernel(table, scale, back, mixed, input_grad):
     number = mixed.shape[0]
-    rows = back[...].reshape(EXPERTS * BLOCK, back.shape[2])
-    pairs = dot(table[...], rows)
-    mixed[...] = (scale[0] * pairs[:number] + scale[1] * pairs[number : 2 * number]).astype(BF16)
-    input_grad[...] = pairs[2 * number :].astype(BF16)
+    half = back.shape[2]
+    over = back[:, 4 * BODY :, :].reshape(EXPERTS * 4 * REST, half)
+    for side in range(2):
+        columns = slice(side * half, (side + 1) * half)
+        kinds = []
+        for kind in range(2):
+            at = (2 * kind + side) * BODY
+            body = back[:, at : at + BODY, :].reshape(EXPERTS * BODY, half)
+            kinds.append(jnp.concatenate([body, over], axis=0))
+        pairs = dot(table[side, : 2 * number], kinds[0])
+        mixed[:, columns] = (scale[0] * pairs[:number] + scale[1] * pairs[number:]).astype(BF16)
+        input_grad[:, columns] = dot(table[side, 2 * number :], kinds[1]).astype(BF16)
 
 
 def combine(table, scale, back):
     number = scale.shape[1]
-    width = back.shape[2]
-    step = 512
-    column = pl.BlockSpec((number, step), lambda i: (0, i))
+    width = 2 * back.shape[2]
     return pl.pallas_call(
         combine_kernel,
-        grid=(width // step,),
-        in_specs=[
-            pl.BlockSpec(table.shape, lambda i: (0, 0)),
-            pl.BlockSpec(scale.shape, lambda i: (0, 0, 0)),
-            pl.BlockSpec((EXPERTS, BLOCK, step), lambda i: (0, 0, i)),
-        ],
-        out_specs=[column, column],
         out_shape=[jax.ShapeDtypeStruct((number, width), BF16)] * 2,
         compiler_params=pltpu.CompilerParams(vmem_limit_bytes=SMALL),
         name="combine",
     )(table, scale, back)
 
 
+def last_kernel(own, first, second, third, up, down):
+    hidden = up.shape[2]
+    summed = own[...].astype(F32) + first[...].astype(F32)
+    summed = summed + second[...].astype(F32) + third[...].astype(F32)
+    up[0] = summed[:, :hidden].astype(BF16)
+    down[0] = summed[:, hidden:].astype(BF16)
+
+
+def last_sum(own, arrived):
+    share, wide = own.shape
+    grad = jax.ShapeDtypeStruct((1, share, wide // 2), BF16)
+    return pl.pallas_call(last_kernel, out_shape=[grad, grad], name="last_sum")(own, *arrived)
+
+
 def local(chips, tokens, routes, gates, cotangent, up_weight, down_weight):
-    hidden = up_weight.shape[2]
     near = 4
     far = chips // near
 
@@ -299,6 +328,7 @@
     def total(*arrays):
         return sum(a.astype(F32) for a in arrays)
 
+    got, back = lax.optimization_barrier((got, returns(act, dh, weights)))
     quarter = total(keep[0], got[0])
     for r in range(1, near):
         chip_sum = total(keep[r], got[r]).astype(BF16)
@@ -306,13 +336,13 @@
         quarter = quarter + arrived.astype(F32)
     quarter = quarter.astype(BF16)
     arrived = [moved(quarter[j], lambda core: near * j) for j in range(1, far)]
+    routes, gates, quarter = lax.optimization_barrier((routes, gates, quarter))
     table, scale = tables(routes, gates)
-    back = returns(act, dh, weights)
     back = lax.all_to_all(back, "expert", split_axis=0, concat_axis=0, tiled=True)
     mixed, input_grad = combine(table, scale, back)
     mixed, input_grad, arrived = lax.optimization_barrier((mixed, input_grad, arrived))
-    summed = total(quarter[0], *arrived).astype(BF16)[None]
-    return mixed, input_grad, summed[:, :, :hidden], summed[:, :, hidden:]
+    up_grad, down_grad = last_sum(quarter[0], arrived)
+    return mixed, input_grad, up_grad, down_grad
 
 
 def solution(mesh):

time: 145 us -> 131 us (0.903)
  waiting for transfers between devices: 28.3 us -> 17.5 us
  local copies, waits for them, and re-layouts: 3.34 us -> 1.34 us
  other arithmetic: 5.05 us -> 3.57 us
    ppermute x7, waiting for transfers between devices: 28.3 us -> 9.36 us  [moved(): return lax.ppermute(array, 'dp', pairs)]
    all_to_all x1, waiting for transfers between devices: 0.01 us -> 8.12 us  [local(): lax.all_to_all(back, 'expert', split_axis=0, concat_axis=0, tiled=True)]
    unnamed x12 -> x14, local copies, waits for them, and re-layouts: 2.67 us -> 0.66 us
    pallas_call x3 -> x4, Pallas kernels: 8.1 us -> 8.54 us  [the longest x1 4.65 us: dispatch(): pl.pallas_call(dispatch_kernel, in_specs=[vmem] * 4 + [anywhere] * 2, out...]
  transfers between devices with their start and end apart: 9 -> 9, of which waited for: 5 -> 3; matrix products, arithmetic and copies ran while one was open for 3% -> 2% of each run, Pallas kernels for 4% -> 3%
where the time goes in v3:
time: 131 us; the launch traced here: 130 us
  blocking collectives  48 us (37%)
  starting transfers between devices  42.5 us (32%)
  waiting for transfers between devices  17.5 us (13%)
  Pallas kernels  16.7 us (13%)
  other arithmetic  3.57 us (3%)
  local copies, waits for them, and re-layouts  1.34 us (1%)
    all_gather x1, blocking collectives, local(): codes = lax.all_gather(codes.astype(jnp.float16), 'dp').astype(BF16)  48 us
    ppermute x7, starting transfers between devices, moved(): return lax.ppermute(array, 'dp', pairs)  27.9 us
    ppermute x7, waiting for transfers between devices, moved(): return lax.ppermute(array, 'dp', pairs)  9.36 us
    all_to_all x1, waiting for transfers between devices, local(): lax.all_to_all(back, 'expert', split_axis=0, concat_axis=0, tiled=True)  8.12 us
    all_to_all x1, starting transfers between devices, local(): lax.all_to_all(send, 'expert', split_axis=0, concat_axis=0, tiled=True)  7.77 us
    all_to_all x1, starting transfers between devices, local(): lax.all_to_all(back, 'expert', split_axis=0, concat_axis=0, tiled=True)  6.88 us
    pallas_call x1, Pallas kernels, expert(): pl.pallas_call(expert_kernel, in_specs=[pl.BlockSpec(memory_space=pltpu.S...  5.97 us
    pallas_call x1, Pallas kernels, dispatch(): pl.pallas_call(dispatch_kernel, in_specs=[vmem] * 4 + [anywhere] * 2, out...  4.65 us
  transfers between devices with their start and end apart: 9, of which 3 were waited for; matrix products, arithmetic and copies ran while one was open for 2% of the time, Pallas kernels for 3%

profile of v3, /device:TPU:1, one launch (start us, length us, event | category | flops | bytes accessed | tf_op | source)
XLA Modules:
  0.0 130.5 jit_solution(15626287927416736054)
XLA Ops:
  0.6 4.6 %dispatch.1 = (bf16[16,40,2048]{2,1,0:T(8,128)(2,1)}, bf16[72,768]{1,0:T(8,128)(2,1)}) custom-call(s32[2,128]{1,0:T(2,128)} %bitcast.28, f32[2,128]{1,0:T(2,128)} %bitcast.30, bf16[1,64,384]{2,1,0:T(8,128)(2,1)} %up.1, bf16[1,64,384]{2,1,0:T(8,128)(2,1)} %down.1, bf16[128,2048]{1,0:T(8,128)(2,1)} %tokens.1, bf16[128,2048]{1,0:T(8,128)(2,1)} %cotangent.1), custom_call_target="tpu_custom_call" | custom-call | tf_op jit(solution)/shard_map/dispatch/pallas_call | solution.py:110
  5.3 0.0 copy-start.5
  5.3 7.8 %all-to-all-start = ((bf16[16,40,2048]{2,1,0:T(8,128)(2,1)}), bf16[16,40,2048]{2,1,0:T(8,128)(2,1)}, u32[]{:S(2)}, u32[]{:S(2)}) async-start(bf16[16,40,2048]{2,1,0:T(8,128)(2,1)} %get-tuple-element.27), calls=%async_computation | async-start | bytes 5242880 | tf_op jit(solution)/shard_map/all_to_all | solution.py:322
  13.1 48.0 %all-gather.2 = f16[2304,768]{1,0:T(8,128)(2,1)S(1)} all-gather(f16[72,768]{1,0:T(8,128)(2,1)S(1)} %convert_element_type.68), channel_id=2, replica_groups=mesh['dp'=32,'expert'=16] {'dp'}, dimensions={0}, use_global_device_ids=true | all-gather | bytes 3649536 | tf_op jit(solution)/shard_map/all_gather | solution.py:321
  61.1 0.6 convert_element_type.88
  61.7 0.1 pad_add_fusion.place
  61.8 0.0 all-to-all-done.received
  61.8 6.0 %expert.1 = (bf16[384,384]{1,0:T(8,128)(2,1)S(1)}, bf16[384,384]{1,0:T(8,128)(2,1)S(1)}, bf16[2048,768]{1,0:T(8,128)(2,1)S(1)}, bf16[4,4,64,768]{3,2,1,0:T(8,128)(2,1)S(1)}, bf16[4,4,64,768]{3,2,1,0:T(8,128)(2,1)S(1)}) custom-call(s32[2]{0:T(128)S(1)} %pad_add_fusion.place, bf16[16,40,2048]{2,1,0:T(8,128)(2,1)} %all-to-all-done.received, ...), custom_call_target="tpu_custom_call" | custom-call | tf_op jit(solution)/shard_map/expert/pallas_call | solution.py:183
  67.8 2.1 %collective-permute-start = (bf16[4,4,64,768]{3,2,1,0:T(8,128)(2,1)S(1)}, bf16[4,4,64,768]{3,2,1,0:T(8,128)(2,1)S(1)}, u32[]{:S(2)}, u32[]{:S(2)}) collective-permute-start(bf16[4,4,64,768]{3,2,1,0:T(8,128)(2,1)S(1)} %get-tuple-element.30), channel_id=1, source_target_pairs={{0,16},{16,0},{32,48},{48,32},{64,80},{80,64},{96,112},{112,96},{1... | collective-permute-start | bytes 4718600 | tf_op jit(solution)/shard_map/ppermute | solution.py:317
  69.9 2.2 %returns.1 = bf16[16,72,1024]{2,1,0:T(8,128)(2,1)S(1)} custom-call(bf16[384,384]{1,0:T(8,128)(2,1)S(1)} %get-tuple-element.31.act, bf16[384,384]{1,0:T(8,128)(2,1)S(1)} %get-tuple-element.32.dh, bf16[2048,768]{1,0:T(8,128)(2,1)S(1)} %get-tuple-element.33.weights), custom_call_target="tpu_custom_call" | custom-call | flops 49999998976 | bytes 1000000 | tf_op jit(solution)/shard_map/returns/pallas_call | solution.py:219
  72.1 1.0 collective-permute-done
  73.1 1.4 %fusion.3 = (bf16[4,64,768]{2,1,0:T(8,128)(2,1)}, bf16[4,64,768]{2,1,0:T(8,128)(2,1)}, bf16[4,64,768]{2,1,0:T(8,128)(2,1)S(1)}) fusion(bf16[4,4,64,768]{3,2,1,0:T(8,128)(2,1)S(1)} %collective-permute-done, bf16[4,4,64,768]{3,2,1,0:T(8,128)(2,1)S(1)} %get-tuple-element.29), kind=kLoop, calls=%fused_computation.7 | loop fusion | flops 2359296 | bytes 3538944 | tf_op jit(solution)/shard_map/convert_element_type | solution.py:334
  74.5 1.9 %collective-permute-start.1 = (bf16[4,64,768]{2,1,0:T(8,128)(2,1)}, bf16[4,64,768]{2,1,0:T(8,128)(2,1)S(1)}, u32[]{:S(2)}, u32[]{:S(2)}) collective-permute-start(bf16[4,64,768]{2,1,0:T(8,128)(2,1)} %get-tuple-element.50), channel_id=1, source_target_pairs={{0,32},{16,48},{32,64},{48,80},{64,96},{80,112},{96,128},{112,144}... | collective-permute-start | bytes 1179656 | tf_op jit(solution)/shard_map/ppermute | solution.py:317
  76.4 4.6 %collective-permute-start.3 = (bf16[4,64,768]{2,1,0:T(8,128)(2,1)}, bf16[4,64,768]{2,1,0:T(8,128)(2,1)S(1)}, u32[]{:S(2)}, u32[]{:S(2)}) collective-permute-start(bf16[4,64,768]{2,1,0:T(8,128)(2,1)} %get-tuple-element.51), channel_id=1, source_target_pairs={{0,480},{16,496},{32,0},{48,16},{64,32},{80,48},{96,64},{112,80},{... | collective-permute-start | bytes 1179656 | tf_op jit(solution)/shard_map/ppermute | solution.py:317
  81.0 2.3 %collective-permute-start.2 = (bf16[4,64,768]{2,1,0:T(8,128)(2,1)S(1)}, bf16[4,64,768]{2,1,0:T(8,128)(2,1)}, u32[]{:S(2)}, u32[]{:S(2)}) collective-permute-start(bf16[4,64,768]{2,1,0:T(8,128)(2,1)S(1)} %get-tuple-element.52), channel_id=1, source_target_pairs={{0,64},{16,464},{32,96},{48,496},{64,128},{80,16},{96,160},{112,48... | collective-permute-start | bytes 1179656 | tf_op jit(solution)/shard_map/ppermute | solution.py:317
  83.3 6.9 %all-to-all-start.1 = ((bf16[16,72,1024]{2,1,0:T(8,128)(2,1)}), bf16[16,72,1024]{2,1,0:T(8,128)(2,1)S(1)}, u32[]{:S(2)}, u32[]{:S(2)}) async-start(bf16[16,72,1024]{2,1,0:T(8,128)(2,1)} %copy-done), calls=%async_computation.1 | async-start | bytes 4718592 | tf_op jit(solution)/shard_map/all_to_all | solution.py:341
  90.2 0.0 copy-start.2
  90.2 0.0 copy-start.3
  90.2 0.0 collective-permute-done.1
  90.2 8.3 %collective-permute-done.2 = bf16[4,64,768]{2,1,0:T(8,128)(2,1)} collective-permute-done((bf16[4,64,768]{2,1,0:T(8,128)(2,1)S(1)}, bf16[4,64,768]{2,1,0:T(8,128)(2,1)}, u32[]{:S(2)}, u32[]{:S(2)}) %collective-permute-start.2) | collective-permute-done | bytes 393248 | tf_op jit(solution)/shard_map/ppermute | solution.py:317
  98.5 1.5 %fusion.2 = bf16[4,64,768]{2,1,0:T(8,128)(2,1)S(1)} fusion(bf16[4,64,768]{2,1,0:T(8,128)(2,1)S(1)} %collective-permute-done.3, bf16[4,64,768]{2,1,0:T(8,128)(2,1)} %collective-permute-done.2, bf16[4,64,768]{2,1,0:T(8,128)(2,1)S(1)} %collective-permute-done.1, bf16[4,4,64,768]{3,2,1,0:T(8,128)(2,1)} %copy-done.4, bf16[4,4,64,768]{3,2,1,0:T(8,128)(2,1)} %copy-done.1), kind=kLoop, calls=%fused_computation.3 | loop fusion | flops 1966080 | bytes 2359296 | tf_op jit(solution)/shard_map/convert_element_type | solution.py:337
  100.1 5.2 %collective-permute-start.6 = (bf16[64,768]{1,0:T(8,128)(2,1)S(1)}, bf16[64,768]{1,0:T(8,128)(2,1)S(1)}, u32[]{:S(2)}, u32[]{:S(2)}) collective-permute-start(bf16[64,768]{1,0:T(8,128)(2,1)S(1)} %get-tuple-element.53), channel_id=1, source_target_pairs={{0,384},{16,400},{32,416},{48,432},{64,448},{80,464},{96,480},{112... | collective-permute-start | bytes 294920 | tf_op jit(solution)/shard_map/ppermute | solution.py:317
  105.2 5.8 %collective-permute-start.5 = (bf16[64,768]{1,0:T(8,128)(2,1)S(1)}, bf16[64,768]{1,0:T(8,128)(2,1)}, u32[]{:S(2)}, u32[]{:S(2)}) collective-permute-start(bf16[64,768]{1,0:T(8,128)(2,1)S(1)} %get-tuple-element.54), channel_id=1, source_target_pairs={{0,256},{16,272},{32,288},{48,304},{64,320},{80,336},{96,352},{112... | collective-permute-start | bytes 294920 | tf_op jit(solution)/shard_map/ppermute | solution.py:317
  111.0 6.1 %collective-permute-start.4 = (bf16[64,768]{1,0:T(8,128)(2,1)S(1)}, bf16[64,768]{1,0:T(8,128)(2,1)}, u32[]{:S(2)}, u32[]{:S(2)}) collective-permute-start(bf16[64,768]{1,0:T(8,128)(2,1)S(1)} %get-tuple-element.55), channel_id=1, source_target_pairs={{0,128},{16,144},{32,160},{48,176},{64,192},{80,208},{96,224},{112... | collective-permute-start | bytes 294920 | tf_op jit(solution)/shard_map/ppermute | solution.py:317
  117.1 0.4 tables.1
  117.5 0.7 slice_bitcast_fusion.3.own
  118.2 8.1 %all-to-all-done.1.back = bf16[16,72,1024]{2,1,0:T(8,128)(2,1)S(1)} async-done(((bf16[16,72,1024]{2,1,0:T(8,128)(2,1)}), bf16[16,72,1024]{2,1,0:T(8,128)(2,1)S(1)}, u32[]{:S(2)}, u32[]{:S(2)}) %all-to-all-start.1) | async-done | bytes 2359328 | tf_op jit(solution)/shard_map/all_to_all | solution.py:341
  126.3 1.8 %combine.1 = (bf16[128,2048]{1,0:T(8,128)(2,1)}, bf16[128,2048]{1,0:T(8,128)(2,1)}) custom-call(bf16[2,384,384]{2,1,0:T(8,128)(2,1)S(1)} %get-tuple-element.37.table, f32[2,128,1]{2,1,0:T(8,128)S(1)} %get-tuple-element.38.scale, bf16[16,72,1024]{2,1,0:T(8,128)(2,1)S(1)} %all-to-all-done.1.back), custom_call_target="tpu_custom_call" | custom-call | tf_op jit(solution)/shard_map/combine/pallas_call | solution.py:285
  128.1 0.0 collective-permute-done.6.third
  128.1 0.0 collective-permute-done.5.second
  128.1 0.6 copy-done.6
  128.7 1.7 %last_sum.1 = (bf16[1,64,384]{2,1,0:T(8,128)(2,1)}, bf16[1,64,384]{2,1,0:T(8,128)(2,1)}) custom-call(bf16[64,768]{1,0:T(8,128)(2,1)} %slice_bitcast_fusion.3.own, bf16[64,768]{1,0:T(8,128)(2,1)} %collective-permute-done.4.first, bf16[64,768]{1,0:T(8,128)(2,1)} %collective-permute-done.5.second, bf16[64,768]{1,0:T(8,128)(2,1)} %copy-done.6), custom_call_target="tpu_custom_call" | custom-call | tf_op jit(solution)/shard_map/last_sum/pallas_call | solution.py:304
  (14 shorter events, 0.1 us)
Async XLA Ops:
  5.3 7.8 %copy-start.5 = (bf16[72,768]{1,0:T(8,128)(2,1)S(1)}, bf16[72,768]{1,0:T(8,128)(2,1)}, u32[]{:S(2)}) copy-start(bf16[72,768]{1,0:T(8,128)(2,1)} %get-tuple-element.28) | copy-start | bytes 331780
  5.3 56.5 %all-to-all-start = ((bf16[16,40,2048]{2,1,0:T(8,128)(2,1)}), bf16[16,40,2048]{2,1,0:T(8,128)(2,1)}, u32[]{:S(2)}, u32[]{:S(2)}) async-start(bf16[16,40,2048]{2,1,0:T(8,128)(2,1)} %get-tuple-element.27), calls=%async_computation | async-start | bytes 5242880 | tf_op jit(solution)/shard_map/all_to_all | solution.py:322
  67.8 5.3 %copy-start.1 = (bf16[4,4,64,768]{3,2,1,0:T(8,128)(2,1)}, bf16[4,4,64,768]{3,2,1,0:T(8,128)(2,1)S(1)}, u32[]{:S(2)}) copy-start(bf16[4,4,64,768]{3,2,1,0:T(8,128)(2,1)S(1)} %get-tuple-element.29) | copy-start | bytes 4718596
  67.8 5.3 %collective-permute-start = (bf16[4,4,64,768]{3,2,1,0:T(8,128)(2,1)S(1)}, bf16[4,4,64,768]{3,2,1,0:T(8,128)(2,1)S(1)}, u32[]{:S(2)}, u32[]{:S(2)}) collective-permute-start(bf16[4,4,64,768]{3,2,1,0:T(8,128)(2,1)S(1)} %get-tuple-element.30), channel_id=1, source_target_pairs={{0,16},{16,0},{32,48},{48,32},{64,80},{80,64},{96,112},{112,96},{1... | collective-permute-start | bytes 4718600 | tf_op jit(solution)/shard_map/ppermute | solution.py:317
  72.1 8.9 %copy-start = (bf16[16,72,1024]{2,1,0:T(8,128)(2,1)}, bf16[16,72,1024]{2,1,0:T(8,128)(2,1)S(1)}, u32[]{:S(2)}) copy-start(bf16[16,72,1024]{2,1,0:T(8,128)(2,1)S(1)} %returns.1) | copy-start | bytes 7077892
  73.1 1.4 %copy-start.4 = (bf16[4,4,64,768]{3,2,1,0:T(8,128)(2,1)}, bf16[4,4,64,768]{3,2,1,0:T(8,128)(2,1)S(1)}, u32[]{:S(2)}) copy-start(bf16[4,4,64,768]{3,2,1,0:T(8,128)(2,1)S(1)} %collective-permute-done) | copy-start | bytes 4718596
  74.5 15.7 %collective-permute-start.1 = (bf16[4,64,768]{2,1,0:T(8,128)(2,1)}, bf16[4,64,768]{2,1,0:T(8,128)(2,1)S(1)}, u32[]{:S(2)}, u32[]{:S(2)}) collective-permute-start(bf16[4,64,768]{2,1,0:T(8,128)(2,1)} %get-tuple-element.50), channel_id=1, source_target_pairs={{0,32},{16,48},{32,64},{48,80},{64,96},{80,112},{96,128},{112,144}... | collective-permute-start | bytes 1179656 | tf_op jit(solution)/shard_map/ppermute | solution.py:317
  76.4 13.8 %collective-permute-start.3 = (bf16[4,64,768]{2,1,0:T(8,128)(2,1)}, bf16[4,64,768]{2,1,0:T(8,128)(2,1)S(1)}, u32[]{:S(2)}, u32[]{:S(2)}) collective-permute-start(bf16[4,64,768]{2,1,0:T(8,128)(2,1)} %get-tuple-element.51), channel_id=1, source_target_pairs={{0,480},{16,496},{32,0},{48,16},{64,32},{80,48},{96,64},{112,80},{... | collective-permute-start | bytes 1179656 | tf_op jit(solution)/shard_map/ppermute | solution.py:317
  81.0 17.5 %collective-permute-start.2 = (bf16[4,64,768]{2,1,0:T(8,128)(2,1)S(1)}, bf16[4,64,768]{2,1,0:T(8,128)(2,1)}, u32[]{:S(2)}, u32[]{:S(2)}) collective-permute-start(bf16[4,64,768]{2,1,0:T(8,128)(2,1)S(1)} %get-tuple-element.52), channel_id=1, source_target_pairs={{0,64},{16,464},{32,96},{48,496},{64,128},{80,16},{96,160},{112,48... | collective-permute-start | bytes 1179656 | tf_op jit(solution)/shard_map/ppermute | solution.py:317
  83.3 43.0 %all-to-all-start.1 = ((bf16[16,72,1024]{2,1,0:T(8,128)(2,1)}), bf16[16,72,1024]{2,1,0:T(8,128)(2,1)S(1)}, u32[]{:S(2)}, u32[]{:S(2)}) async-start(bf16[16,72,1024]{2,1,0:T(8,128)(2,1)} %copy-done), calls=%async_computation.1 | async-start | bytes 4718592 | tf_op jit(solution)/shard_map/all_to_all | solution.py:341
  90.2 26.9 %copy-start.2 = (s32[128,2]{0,1:T(2,128)S(1)}, s32[128,2]{0,1:T(2,128)}, u32[]{:S(2)}) copy-start(s32[128,2]{0,1:T(2,128)} %param.7) | copy-start | bytes 3076
  90.2 26.9 %copy-start.3 = (f32[128,2]{0,1:T(2,128)S(1)}, f32[128,2]{0,1:T(2,128)}, u32[]{:S(2)}) copy-start(f32[128,2]{0,1:T(2,128)} %param.8) | copy-start | bytes 3076
  100.1 28.0 %collective-permute-start.6 = (bf16[64,768]{1,0:T(8,128)(2,1)S(1)}, bf16[64,768]{1,0:T(8,128)(2,1)S(1)}, u32[]{:S(2)}, u32[]{:S(2)}) collective-permute-start(bf16[64,768]{1,0:T(8,128)(2,1)S(1)} %get-tuple-element.53), channel_id=1, source_target_pairs={{0,384},{16,400},{32,416},{48,432},{64,448},{80,464},{96,480},{112... | collective-permute-start | bytes 294920 | tf_op jit(solution)/shard_map/ppermute | solution.py:317
  105.2 22.9 %collective-permute-start.5 = (bf16[64,768]{1,0:T(8,128)(2,1)S(1)}, bf16[64,768]{1,0:T(8,128)(2,1)}, u32[]{:S(2)}, u32[]{:S(2)}) collective-permute-start(bf16[64,768]{1,0:T(8,128)(2,1)S(1)} %get-tuple-element.54), channel_id=1, source_target_pairs={{0,256},{16,272},{32,288},{48,304},{64,320},{80,336},{96,352},{112... | collective-permute-start | bytes 294920 | tf_op jit(solution)/shard_map/ppermute | solution.py:317
  111.0 17.1 %collective-permute-start.4 = (bf16[64,768]{1,0:T(8,128)(2,1)S(1)}, bf16[64,768]{1,0:T(8,128)(2,1)}, u32[]{:S(2)}, u32[]{:S(2)}) collective-permute-start(bf16[64,768]{1,0:T(8,128)(2,1)S(1)} %get-tuple-element.55), channel_id=1, source_target_pairs={{0,128},{16,144},{32,160},{48,176},{64,192},{80,208},{96,224},{112... | collective-permute-start | bytes 294920 | tf_op jit(solution)/shard_map/ppermute | solution.py:317
  128.1 0.6 copy-start.6

commit v4 on v3

--- a/solution.py
+++ b/solution.py
@@ -65,36 +65,47 @@
 
 
 def dispatch_kernel(
-    routes, gates, up, down, tokens, cotangent, send, codes, both, table, rows, in_sems, out_sems
+    routes, gates, up, down, tokens, cotangent, send, codes,
+    routes_in, gates_in, up_in, down_in, both, table, rows, small_sems, in_sems, out_sems,
 ):
     number, width = tokens.shape
-    step = rows.shape[3]
-    loads = [
+    steps, step = rows.shape[:2]
+    small = [
+        pltpu.make_async_copy(source, target, small_sems.at[k])
+        for k, (source, target) in enumerate(
+            ((routes, routes_in), (gates, gates_in), (up, up_in), (down, down_in))
+        )
+    ]
+    large = [
         pltpu.make_async_copy(source, both.at[pl.ds(k * number, number)], in_sems.at[k])
         for k, source in enumerate((tokens, cotangent))
     ]
-    for load in loads:
+    for load in small + large:
         load.start()
+    for load in small:
+        load.wait()
     hidden = up.shape[2]
-    codes[:, :hidden] = coded(up[0])
-    codes[:, hidden:] = coded(down[0])
-    first, second, count = named_and_earlier(routes[...])
+    codes[:, :hidden] = coded(up_in[0])
+    codes[:, hidden:] = coded(down_in[0])
+    first, second, count = named_and_earlier(routes_in[...])
     held = jnp.where(first | second, count, -2)[:, None, :]
     one, two = slots_of_rows(BLOCK, number)
-    gate = jnp.where(first, gates[0:1], 0.0) + jnp.where(second, gates[1:2], 0.0)
+    gate = jnp.where(first, gates_in[0:1], 0.0) + jnp.where(second, gates_in[1:2], 0.0)
     in_one, in_two = held == one, held == two
     table[:, :number] = jnp.where(in_one, 1.0, 0.0).reshape(EXPERTS * BLOCK, number).astype(BF16)
     table[:, number:] = jnp.where(in_two, 1.0, 0.0).reshape(EXPERTS * BLOCK, number).astype(BF16)
     scale = jnp.where(in_two, gate[:, None, :], 0.0) + jnp.where(in_one, 1.0, 0.0)
     scale = jnp.sum(scale.reshape(EXPERTS * BLOCK, number), axis=1, keepdims=True)
-    for load in loads:
+    for load in large:
         load.wait()
     stores = []
-    for k in range(width // step):
-        columns = pl.ds(k * step, step)
-        block = dot(table[...], both[:, columns]) * scale
-        rows[k] = block.astype(BF16).reshape(EXPERTS, BLOCK, step)
-        stores.append(pltpu.make_async_copy(rows.at[k], send.at[:, :, columns], out_sems.at[k]))
+    for k in range(steps):
+        at = slice(k * step * BLOCK, (k + 1) * step * BLOCK)
+        block = dot(table[at], both[...]) * scale[at]
+        rows[k] = block.astype(BF16).reshape(step, BLOCK, width)
+        stores.append(
+            pltpu.make_async_copy(rows.at[k], send.at[pl.ds(k * step, step)], out_sems.at[k])
+        )
         stores[-1].start()
     for store in stores:
         store.wait()
@@ -103,22 +114,26 @@
 def dispatch(routes, gates, tokens, cotangent, up_weight, down_weight):
     number, width = tokens.shape
     share, hidden = up_weight.shape[1:]
-    step = 512
-    steps = width // step
-    vmem = pl.BlockSpec(memory_space=pltpu.VMEM)
+    step = 4
+    steps = EXPERTS // step
     anywhere = pl.BlockSpec(memory_space=pl.ANY)
     return pl.pallas_call(
         dispatch_kernel,
-        in_specs=[vmem] * 4 + [anywhere] * 2,
-        out_specs=[anywhere, vmem],
+        in_specs=[anywhere] * 6,
+        out_specs=[anywhere, pl.BlockSpec(memory_space=pltpu.VMEM)],
         out_shape=[
             jax.ShapeDtypeStruct((EXPERTS, BLOCK, width), BF16),
             jax.ShapeDtypeStruct((share + NOTE, 2 * hidden), BF16),
         ],
         scratch_shapes=[
+            pltpu.VMEM(routes.shape, jnp.int32),
+            pltpu.VMEM(gates.shape, F32),
+            pltpu.VMEM(up_weight.shape, BF16),
+            pltpu.VMEM(down_weight.shape, BF16),
             pltpu.VMEM((2 * number, width), BF16),
             pltpu.VMEM((EXPERTS * BLOCK, 2 * number), BF16),
-            pltpu.VMEM((steps, EXPERTS, BLOCK, step), BF16),
+            pltpu.VMEM((steps, step, BLOCK, width), BF16),
+            pltpu.SemaphoreType.DMA((4,)),
             pltpu.SemaphoreType.DMA((2,)),
             pltpu.SemaphoreType.DMA((steps,)),
         ],
@@ -131,55 +146,75 @@
     return (0, 1, 2 - 4 * core, -1)[r]
 
 
-def expert_kernel(place, received, codes, act_out, dh_out, weights, keep, give, part):
+def ones_where(rows, columns, chosen):
+    row = lax.broadcasted_iota(jnp.int32, (rows, columns), 0)
+    column = lax.broadcasted_iota(jnp.int32, (rows, columns), 1)
+    return jnp.where(chosen(row) == column, 1.0, 0.0).astype(BF16)
+
+
+def expert_kernel(
+    place, received, codes, act_out, dh_out, weights, keep, give, x, g
+):
     width = received.shape[2]
     hidden = codes.shape[2] // 2
-    rows = codes.shape[1] - NOTE
-    factor = jnp.exp2(-codes[:, rows:, :].astype(F32)).astype(BF16)[:, :1, :]
-    weights[...] = (codes[:, :rows, :] * factor).reshape(weights.shape)
+    share = codes.shape[1] - NOTE
     body = EXPERTS * BODY
-    x = received[:, :BODY, :].reshape(body, width)
-    g = received[:, BODY : 2 * BODY, :].reshape(body, width)
-    over = received[:, 2 * BODY :, :].reshape(EXPERTS * (BLOCK - 2 * BODY), width)
-    rest = over.shape[0]
-    up, down = weights[:, :hidden], weights[:, hidden:]
-    valid = lax.broadcasted_iota(jnp.int32, (rest, hidden), 0) % (BLOCK - 2 * BODY) < REST
-
-    def hidden_part(hpre, dact):
-        s = 1.0 / (1.0 + jnp.exp(-hpre))
-        return hpre * s, dact * s * (1.0 + hpre * (1.0 - s))
-
-    act, dh = hidden_part(dot(x, up), dot(g, down))
-    act, dh = act.astype(BF16), dh.astype(BF16)
-    dact_over = pltpu.roll(dot(over, down), rest - REST, 0)
-    act_over, dh_over = hidden_part(dot(over, up), dact_over)
-    act_over = jnp.where(valid, act_over, 0.0)
-    dh_over = jnp.where(valid, dh_over, 0.0).astype(BF16)
-    act_moved = pltpu.roll(act_over, REST, 0).astype(BF16)
-    act_out[:body] = act
-    act_out[body:] = act_over.astype(BF16)
-    dh_out[:body] = dh
-    dh_out[body:] = dh_over
-    part[:, :hidden] = (contract_rows(x, dh) + contract_rows(over, dh_over)).astype(BF16)
-    part[:, hidden:] = (contract_rows(g, act) + contract_rows(over, act_moved)).astype(BF16)
-    near, far, share = keep.shape[:3]
+    rest = EXPERTS * REST
+    factor = jnp.exp2(-codes[:, share:, :].astype(F32)).astype(BF16)[:, :1, :]
+    weights[...] = (codes[:, :share, :] * factor).reshape(weights.shape)
+    x[:body] = received[:, :BODY, :].reshape(body, width)
+    g[:body] = received[:, BODY : 2 * BODY, :].reshape(body, width)
+    eight = BLOCK - 2 * BODY
+    over = received[:, 2 * BODY :, :].reshape(EXPERTS * eight, width)
+    pick = ones_where(
+        2 * rest,
+        EXPERTS * eight,
+        lambda row: (row % rest) // REST * eight + row // rest * REST + row % REST,
+    )
+    over = dot(pick, over).astype(BF16)
+    x[body:] = over[:rest]
+    g[body:] = over[rest:]
+    hpre = dot(x[...], weights[:, :hidden])
+    dact = dot(g[...], weights[:, hidden:])
+    s = 1.0 / (1.0 + jnp.exp(-hpre))
+    act = (hpre * s).astype(BF16)
+    dh = (dact * s * (1.0 + hpre * (1.0 - s))).astype(BF16)
+    act_out[...] = act
+    dh_out[...] = dh
+    near, far = keep.shape[:2]
     z, mine = place[0], place[1]
-    for out, owner in ((keep, mine), (give, 1 - mine)):
-        for r in range(near):
-            for j in range(far):
-                chip = lax.rem(z + offset_of(r, owner) + near * j + near * far, near * far)
-                at = (chip * CORES + owner) * share
-                out[r, j] = part[pl.ds(pl.multiple_of(at, share), share), :]
+    step = 512
+    each = step // (CORES * share)
+
+    def parts_of(core):
+        for k in range(width // step):
+            rows = slice(k * step, (k + 1) * step)
+            halves = (
+                contract_rows(x[:, rows], dh).astype(BF16),
+                contract_rows(g[:, rows], act).astype(BF16),
+            )
+            for n in range(each):
+                away = lax.rem(k * each + n - z + near * far, near * far)
+                r = lax.rem(away, near)
+                for owner, out in ((core, keep), (1 - core, give)):
+                    later = jnp.where(r == 3, 1, jnp.where(r == 2, owner, 0))
+                    j = lax.rem(away // near + later, far)
+                    at = slice((n * CORES + owner) * share, (n * CORES + owner + 1) * share)
+                    out[r, j, :, :hidden] = halves[0][at]
+                    out[r, j, :, hidden:] = halves[1][at]
+
+    for core in range(CORES):
+        pl.when(mine == core)(functools.partial(parts_of, core))
 
 
 def expert(place, received, codes):
     width = received.shape[2]
     wide = codes.shape[2]
     share = codes.shape[1] - NOTE
-    rows = EXPERTS * (BLOCK - BODY)
+    rows = EXPERTS * CAP
     whole = pl.BlockSpec(memory_space=pltpu.VMEM)
+    chips = width // share // CORES
     near = 4
-    far = width // share // CORES // near
     return pl.pallas_call(
         expert_kernel,
         in_specs=[pl.BlockSpec(memory_space=pltpu.SMEM), whole, whole],
@@ -188,10 +223,13 @@
             jax.ShapeDtypeStruct((rows, wide // 2), BF16),
             jax.ShapeDtypeStruct((rows, wide // 2), BF16),
             jax.ShapeDtypeStruct((width, wide), BF16),
-            jax.ShapeDtypeStruct((near, far, share, wide), BF16),
-            jax.ShapeDtypeStruct((near, far, share, wide), BF16),
-        ],
-        scratch_shapes=[pltpu.VMEM((width, wide), BF16)],
+            jax.ShapeDtypeStruct((near, chips // near, share, wide), BF16),
+            jax.ShapeDtypeStruct((near, chips // near, share, wide), BF16),
+        ],
+        scratch_shapes=[
+            pltpu.VMEM((rows, width), BF16),
+            pltpu.VMEM((rows, width), BF16),
+        ],
         compiler_params=pltpu.CompilerParams(vmem_limit_bytes=LARGE),
         name="expert",
     )(place, received, codes)
@@ -201,17 +239,23 @@
     hidden = weights.shape[1] // 2
     half = weights.shape[0] // 2
     body = EXPERTS * BODY
-    over = jnp.zeros((act.shape[0] - body, half), F32)
+    rest = EXPERTS * REST
+    over = []
     for kind, value in enumerate((act, dh)):
         for side in range(2):
-            place = 2 * kind + side
+            at = (2 * kind + side) * BODY
             weight = weights[side * half : (side + 1) * half, (1 - kind) * hidden : (2 - kind) * hidden]
-            back[:, place * BODY : (place + 1) * BODY, :] = (
-                contract_last(value[:body], weight).astype(BF16).reshape(EXPERTS, BODY, half)
-            )
-            rest = contract_last(value[body:], weight)
-            over = over + (pltpu.roll(rest, REST * place, 0) if place else rest)
-    back[:, 4 * BODY :, :] = over.astype(BF16).reshape(EXPERTS, 4 * REST, half)
+            rows = contract_last(value[...], weight).astype(BF16)
+            back[:, at : at + BODY, :] = rows[:body].reshape(EXPERTS, BODY, half)
+            over.append(rows[body:])
+    eight = 4 * REST
+    spread = ones_where(
+        EXPERTS * eight,
+        4 * rest,
+        lambda row: row % eight // REST * rest + row // eight * REST + row % REST,
+    )
+    over = dot(spread, jnp.concatenate(over, axis=0)).astype(BF16)
+    back[:, 4 * BODY :, :] = over.reshape(EXPERTS, eight, half)
 
 
 def returns(act, dh, weights):
@@ -290,20 +334,6 @@
     )(table, scale, back)
 
 
-def last_kernel(own, first, second, third, up, down):
-    hidden = up.shape[2]
-    summed = own[...].astype(F32) + first[...].astype(F32)
-    summed = summed + second[...].astype(F32) + third[...].astype(F32)
-    up[0] = summed[:, :hidden].astype(BF16)
-    down[0] = summed[:, hidden:].astype(BF16)
-
-
-def last_sum(own, arrived):
-    share, wide = own.shape
-    grad = jax.ShapeDtypeStruct((1, share, wide // 2), BF16)
-    return pl.pallas_call(last_kernel, out_shape=[grad, grad], name="last_sum")(own, *arrived)
-
-
 def local(chips, tokens, routes, gates, cotangent, up_weight, down_weight):
     near = 4
     far = chips // near
@@ -335,13 +365,17 @@
         arrived = moved(chip_sum, lambda core: offset_of(r, core))
         quarter = quarter + arrived.astype(F32)
     quarter = quarter.astype(BF16)
-    arrived = [moved(quarter[j], lambda core: near * j) for j in range(1, far)]
+    arrived = [moved(quarter[j], lambda core: near * j) for j in (1, 3, 2)]
     routes, gates, quarter = lax.optimization_barrier((routes, gates, quarter))
     table, scale = tables(routes, gates)
     back = lax.all_to_all(back, "expert", split_axis=0, concat_axis=0, tiled=True)
     mixed, input_grad = combine(table, scale, back)
     mixed, input_grad, arrived = lax.optimization_barrier((mixed, input_grad, arrived))
-    up_grad, down_grad = last_sum(quarter[0], arrived)
+    hidden = up_weight.shape[2]
+    up_grad, down_grad = (
+        total(quarter[0][:, half], *[a[:, half] for a in arrived]).astype(BF16)[None]
+        for half in (slice(0, hidden), slice(hidden, 2 * hidden))
+    )
     return mixed, input_grad, up_grad, down_grad
 
 

time: 131 us -> 129 us (0.985)
  Pallas kernels: 16.7 us -> 13.2 us
  other arithmetic: 3.57 us -> 5.17 us
    pallas_call x2 -> x1, Pallas kernels: 6.35 us -> 3.93 us  [dispatch(): pl.pallas_call(dispatch_kernel, in_specs=[anywhere] * 6, out_specs=[anywh...]
    broadcast_in_dim x0 -> x1, other arithmetic: none -> 1.61 us  [local(): total(quarter[0][:, half], *[a[:, half] for a in arrived]).astype(BF16)]
where the time goes in v4:
time: 129 us
  blocking collectives  48 us (37%)
  starting transfers between devices  42.5 us (33%)
  waiting for transfers between devices  18.7 us (14%)
  Pallas kernels  13.2 us (10%)
  other arithmetic  5.17 us (4%)
    all_gather x1, blocking collectives, local(): codes = lax.all_gather(codes.astype(jnp.float16), 'dp').astype(BF16)  48 us
    ppermute x7, starting transfers between devices, moved(): return lax.ppermute(array, 'dp', pairs)  27.9 us
    ppermute x7, waiting for transfers between devices, moved(): return lax.ppermute(array, 'dp', pairs)  9.95 us
    all_to_all x1, waiting for transfers between devices, local(): lax.all_to_all(back, 'expert', split_axis=0, concat_axis=0, tiled=True)  8.74 us
    all_to_all x1, starting transfers between devices, local(): lax.all_to_all(send, 'expert', split_axis=0, concat_axis=0, tiled=True)  7.77 us
    all_to_all x1, starting transfers between devices, local(): lax.all_to_all(back, 'expert', split_axis=0, concat_axis=0, tiled=True)  6.88 us
    pallas_call x1, Pallas kernels, expert(): pl.pallas_call(expert_kernel, in_specs=[pl.BlockSpec(memory_space=pltpu.S...  5.52 us
    pallas_call x1, Pallas kernels, dispatch(): pl.pallas_call(dispatch_kernel, in_specs=[anywhere] * 6, out_specs=[anywh...  3.93 us
  transfers between devices with their start and end apart: 9, of which 3 were waited for; matrix products, arithmetic and copies ran while one was open for 2% of the time, Pallas kernels for 3%

profile of v4, /device:TPU:1, one launch (start us, length us, event | category | flops | bytes accessed | tf_op | source)
XLA Modules:
  0.0 128.6 jit_solution(8778244097497957258)
XLA Ops:
  0.6 3.9 %dispatch.1 = (bf16[16,40,2048]{2,1,0:T(8,128)(2,1)}, bf16[72,768]{1,0:T(8,128)(2,1)}) custom-call(s32[2,128]{1,0:T(2,128)} %bitcast.32, f32[2,128]{1,0:T(2,128)} %bitcast.34, bf16[1,64,384]{2,1,0:T(8,128)(2,1)} %up.1, bf16[1,64,384]{2,1,0:T(8,128)(2,1)} %down.1, bf16[128,2048]{1,0:T(8,128)(2,1)} %tokens.1, bf16[128,2048]{1,0:T(8,128)(2,1)} %cotangent.1), custom_call_target="tpu_custom_call" | custom-call | tf_op jit(solution)/shard_map/dispatch/pallas_call | solution.py:120
  4.6 0.0 copy-start.5
  4.6 7.8 %all-to-all-start = ((bf16[16,40,2048]{2,1,0:T(8,128)(2,1)}), bf16[16,40,2048]{2,1,0:T(8,128)(2,1)}, u32[]{:S(2)}, u32[]{:S(2)}) async-start(bf16[16,40,2048]{2,1,0:T(8,128)(2,1)} %get-tuple-element.25), calls=%async_computation | async-start | bytes 5242880 | tf_op jit(solution)/shard_map/all_to_all | solution.py:352
  12.4 48.0 %all-gather.2 = f16[2304,768]{1,0:T(8,128)(2,1)S(1)} all-gather(f16[72,768]{1,0:T(8,128)(2,1)S(1)} %convert_element_type.98), channel_id=2, replica_groups=mesh['dp'=32,'expert'=16] {'dp'}, dimensions={0}, use_global_device_ids=true | all-gather | bytes 3649536 | tf_op jit(solution)/shard_map/all_gather | solution.py:351
  60.4 0.6 convert_element_type.128
  61.0 0.1 pad_add_fusion.place
  61.1 0.0 all-to-all-done.received
  61.1 5.5 %expert.1 = (bf16[288,384]{1,0:T(8,128)(2,1)S(1)}, bf16[288,384]{1,0:T(8,128)(2,1)S(1)}, bf16[2048,768]{1,0:T(8,128)(2,1)S(1)}, bf16[4,4,64,768]{3,2,1,0:T(8,128)(2,1)S(1)}, bf16[4,4,64,768]{3,2,1,0:T(8,128)(2,1)S(1)}) custom-call(s32[2]{0:T(128)S(1)} %pad_add_fusion.place, bf16[16,40,2048]{2,1,0:T(8,128)(2,1)} %all-to-all-done.received, ...), custom_call_target="tpu_custom_call" | custom-call | tf_op jit(solution)/shard_map/expert/pallas_call | solution.py:218
  66.6 2.1 %collective-permute-start = (bf16[4,4,64,768]{3,2,1,0:T(8,128)(2,1)S(1)}, bf16[4,4,64,768]{3,2,1,0:T(8,128)(2,1)S(1)}, u32[]{:S(2)}, u32[]{:S(2)}) collective-permute-start(bf16[4,4,64,768]{3,2,1,0:T(8,128)(2,1)S(1)} %get-tuple-element.28), channel_id=1, source_target_pairs={{0,16},{16,0},{32,48},{48,32},{64,80},{80,64},{96,112},{112,96},{1... | collective-permute-start | bytes 4718600 | tf_op jit(solution)/shard_map/ppermute | solution.py:347
  68.7 1.6 %returns.1 = bf16[16,72,1024]{2,1,0:T(8,128)(2,1)S(1)} custom-call(bf16[288,384]{1,0:T(8,128)(2,1)S(1)} %get-tuple-element.29.act, bf16[288,384]{1,0:T(8,128)(2,1)S(1)} %get-tuple-element.30.dh, bf16[2048,768]{1,0:T(8,128)(2,1)S(1)} %get-tuple-element.31.weights), custom_call_target="tpu_custom_call" | custom-call | flops 49999998976 | bytes 1000000 | tf_op jit(solution)/shard_map/returns/pallas_call | solution.py:263
  70.3 1.6 %collective-permute-done = bf16[4,4,64,768]{3,2,1,0:T(8,128)(2,1)S(1)} collective-permute-done((bf16[4,4,64,768]{3,2,1,0:T(8,128)(2,1)S(1)}, bf16[4,4,64,768]{3,2,1,0:T(8,128)(2,1)S(1)}, u32[]{:S(2)}, u32[]{:S(2)}) %collective-permute-start) | collective-permute-done | bytes 1572896 | tf_op jit(solution)/shard_map/ppermute | solution.py:347
  71.9 1.4 %fusion.3 = (bf16[4,64,768]{2,1,0:T(8,128)(2,1)}, bf16[4,64,768]{2,1,0:T(8,128)(2,1)}, bf16[4,64,768]{2,1,0:T(8,128)(2,1)S(1)}) fusion(bf16[4,4,64,768]{3,2,1,0:T(8,128)(2,1)S(1)} %collective-permute-done, bf16[4,4,64,768]{3,2,1,0:T(8,128)(2,1)S(1)} %get-tuple-element.27), kind=kLoop, calls=%fused_computation.7 | loop fusion | flops 2359296 | bytes 3538944 | tf_op jit(solution)/shard_map/convert_element_type | solution.py:364
  73.3 1.9 %collective-permute-start.1 = (bf16[4,64,768]{2,1,0:T(8,128)(2,1)}, bf16[4,64,768]{2,1,0:T(8,128)(2,1)S(1)}, u32[]{:S(2)}, u32[]{:S(2)}) collective-permute-start(bf16[4,64,768]{2,1,0:T(8,128)(2,1)} %get-tuple-element.46), channel_id=1, source_target_pairs={{0,32},{16,48},{32,64},{48,80},{64,96},{80,112},{96,128},{112,144}... | collective-permute-start | bytes 1179656 | tf_op jit(solution)/shard_map/ppermute | solution.py:347
  75.3 4.6 %collective-permute-start.3 = (bf16[4,64,768]{2,1,0:T(8,128)(2,1)}, bf16[4,64,768]{2,1,0:T(8,128)(2,1)S(1)}, u32[]{:S(2)}, u32[]{:S(2)}) collective-permute-start(bf16[4,64,768]{2,1,0:T(8,128)(2,1)} %get-tuple-element.47), channel_id=1, source_target_pairs={{0,480},{16,496},{32,0},{48,16},{64,32},{80,48},{96,64},{112,80},{... | collective-permute-start | bytes 1179656 | tf_op jit(solution)/shard_map/ppermute | solution.py:347
  79.8 2.3 %collective-permute-start.2 = (bf16[4,64,768]{2,1,0:T(8,128)(2,1)S(1)}, bf16[4,64,768]{2,1,0:T(8,128)(2,1)}, u32[]{:S(2)}, u32[]{:S(2)}) collective-permute-start(bf16[4,64,768]{2,1,0:T(8,128)(2,1)S(1)} %get-tuple-element.48), channel_id=1, source_target_pairs={{0,64},{16,464},{32,96},{48,496},{64,128},{80,16},{96,160},{112,48... | collective-permute-start | bytes 1179656 | tf_op jit(solution)/shard_map/ppermute | solution.py:347
  82.1 6.9 %all-to-all-start.1 = ((bf16[16,72,1024]{2,1,0:T(8,128)(2,1)}), bf16[16,72,1024]{2,1,0:T(8,128)(2,1)S(1)}, u32[]{:S(2)}, u32[]{:S(2)}) async-start(bf16[16,72,1024]{2,1,0:T(8,128)(2,1)} %copy-done), calls=%async_computation.1 | async-start | bytes 4718592 | tf_op jit(solution)/shard_map/all_to_all | solution.py:371
  89.0 0.0 copy-start.2
  89.0 0.0 copy-start.3
  89.0 0.0 collective-permute-done.1
  89.1 0.0 collective-permute-done.3
  89.1 8.3 %collective-permute-done.2 = bf16[4,64,768]{2,1,0:T(8,128)(2,1)} collective-permute-done((bf16[4,64,768]{2,1,0:T(8,128)(2,1)S(1)}, bf16[4,64,768]{2,1,0:T(8,128)(2,1)}, u32[]{:S(2)}, u32[]{:S(2)}) %collective-permute-start.2) | collective-permute-done | bytes 393248 | tf_op jit(solution)/shard_map/ppermute | solution.py:347
  97.4 1.5 %fusion.2 = bf16[4,64,768]{2,1,0:T(8,128)(2,1)S(1)} fusion(bf16[4,64,768]{2,1,0:T(8,128)(2,1)S(1)} %collective-permute-done.3, bf16[4,64,768]{2,1,0:T(8,128)(2,1)} %collective-permute-done.2, bf16[4,64,768]{2,1,0:T(8,128)(2,1)S(1)} %collective-permute-done.1, bf16[4,4,64,768]{3,2,1,0:T(8,128)(2,1)} %copy-done.4, bf16[4,4,64,768]{3,2,1,0:T(8,128)(2,1)} %copy-done.1), kind=kLoop, calls=%fused_computation.3 | loop fusion | flops 1966080 | bytes 2359296 | tf_op jit(solution)/shard_map/convert_element_type | solution.py:367
  98.9 7.9 %collective-permute-start.6 = (bf16[64,768]{1,0:T(8,128)(2,1)S(1)}, bf16[64,768]{1,0:T(8,128)(2,1)}, u32[]{:S(2)}, u32[]{:S(2)}) collective-permute-start(bf16[64,768]{1,0:T(8,128)(2,1)S(1)} %get-tuple-element.51), channel_id=1, source_target_pairs={{0,256},{16,272},{32,288},{48,304},{64,320},{80,336},{96,352},{112... | collective-permute-start | bytes 294920 | tf_op jit(solution)/shard_map/ppermute | solution.py:347
  106.8 3.1 %collective-permute-start.5 = (bf16[64,768]{1,0:T(8,128)(2,1)S(1)}, bf16[64,768]{1,0:T(8,128)(2,1)}, u32[]{:S(2)}, u32[]{:S(2)}) collective-permute-start(bf16[64,768]{1,0:T(8,128)(2,1)S(1)} %get-tuple-element.52), channel_id=1, source_target_pairs={{0,384},{16,400},{32,416},{48,432},{64,448},{80,464},{96,480},{112... | collective-permute-start | bytes 294920 | tf_op jit(solution)/shard_map/ppermute | solution.py:347
  109.8 6.1 %collective-permute-start.4 = (bf16[64,768]{1,0:T(8,128)(2,1)S(1)}, bf16[64,768]{1,0:T(8,128)(2,1)}, u32[]{:S(2)}, u32[]{:S(2)}) collective-permute-start(bf16[64,768]{1,0:T(8,128)(2,1)S(1)} %get-tuple-element.53), channel_id=1, source_target_pairs={{0,128},{16,144},{32,160},{48,176},{64,192},{80,208},{96,224},{112... | collective-permute-start | bytes 294920 | tf_op jit(solution)/shard_map/ppermute | solution.py:347
  116.0 0.4 tables.1
  116.4 8.7 %all-to-all-done.1.back = bf16[16,72,1024]{2,1,0:T(8,128)(2,1)S(1)} async-done(((bf16[16,72,1024]{2,1,0:T(8,128)(2,1)}), bf16[16,72,1024]{2,1,0:T(8,128)(2,1)S(1)}, u32[]{:S(2)}, u32[]{:S(2)}) %all-to-all-start.1) | async-done | bytes 2359328 | tf_op jit(solution)/shard_map/all_to_all | solution.py:371
  125.1 1.8 %combine.1 = (bf16[128,2048]{1,0:T(8,128)(2,1)}, bf16[128,2048]{1,0:T(8,128)(2,1)}) custom-call(bf16[2,384,384]{2,1,0:T(8,128)(2,1)S(1)} %get-tuple-element.35.table, f32[2,128,1]{2,1,0:T(8,128)S(1)} %get-tuple-element.36.scale, bf16[16,72,1024]{2,1,0:T(8,128)(2,1)S(1)} %all-to-all-done.1.back), custom_call_target="tpu_custom_call" | custom-call | tf_op jit(solution)/shard_map/combine/pallas_call | solution.py:329
  126.9 0.0 collective-permute-done.6
  126.9 0.0 collective-permute-done.5
  126.9 0.0 collective-permute-done.4
  126.9 1.6 %fusion.7 = (bf16[1,64,384]{2,1,0:T(8,128)(2,1)}, bf16[1,64,384]{2,1,0:T(8,128)(2,1)}) fusion(bf16[64,768]{1,0:T(8,128)(2,1)S(1)} %slice_bitcast_fusion.3, bf16[64,768]{1,0:T(8,128)(2,1)} %collective-permute-done.6, bf16[64,768]{1,0:T(8,128)(2,1)} %collective-permute-done.5, bf16[64,768]{1,0:T(8,128)(2,1)} %collective-permute-done.4), kind=kLoop, calls=%fused_computation.17 | loop fusion | flops 393216 | bytes 491520 | tf_op jit(solution)/shard_map/broadcast_in_dim | solution.py:376
  (12 shorter events, 0.1 us)
Async XLA Ops:
  4.6 7.8 %copy-start.5 = (bf16[72,768]{1,0:T(8,128)(2,1)S(1)}, bf16[72,768]{1,0:T(8,128)(2,1)}, u32[]{:S(2)}) copy-start(bf16[72,768]{1,0:T(8,128)(2,1)} %get-tuple-element.26) | copy-start | bytes 331780
  4.6 56.5 %all-to-all-start = ((bf16[16,40,2048]{2,1,0:T(8,128)(2,1)}), bf16[16,40,2048]{2,1,0:T(8,128)(2,1)}, u32[]{:S(2)}, u32[]{:S(2)}) async-start(bf16[16,40,2048]{2,1,0:T(8,128)(2,1)} %get-tuple-element.25), calls=%async_computation | async-start | bytes 5242880 | tf_op jit(solution)/shard_map/all_to_all | solution.py:352
  66.6 5.3 %copy-start.1 = (bf16[4,4,64,768]{3,2,1,0:T(8,128)(2,1)}, bf16[4,4,64,768]{3,2,1,0:T(8,128)(2,1)S(1)}, u32[]{:S(2)}) copy-start(bf16[4,4,64,768]{3,2,1,0:T(8,128)(2,1)S(1)} %get-tuple-element.27) | copy-start | bytes 4718596
  66.6 5.3 %collective-permute-start = (bf16[4,4,64,768]{3,2,1,0:T(8,128)(2,1)S(1)}, bf16[4,4,64,768]{3,2,1,0:T(8,128)(2,1)S(1)}, u32[]{:S(2)}, u32[]{:S(2)}) collective-permute-start(bf16[4,4,64,768]{3,2,1,0:T(8,128)(2,1)S(1)} %get-tuple-element.28), channel_id=1, source_target_pairs={{0,16},{16,0},{32,48},{48,32},{64,80},{80,64},{96,112},{112,96},{1... | collective-permute-start | bytes 4718600 | tf_op jit(solution)/shard_map/ppermute | solution.py:347
  70.3 9.5 %copy-start = (bf16[16,72,1024]{2,1,0:T(8,128)(2,1)}, bf16[16,72,1024]{2,1,0:T(8,128)(2,1)S(1)}, u32[]{:S(2)}) copy-start(bf16[16,72,1024]{2,1,0:T(8,128)(2,1)S(1)} %returns.1) | copy-start | bytes 7077892
  71.9 1.4 %copy-start.4 = (bf16[4,4,64,768]{3,2,1,0:T(8,128)(2,1)}, bf16[4,4,64,768]{3,2,1,0:T(8,128)(2,1)S(1)}, u32[]{:S(2)}) copy-start(bf16[4,4,64,768]{3,2,1,0:T(8,128)(2,1)S(1)} %collective-permute-done) | copy-start | bytes 4718596
  73.3 15.7 %collective-permute-start.1 = (bf16[4,64,768]{2,1,0:T(8,128)(2,1)}, bf16[4,64,768]{2,1,0:T(8,128)(2,1)S(1)}, u32[]{:S(2)}, u32[]{:S(2)}) collective-permute-start(bf16[4,64,768]{2,1,0:T(8,128)(2,1)} %get-tuple-element.46), channel_id=1, source_target_pairs={{0,32},{16,48},{32,64},{48,80},{64,96},{80,112},{96,128},{112,144}... | collective-permute-start | bytes 1179656 | tf_op jit(solution)/shard_map/ppermute | solution.py:347
  75.3 13.8 %collective-permute-start.3 = (bf16[4,64,768]{2,1,0:T(8,128)(2,1)}, bf16[4,64,768]{2,1,0:T(8,128)(2,1)S(1)}, u32[]{:S(2)}, u32[]{:S(2)}) collective-permute-start(bf16[4,64,768]{2,1,0:T(8,128)(2,1)} %get-tuple-element.47), channel_id=1, source_target_pairs={{0,480},{16,496},{32,0},{48,16},{64,32},{80,48},{96,64},{112,80},{... | collective-permute-start | bytes 1179656 | tf_op jit(solution)/shard_map/ppermute | solution.py:347
  79.8 17.5 %collective-permute-start.2 = (bf16[4,64,768]{2,1,0:T(8,128)(2,1)S(1)}, bf16[4,64,768]{2,1,0:T(8,128)(2,1)}, u32[]{:S(2)}, u32[]{:S(2)}) collective-permute-start(bf16[4,64,768]{2,1,0:T(8,128)(2,1)S(1)} %get-tuple-element.48), channel_id=1, source_target_pairs={{0,64},{16,464},{32,96},{48,496},{64,128},{80,16},{96,160},{112,48... | collective-permute-start | bytes 1179656 | tf_op jit(solution)/shard_map/ppermute | solution.py:347
  82.1 43.0 %all-to-all-start.1 = ((bf16[16,72,1024]{2,1,0:T(8,128)(2,1)}), bf16[16,72,1024]{2,1,0:T(8,128)(2,1)S(1)}, u32[]{:S(2)}, u32[]{:S(2)}) async-start(bf16[16,72,1024]{2,1,0:T(8,128)(2,1)} %copy-done), calls=%async_computation.1 | async-start | bytes 4718592 | tf_op jit(solution)/shard_map/all_to_all | solution.py:371
  89.0 26.9 %copy-start.2 = (s32[128,2]{0,1:T(2,128)S(1)}, s32[128,2]{0,1:T(2,128)}, u32[]{:S(2)}) copy-start(s32[128,2]{0,1:T(2,128)} %param.7) | copy-start | bytes 3076
  89.0 26.9 %copy-start.3 = (f32[128,2]{0,1:T(2,128)S(1)}, f32[128,2]{0,1:T(2,128)}, u32[]{:S(2)}) copy-start(f32[128,2]{0,1:T(2,128)} %param.8) | copy-start | bytes 3076
  98.9 28.0 %collective-permute-start.6 = (bf16[64,768]{1,0:T(8,128)(2,1)S(1)}, bf16[64,768]{1,0:T(8,128)(2,1)}, u32[]{:S(2)}, u32[]{:S(2)}) collective-permute-start(bf16[64,768]{1,0:T(8,128)(2,1)S(1)} %get-tuple-element.51), channel_id=1, source_target_pairs={{0,256},{16,272},{32,288},{48,304},{64,320},{80,336},{96,352},{112... | collective-permute-start | bytes 294920 | tf_op jit(solution)/shard_map/ppermute | solution.py:347
  106.8 20.2 %collective-permute-start.5 = (bf16[64,768]{1,0:T(8,128)(2,1)S(1)}, bf16[64,768]{1,0:T(8,128)(2,1)}, u32[]{:S(2)}, u32[]{:S(2)}) collective-permute-start(bf16[64,768]{1,0:T(8,128)(2,1)S(1)} %get-tuple-element.52), channel_id=1, source_target_pairs={{0,384},{16,400},{32,416},{48,432},{64,448},{80,464},{96,480},{112... | collective-permute-start | bytes 294920 | tf_op jit(solution)/shard_map/ppermute | solution.py:347
  109.8 17.1 %collective-permute-start.4 = (bf16[64,768]{1,0:T(8,128)(2,1)S(1)}, bf16[64,768]{1,0:T(8,128)(2,1)}, u32[]{:S(2)}, u32[]{:S(2)}) collective-permute-start(bf16[64,768]{1,0:T(8,128)(2,1)S(1)} %get-tuple-element.53), channel_id=1, source_target_pairs={{0,128},{16,144},{32,160},{48,176},{64,192},{80,208},{96,224},{112... | collective-permute-start | bytes 294920 | tf_op jit(solution)/shard_map/ppermute | solution.py:347

commit v5 on v4

--- a/solution.py
+++ b/solution.py
@@ -271,67 +271,84 @@
     )(act, dh, weights)
 
 
-def table_kernel(routes, gates, table, scale):
+def table_kernel(routes, body, over):
     number = routes.shape[1]
     first, second, count = named_and_earlier(routes[...])
     slot = lax.broadcasted_iota(jnp.int32, (1, BODY, number), 1)
     place = lax.broadcasted_iota(jnp.int32, (1, 4 * REST, number), 1)
     for k, chosen in enumerate((first, second, first | second)):
         held = jnp.where(chosen, count, -2)[:, None, :]
-        body = jnp.where(held == slot, 1.0, 0.0).reshape(EXPERTS * BODY, number).T
+        at = slice(k * number, (k + 1) * number)
+        here = jnp.where(held == slot, 1.0, 0.0).reshape(EXPERTS * BODY, number)
+        body[at] = here.T.astype(BF16)
         for side in range(2):
             start = REST * (2 * (k // 2) + side)
             mine = (place >= start) & (place < start + REST)
-            over = jnp.where(mine & (held == place - start + BODY), 1.0, 0.0)
-            over = over.reshape(EXPERTS * 4 * REST, number).T
-            at = slice(k * number, (k + 1) * number)
-            table[side, at] = jnp.concatenate([body, over], axis=1).astype(BF16)
+            here = jnp.where(mine & (held == place - start + BODY), 1.0, 0.0)
+            over[side, at] = here.reshape(EXPERTS * 4 * REST, number).T.astype(BF16)
+
+
+def tables(routes):
+    number = routes.shape[1]
+    return pl.pallas_call(
+        table_kernel,
+        out_shape=[
+            jax.ShapeDtypeStruct((3 * number, EXPERTS * BODY), BF16),
+            jax.ShapeDtypeStruct((2, 3 * number, EXPERTS * 4 * REST), BF16),
+        ],
+        compiler_params=pltpu.CompilerParams(vmem_limit_bytes=SMALL),
+        name="tables",
+    )(routes)
+
+
+def combine_kernel(in_body, in_over, gates, back, mixed, input_grad):
+    number = mixed.shape[0]
+    half = back.shape[2]
     here = lax.broadcasted_iota(jnp.int32, (number, number), 0) == lax.broadcasted_iota(
         jnp.int32, (number, number), 1
     )
-    for k in range(2):
-        scale[k] = jnp.sum(jnp.where(here, gates[k : k + 1], 0.0), axis=1, keepdims=True)
-
-
-def tables(routes, gates):
-    number = routes.shape[1]
-    return pl.pallas_call(
-        table_kernel,
-        out_shape=[
-            jax.ShapeDtypeStruct((2, 3 * number, EXPERTS * (BODY + 4 * REST)), BF16),
-            jax.ShapeDtypeStruct((2, number, 1), F32),
-        ],
-        compiler_params=pltpu.CompilerParams(vmem_limit_bytes=SMALL),
-        cost_estimate=LONG,
-        name="tables",
-    )(routes, gates)
-
-
-def combine_kernel(table, scale, back, mixed, input_grad):
-    number = mixed.shape[0]
-    half = back.shape[2]
+    gate = [
+        jnp.sum(jnp.where(here, gates[k : k + 1], 0.0), axis=1, keepdims=True) for k in range(2)
+    ]
     over = back[:, 4 * BODY :, :].reshape(EXPERTS * 4 * REST, half)
+
+    def picked(at, kind, side):
+        body = back[:, (2 * kind + side) * BODY : (2 * kind + side + 1) * BODY, :]
+        return dot(
+            jnp.concatenate([in_body[at], in_over[side, at]], axis=1),
+            jnp.concatenate([body.reshape(EXPERTS * BODY, half), over], axis=0),
+        )
+
     for side in range(2):
         columns = slice(side * half, (side + 1) * half)
-        kinds = []
-        for kind in range(2):
-            at = (2 * kind + side) * BODY
-            body = back[:, at : at + BODY, :].reshape(EXPERTS * BODY, half)
-            kinds.append(jnp.concatenate([body, over], axis=0))
-        pairs = dot(table[side, : 2 * number], kinds[0])
-        mixed[:, columns] = (scale[0] * pairs[:number] + scale[1] * pairs[number:]).astype(BF16)
-        input_grad[:, columns] = dot(table[side, 2 * number :], kinds[1]).astype(BF16)
-
-
-def combine(table, scale, back):
-    number = scale.shape[1]
+        pairs = picked(slice(0, 2 * number), 0, side)
+        mixed[:, columns] = (gate[0] * pairs[:number] + gate[1] * pairs[number:]).astype(BF16)
+        input_grad[:, columns] = picked(slice(2 * number, 3 * number), 1, side).astype(BF16)
+
+
+def combine(in_body, in_over, gates, back):
+    number = gates.shape[1]
     width = 2 * back.shape[2]
     return pl.pallas_call(
         combine_kernel,
         out_shape=[jax.ShapeDtypeStruct((number, width), BF16)] * 2,
         compiler_params=pltpu.CompilerParams(vmem_limit_bytes=SMALL),
         name="combine",
-    )(table, scale, back)
+    )(in_body, in_over, gates, back)
+
+
+def partial_kernel(own, two, out):
+    out[...] = own[...] + two[...].astype(F32)
+
+
+def partial_sum(own, two):
+    return pl.pallas_call(
+        partial_kernel,
+        out_shape=jax.ShapeDtypeStruct(two.shape, F32),
+        compiler_params=pltpu.CompilerParams(vmem_limit_bytes=SMALL),
+        cost_estimate=LONG,
+        name="partial_sum",
+    )(own, two)
 
 
 def local(chips, tokens, routes, gates, cotangent, up_weight, down_weight):
@@ -359,17 +376,18 @@
         return sum(a.astype(F32) for a in arrays)
 
     got, back = lax.optimization_barrier((got, returns(act, dh, weights)))
-    quarter = total(keep[0], got[0])
-    for r in range(1, near):
-        chip_sum = total(keep[r], got[r]).astype(BF16)
-        arrived = moved(chip_sum, lambda core: offset_of(r, core))
-        quarter = quarter + arrived.astype(F32)
+    sums = [total(keep[r], got[r]) for r in range(near)]
+    two = moved(sums[2].astype(BF16), lambda core: offset_of(2, core))
+    partial = partial_sum(sums[0], two)
+    routes, gates, partial = lax.optimization_barrier((routes, gates, partial))
+    quarter = total(
+        partial, *[moved(sums[r].astype(BF16), lambda core: offset_of(r, core)) for r in (1, 3)]
+    )
     quarter = quarter.astype(BF16)
     arrived = [moved(quarter[j], lambda core: near * j) for j in (1, 3, 2)]
-    routes, gates, quarter = lax.optimization_barrier((routes, gates, quarter))
-    table, scale = tables(routes, gates)
+    in_body, in_over = tables(routes)
     back = lax.all_to_all(back, "expert", split_axis=0, concat_axis=0, tiled=True)
-    mixed, input_grad = combine(table, scale, back)
+    mixed, input_grad = combine(in_body, in_over, gates, back)
     mixed, input_grad, arrived = lax.optimization_barrier((mixed, input_grad, arrived))
     hidden = up_weight.shape[2]
     up_grad, down_grad = (

time: 129 us -> 127 us (0.984)
  other arithmetic: 5.17 us -> 2.77 us
    ppermute x7, waiting for transfers between devices: 9.95 us -> 12.2 us  [moved(): return lax.ppermute(array, 'dp', pairs)]
    convert_element_type x1, other arithmetic: 1.48 us -> 0.13 us  [local(): quarter = quarter.astype(BF16)]
  transfers between devices with their start and end apart: 9 -> 9, of which waited for: 3 -> 5; matrix products, arithmetic and copies ran while one was open for 2% -> 1% of each run, Pallas kernels for 3% -> 3%
where the time goes in v5:
time: 127 us; the launch traced here: 126 us
  blocking collectives  48 us (38%)
  starting transfers between devices  41.5 us (33%)
  waiting for transfers between devices  19.9 us (16%)
  Pallas kernels  13.3 us (10%)
  other arithmetic  2.77 us (2%)
    all_gather x1, blocking collectives, local(): codes = lax.all_gather(codes.astype(jnp.float16), 'dp').astype(BF16)  48 us
    ppermute x7, starting transfers between devices, moved(): return lax.ppermute(array, 'dp', pairs)  26.9 us
    ppermute x7, waiting for transfers between devices, moved(): return lax.ppermute(array, 'dp', pairs)  12.2 us
    all_to_all x1, starting transfers between devices, local(): lax.all_to_all(send, 'expert', split_axis=0, concat_axis=0, tiled=True)  7.77 us
    all_to_all x1, waiting for transfers between devices, local(): lax.all_to_all(back, 'expert', split_axis=0, concat_axis=0, tiled=True)  7.77 us
    all_to_all x1, starting transfers between devices, local(): lax.all_to_all(back, 'expert', split_axis=0, concat_axis=0, tiled=True)  6.88 us
    pallas_call x1, Pallas kernels, expert(): pl.pallas_call(expert_kernel, in_specs=[pl.BlockSpec(memory_space=pltpu.S...  5.52 us
    pallas_call x1, Pallas kernels, dispatch(): pl.pallas_call(dispatch_kernel, in_specs=[anywhere] * 6, out_specs=[anywh...  3.92 us
  transfers between devices with their start and end apart: 9, of which 5 were waited for; matrix products, arithmetic and copies ran while one was open for 1% of the time, Pallas kernels for 3%

profile of v5, /device:TPU:1, one launch (start us, length us, event | category | flops | bytes accessed | tf_op | source)
XLA Modules:
  0.0 126.4 jit_solution(3372349377972380868)
XLA Ops:
  0.6 3.9 %dispatch.1 = (bf16[16,40,2048]{2,1,0:T(8,128)(2,1)}, bf16[72,768]{1,0:T(8,128)(2,1)}) custom-call(s32[2,128]{1,0:T(2,128)} %bitcast.28, f32[2,128]{1,0:T(2,128)} %bitcast.26, bf16[1,64,384]{2,1,0:T(8,128)(2,1)} %up.1, bf16[1,64,384]{2,1,0:T(8,128)(2,1)} %down.1, bf16[128,2048]{1,0:T(8,128)(2,1)} %tokens.1, bf16[128,2048]{1,0:T(8,128)(2,1)} %cotangent.1), custom_call_target="tpu_custom_call" | custom-call | tf_op jit(solution)/shard_map/dispatch/pallas_call | solution.py:120
  4.6 0.0 copy-start.3
  4.6 7.8 %all-to-all-start = ((bf16[16,40,2048]{2,1,0:T(8,128)(2,1)}), bf16[16,40,2048]{2,1,0:T(8,128)(2,1)}, u32[]{:S(2)}, u32[]{:S(2)}) async-start(bf16[16,40,2048]{2,1,0:T(8,128)(2,1)} %get-tuple-element.25), calls=%async_computation | async-start | bytes 5242880 | tf_op jit(solution)/shard_map/all_to_all | solution.py:369
  12.4 48.0 %all-gather.2 = f16[2304,768]{1,0:T(8,128)(2,1)S(1)} all-gather(f16[72,768]{1,0:T(8,128)(2,1)S(1)} %convert_element_type.95), channel_id=2, replica_groups=mesh['dp'=32,'expert'=16] {'dp'}, dimensions={0}, use_global_device_ids=true | all-gather | bytes 3649536 | tf_op jit(solution)/shard_map/all_gather | solution.py:368
  60.4 0.6 convert_element_type.124
  61.0 0.1 pad_add_fusion.place
  61.1 0.0 all-to-all-done.received
  61.1 5.5 %expert.1 = (bf16[288,384]{1,0:T(8,128)(2,1)S(1)}, bf16[288,384]{1,0:T(8,128)(2,1)S(1)}, bf16[2048,768]{1,0:T(8,128)(2,1)S(1)}, bf16[4,4,64,768]{3,2,1,0:T(8,128)(2,1)S(1)}, bf16[4,4,64,768]{3,2,1,0:T(8,128)(2,1)S(1)}) custom-call(s32[2]{0:T(128)S(1)} %pad_add_fusion.place, bf16[16,40,2048]{2,1,0:T(8,128)(2,1)} %all-to-all-done.received, ...), custom_call_target="tpu_custom_call" | custom-call | tf_op jit(solution)/shard_map/expert/pallas_call | solution.py:218
  66.6 2.1 %collective-permute-start = (bf16[4,4,64,768]{3,2,1,0:T(8,128)(2,1)S(1)}, bf16[4,4,64,768]{3,2,1,0:T(8,128)(2,1)S(1)}, u32[]{:S(2)}, u32[]{:S(2)}) collective-permute-start(bf16[4,4,64,768]{3,2,1,0:T(8,128)(2,1)S(1)} %get-tuple-element.28), channel_id=1, source_target_pairs={{0,16},{16,0},{32,48},{48,32},{64,80},{80,64},{96,112},{112,96},{1... | collective-permute-start | bytes 4718600 | tf_op jit(solution)/shard_map/ppermute | solution.py:364
  68.7 1.6 %returns.1 = bf16[16,72,1024]{2,1,0:T(8,128)(2,1)S(1)} custom-call(bf16[288,384]{1,0:T(8,128)(2,1)S(1)} %get-tuple-element.29.act, bf16[288,384]{1,0:T(8,128)(2,1)S(1)} %get-tuple-element.30.dh, bf16[2048,768]{1,0:T(8,128)(2,1)S(1)} %get-tuple-element.31.weights), custom_call_target="tpu_custom_call" | custom-call | flops 49999998976 | bytes 1000000 | tf_op jit(solution)/shard_map/returns/pallas_call | solution.py:263
  70.3 1.6 %collective-permute-done = bf16[4,4,64,768]{3,2,1,0:T(8,128)(2,1)S(1)} collective-permute-done((bf16[4,4,64,768]{3,2,1,0:T(8,128)(2,1)S(1)}, bf16[4,4,64,768]{3,2,1,0:T(8,128)(2,1)S(1)}, u32[]{:S(2)}, u32[]{:S(2)}) %collective-permute-start) | collective-permute-done | bytes 1572896 | tf_op jit(solution)/shard_map/ppermute | solution.py:364
  71.9 1.3 fusion.1
  73.2 3.5 %collective-permute-start.1 = (bf16[4,64,768]{2,1,0:T(8,128)(2,1)}, bf16[4,64,768]{2,1,0:T(8,128)(2,1)S(1)}, u32[]{:S(2)}, u32[]{:S(2)}) collective-permute-start(bf16[4,64,768]{2,1,0:T(8,128)(2,1)} %get-tuple-element.48), channel_id=1, source_target_pairs={{0,64},{16,464},{32,96},{48,496},{64,128},{80,16},{96,160},{112,48... | collective-permute-start | bytes 1179656 | tf_op jit(solution)/shard_map/ppermute | solution.py:364
  76.7 6.9 %all-to-all-start.1 = ((bf16[16,72,1024]{2,1,0:T(8,128)(2,1)}), bf16[16,72,1024]{2,1,0:T(8,128)(2,1)S(1)}, u32[]{:S(2)}, u32[]{:S(2)}) async-start(bf16[16,72,1024]{2,1,0:T(8,128)(2,1)} %copy-done), calls=%async_computation.1 | async-start | bytes 4718592 | tf_op jit(solution)/shard_map/all_to_all | solution.py:389
  83.6 1.9 %collective-permute-start.2 = (bf16[4,64,768]{2,1,0:T(8,128)(2,1)}, bf16[4,64,768]{2,1,0:T(8,128)(2,1)S(1)}, u32[]{:S(2)}, u32[]{:S(2)}) collective-permute-start(bf16[4,64,768]{2,1,0:T(8,128)(2,1)} %get-tuple-element.46), channel_id=1, source_target_pairs={{0,32},{16,48},{32,64},{48,80},{64,96},{80,112},{96,128},{112,144}... | collective-permute-start | bytes 1179656 | tf_op jit(solution)/shard_map/ppermute | solution.py:364
  85.5 4.6 %collective-permute-start.3 = (bf16[4,64,768]{2,1,0:T(8,128)(2,1)}, bf16[4,64,768]{2,1,0:T(8,128)(2,1)S(1)}, u32[]{:S(2)}, u32[]{:S(2)}) collective-permute-start(bf16[4,64,768]{2,1,0:T(8,128)(2,1)} %get-tuple-element.47), channel_id=1, source_target_pairs={{0,480},{16,496},{32,0},{48,16},{64,32},{80,48},{96,64},{112,80},{... | collective-permute-start | bytes 1179656 | tf_op jit(solution)/shard_map/ppermute | solution.py:364
  90.1 0.0 collective-permute-done.1.two
  90.1 0.1 partial_sum.1
  90.2 0.0 copy-start.2
  90.2 0.0 copy-start.1
  90.2 7.8 %collective-permute-done.2 = bf16[4,64,768]{2,1,0:T(8,128)(2,1)S(1)} collective-permute-done((bf16[4,64,768]{2,1,0:T(8,128)(2,1)}, bf16[4,64,768]{2,1,0:T(8,128)(2,1)S(1)}, u32[]{:S(2)}, u32[]{:S(2)}) %collective-permute-start.2) | collective-permute-done | bytes 393248 | tf_op jit(solution)/shard_map/ppermute | solution.py:364
  98.0 1.0 collective-permute-done.3
  99.0 0.1 add_convert_fusion
  99.2 5.6 %collective-permute-start.6 = (bf16[64,768]{1,0:T(8,128)(2,1)S(1)}, bf16[64,768]{1,0:T(8,128)(2,1)S(1)}, u32[]{:S(2)}, u32[]{:S(2)}) collective-permute-start(bf16[64,768]{1,0:T(8,128)(2,1)S(1)} %get-tuple-element.53), channel_id=1, source_target_pairs={{0,256},{16,272},{32,288},{48,304},{64,320},{80,336},{96,352},{112... | collective-permute-start | bytes 294920 | tf_op jit(solution)/shard_map/ppermute | solution.py:364
  104.8 5.1 %collective-permute-start.5 = (bf16[64,768]{1,0:T(8,128)(2,1)S(1)}, bf16[64,768]{1,0:T(8,128)(2,1)S(1)}, u32[]{:S(2)}, u32[]{:S(2)}) collective-permute-start(bf16[64,768]{1,0:T(8,128)(2,1)S(1)} %get-tuple-element.54), channel_id=1, source_target_pairs={{0,384},{16,400},{32,416},{48,432},{64,448},{80,464},{96,480},{112... | collective-permute-start | bytes 294920 | tf_op jit(solution)/shard_map/ppermute | solution.py:364
  109.9 4.1 %collective-permute-start.4 = (bf16[64,768]{1,0:T(8,128)(2,1)S(1)}, bf16[64,768]{1,0:T(8,128)(2,1)S(1)}, u32[]{:S(2)}, u32[]{:S(2)}) collective-permute-start(bf16[64,768]{1,0:T(8,128)(2,1)S(1)} %get-tuple-element.55), channel_id=1, source_target_pairs={{0,128},{16,144},{32,160},{48,176},{64,192},{80,208},{96,224},{112... | collective-permute-start | bytes 294920 | tf_op jit(solution)/shard_map/ppermute | solution.py:364
  114.0 0.3 tables.1
  114.4 7.8 %all-to-all-done.1.back = bf16[16,72,1024]{2,1,0:T(8,128)(2,1)S(1)} async-done(((bf16[16,72,1024]{2,1,0:T(8,128)(2,1)}), bf16[16,72,1024]{2,1,0:T(8,128)(2,1)S(1)}, u32[]{:S(2)}, u32[]{:S(2)}) %all-to-all-start.1) | async-done | bytes 2359328 | tf_op jit(solution)/shard_map/all_to_all | solution.py:389
  122.1 1.9 %combine.1 = (bf16[128,2048]{1,0:T(8,128)(2,1)}, bf16[128,2048]{1,0:T(8,128)(2,1)}) custom-call(bf16[384,256]{1,0:T(8,128)(2,1)S(1)} %get-tuple-element.34.in_body, bf16[2,384,128]{2,1,0:T(8,128)(2,1)S(1)} %get-tuple-element.35.in_over, f32[2,128]{1,0:T(2,128)S(1)} %bitcast.27, bf16[16,72,1024]{2,1,0:T(8,128)(2,1)S(1)} %all-to-all-done.1.back), custom_call_target="tpu_custom_call" | custom-call | tf_op jit(solution)/shard_map/combine/pallas_call | solution.py:332
  124.0 1.7 %collective-permute-done.5 = bf16[64,768]{1,0:T(8,128)(2,1)S(1)} collective-permute-done((bf16[64,768]{1,0:T(8,128)(2,1)S(1)}, bf16[64,768]{1,0:T(8,128)(2,1)S(1)}, u32[]{:S(2)}, u32[]{:S(2)}) %collective-permute-start.5) | collective-permute-done | bytes 98336 | tf_op jit(solution)/shard_map/ppermute | solution.py:364
  125.7 0.0 collective-permute-done.4
  125.7 0.7 fusion.4
  (8 shorter events, 0.1 us)
Async XLA Ops:
  4.6 7.8 %copy-start.3 = (bf16[72,768]{1,0:T(8,128)(2,1)S(1)}, bf16[72,768]{1,0:T(8,128)(2,1)}, u32[]{:S(2)}) copy-start(bf16[72,768]{1,0:T(8,128)(2,1)} %get-tuple-element.26) | copy-start | bytes 331780
  4.6 56.5 %all-to-all-start = ((bf16[16,40,2048]{2,1,0:T(8,128)(2,1)}), bf16[16,40,2048]{2,1,0:T(8,128)(2,1)}, u32[]{:S(2)}, u32[]{:S(2)}) async-start(bf16[16,40,2048]{2,1,0:T(8,128)(2,1)} %get-tuple-element.25), calls=%async_computation | async-start | bytes 5242880 | tf_op jit(solution)/shard_map/all_to_all | solution.py:369
  66.6 5.3 %collective-permute-start = (bf16[4,4,64,768]{3,2,1,0:T(8,128)(2,1)S(1)}, bf16[4,4,64,768]{3,2,1,0:T(8,128)(2,1)S(1)}, u32[]{:S(2)}, u32[]{:S(2)}) collective-permute-start(bf16[4,4,64,768]{3,2,1,0:T(8,128)(2,1)S(1)} %get-tuple-element.28), channel_id=1, source_target_pairs={{0,16},{16,0},{32,48},{48,32},{64,80},{80,64},{96,112},{112,96},{1... | collective-permute-start | bytes 4718600 | tf_op jit(solution)/shard_map/ppermute | solution.py:364
  70.3 2.9 %copy-start = (bf16[16,72,1024]{2,1,0:T(8,128)(2,1)}, bf16[16,72,1024]{2,1,0:T(8,128)(2,1)S(1)}, u32[]{:S(2)}) copy-start(bf16[16,72,1024]{2,1,0:T(8,128)(2,1)S(1)} %returns.1) | copy-start | bytes 7077892
  73.2 16.9 %collective-permute-start.1 = (bf16[4,64,768]{2,1,0:T(8,128)(2,1)}, bf16[4,64,768]{2,1,0:T(8,128)(2,1)S(1)}, u32[]{:S(2)}, u32[]{:S(2)}) collective-permute-start(bf16[4,64,768]{2,1,0:T(8,128)(2,1)} %get-tuple-element.48), channel_id=1, source_target_pairs={{0,64},{16,464},{32,96},{48,496},{64,128},{80,16},{96,160},{112,48... | collective-permute-start | bytes 1179656 | tf_op jit(solution)/shard_map/ppermute | solution.py:364
  76.7 45.5 %all-to-all-start.1 = ((bf16[16,72,1024]{2,1,0:T(8,128)(2,1)}), bf16[16,72,1024]{2,1,0:T(8,128)(2,1)S(1)}, u32[]{:S(2)}, u32[]{:S(2)}) async-start(bf16[16,72,1024]{2,1,0:T(8,128)(2,1)} %copy-done), calls=%async_computation.1 | async-start | bytes 4718592 | tf_op jit(solution)/shard_map/all_to_all | solution.py:389
  83.6 14.4 %collective-permute-start.2 = (bf16[4,64,768]{2,1,0:T(8,128)(2,1)}, bf16[4,64,768]{2,1,0:T(8,128)(2,1)S(1)}, u32[]{:S(2)}, u32[]{:S(2)}) collective-permute-start(bf16[4,64,768]{2,1,0:T(8,128)(2,1)} %get-tuple-element.46), channel_id=1, source_target_pairs={{0,32},{16,48},{32,64},{48,80},{64,96},{80,112},{96,128},{112,144}... | collective-permute-start | bytes 1179656 | tf_op jit(solution)/shard_map/ppermute | solution.py:364
  85.5 13.5 %collective-permute-start.3 = (bf16[4,64,768]{2,1,0:T(8,128)(2,1)}, bf16[4,64,768]{2,1,0:T(8,128)(2,1)S(1)}, u32[]{:S(2)}, u32[]{:S(2)}) collective-permute-start(bf16[4,64,768]{2,1,0:T(8,128)(2,1)} %get-tuple-element.47), channel_id=1, source_target_pairs={{0,480},{16,496},{32,0},{48,16},{64,32},{80,48},{96,64},{112,80},{... | collective-permute-start | bytes 1179656 | tf_op jit(solution)/shard_map/ppermute | solution.py:364
  90.2 23.9 %copy-start.2 = (s32[128,2]{0,1:T(2,128)S(1)}, s32[128,2]{0,1:T(2,128)}, u32[]{:S(2)}) copy-start(s32[128,2]{0,1:T(2,128)} %param.7) | copy-start | bytes 3076
  90.2 32.0 %copy-start.1 = (f32[128,2]{0,1:T(2,128)S(1)}, f32[128,2]{0,1:T(2,128)}, u32[]{:S(2)}) copy-start(f32[128,2]{0,1:T(2,128)} %param.8) | copy-start | bytes 3076
  99.2 24.8 %collective-permute-start.6 = (bf16[64,768]{1,0:T(8,128)(2,1)S(1)}, bf16[64,768]{1,0:T(8,128)(2,1)S(1)}, u32[]{:S(2)}, u32[]{:S(2)}) collective-permute-start(bf16[64,768]{1,0:T(8,128)(2,1)S(1)} %get-tuple-element.53), channel_id=1, source_target_pairs={{0,256},{16,272},{32,288},{48,304},{64,320},{80,336},{96,352},{112... | collective-permute-start | bytes 294920 | tf_op jit(solution)/shard_map/ppermute | solution.py:364
  104.8 20.9 %collective-permute-start.5 = (bf16[64,768]{1,0:T(8,128)(2,1)S(1)}, bf16[64,768]{1,0:T(8,128)(2,1)S(1)}, u32[]{:S(2)}, u32[]{:S(2)}) collective-permute-start(bf16[64,768]{1,0:T(8,128)(2,1)S(1)} %get-tuple-element.54), channel_id=1, source_target_pairs={{0,384},{16,400},{32,416},{48,432},{64,448},{80,464},{96,480},{112... | collective-permute-start | bytes 294920 | tf_op jit(solution)/shard_map/ppermute | solution.py:364
  109.9 15.8 %collective-permute-start.4 = (bf16[64,768]{1,0:T(8,128)(2,1)S(1)}, bf16[64,768]{1,0:T(8,128)(2,1)S(1)}, u32[]{:S(2)}, u32[]{:S(2)}) collective-permute-start(bf16[64,768]{1,0:T(8,128)(2,1)S(1)} %get-tuple-element.55), channel_id=1, source_target_pairs={{0,128},{16,144},{32,160},{48,176},{64,192},{80,208},{96,224},{112... | collective-permute-start | bytes 294920 | tf_op jit(solution)/shard_map/ppermute | solution.py:364

commit v6 on v5

--- a/solution.py
+++ b/solution.py
@@ -142,10 +142,6 @@
     )(routes, gates, up_weight, down_weight, tokens, cotangent)
 
 
-def offset_of(r, core):
-    return (0, 1, 2 - 4 * core, -1)[r]
-
-
 def ones_where(rows, columns, chosen):
     row = lax.broadcasted_iota(jnp.int32, (rows, columns), 0)
     column = lax.broadcasted_iota(jnp.int32, (rows, columns), 1)
@@ -199,9 +195,12 @@
                 for owner, out in ((core, keep), (1 - core, give)):
                     later = jnp.where(r == 3, 1, jnp.where(r == 2, owner, 0))
                     j = lax.rem(away // near + later, far)
+                    to = (r, j)
+                    if owner == 1:
+                        to = (lax.rem(near - r, near), lax.rem(far - j, far))
                     at = slice((n * CORES + owner) * share, (n * CORES + owner + 1) * share)
-                    out[r, j, :, :hidden] = halves[0][at]
-                    out[r, j, :, hidden:] = halves[1][at]
+                    out[(*to, slice(None), slice(0, hidden))] = halves[0][at]
+                    out[(*to, slice(None), slice(hidden, 2 * hidden))] = halves[1][at]
 
     for core in range(CORES):
         pl.when(mine == core)(functools.partial(parts_of, core))
@@ -377,14 +376,19 @@
 
     got, back = lax.optimization_barrier((got, returns(act, dh, weights)))
     sums = [total(keep[r], got[r]) for r in range(near)]
-    two = moved(sums[2].astype(BF16), lambda core: offset_of(2, core))
+    two = moved(sums[2].astype(BF16), lambda core: 2 - 4 * core)
     partial = partial_sum(sums[0], two)
     routes, gates, partial = lax.optimization_barrier((routes, gates, partial))
-    quarter = total(
-        partial, *[moved(sums[r].astype(BF16), lambda core: offset_of(r, core)) for r in (1, 3)]
-    )
-    quarter = quarter.astype(BF16)
-    arrived = [moved(quarter[j], lambda core: near * j) for j in (1, 3, 2)]
+    def both_ways(ahead, behind, steps):
+        turn = lambda core: steps * (1 - 2 * core)
+        return moved(ahead, turn), moved(behind, lambda core: -turn(core))
+
+    near_sums = both_ways(sums[1].astype(BF16), sums[3].astype(BF16), 1)
+    quarter = total(partial, *near_sums).astype(BF16)
+    arrived = [
+        *both_ways(quarter[1], quarter[3], near),
+        moved(quarter[2], lambda core: 2 * near),
+    ]
     in_body, in_over = tables(routes)
     back = lax.all_to_all(back, "expert", split_axis=0, concat_axis=0, tiled=True)
     mixed, input_grad = combine(in_body, in_over, gates, back)

time: 127 us -> 125 us (0.984)
  waiting for transfers between devices: 19.9 us -> 17.7 us
    ppermute x7, waiting for transfers between devices: 12.2 us -> 10.7 us  [moved(): return lax.ppermute(array, 'dp', pairs)]
  transfers between devices with their start and end apart: 9 -> 9, of which waited for: 5 -> 4; matrix products, arithmetic and copies ran while one was open for 1% -> 1% of each run, Pallas kernels for 3% -> 3%
where the time goes in v6:
time: 125 us
  blocking collectives  48 us (38%)
  starting transfers between devices  42 us (34%)
  waiting for transfers between devices  17.7 us (14%)
  Pallas kernels  13.3 us (11%)
  other arithmetic  2.77 us (2%)
    all_gather x1, blocking collectives, local(): codes = lax.all_gather(codes.astype(jnp.float16), 'dp').astype(BF16)  48 us
    ppermute x7, starting transfers between devices, moved(): return lax.ppermute(array, 'dp', pairs)  27.4 us
    ppermute x7, waiting for transfers between devices, moved(): return lax.ppermute(array, 'dp', pairs)  10.7 us
    all_to_all x1, starting transfers between devices, local(): lax.all_to_all(send, 'expert', split_axis=0, concat_axis=0, tiled=True)  7.77 us
    all_to_all x1, waiting for transfers between devices, local(): lax.all_to_all(back, 'expert', split_axis=0, concat_axis=0, tiled=True)  7.04 us
    all_to_all x1, starting transfers between devices, local(): lax.all_to_all(back, 'expert', split_axis=0, concat_axis=0, tiled=True)  6.88 us
    pallas_call x1, Pallas kernels, expert(): pl.pallas_call(expert_kernel, in_specs=[pl.BlockSpec(memory_space=pltpu.S...  5.52 us
    pallas_call x1, Pallas kernels, dispatch(): pl.pallas_call(dispatch_kernel, in_specs=[anywhere] * 6, out_specs=[anywh...  3.92 us
  transfers between devices with their start and end apart: 9, of which 4 were waited for; matrix products, arithmetic and copies ran while one was open for 1% of the time, Pallas kernels for 3%

profile of v6, /device:TPU:1, one launch (start us, length us, event | category | flops | bytes accessed | tf_op | source)
XLA Modules:
  0.0 124.7 jit_solution(12573549905368736269)
XLA Ops:
  0.6 3.9 %dispatch.1 = (bf16[16,40,2048]{2,1,0:T(8,128)(2,1)}, bf16[72,768]{1,0:T(8,128)(2,1)}) custom-call(s32[2,128]{1,0:T(2,128)} %bitcast.28, f32[2,128]{1,0:T(2,128)} %bitcast.26, bf16[1,64,384]{2,1,0:T(8,128)(2,1)} %up.1, bf16[1,64,384]{2,1,0:T(8,128)(2,1)} %down.1, bf16[128,2048]{1,0:T(8,128)(2,1)} %tokens.1, bf16[128,2048]{1,0:T(8,128)(2,1)} %cotangent.1), custom_call_target="tpu_custom_call" | custom-call | tf_op jit(solution)/shard_map/dispatch/pallas_call | solution.py:120
  4.6 0.0 copy-start.3
  4.6 7.8 %all-to-all-start = ((bf16[16,40,2048]{2,1,0:T(8,128)(2,1)}), bf16[16,40,2048]{2,1,0:T(8,128)(2,1)}, u32[]{:S(2)}, u32[]{:S(2)}) async-start(bf16[16,40,2048]{2,1,0:T(8,128)(2,1)} %get-tuple-element.25), calls=%async_computation | async-start | bytes 5242880 | tf_op jit(solution)/shard_map/all_to_all | solution.py:368
  12.4 48.0 %all-gather.2 = f16[2304,768]{1,0:T(8,128)(2,1)S(1)} all-gather(f16[72,768]{1,0:T(8,128)(2,1)S(1)} %convert_element_type.95), channel_id=2, replica_groups=mesh['dp'=32,'expert'=16] {'dp'}, dimensions={0}, use_global_device_ids=true | all-gather | bytes 3649536 | tf_op jit(solution)/shard_map/all_gather | solution.py:367
  60.4 0.6 convert_element_type.124
  61.0 0.1 pad_add_fusion.place
  61.1 0.0 all-to-all-done.received
  61.1 5.5 %expert.1 = (bf16[288,384]{1,0:T(8,128)(2,1)S(1)}, bf16[288,384]{1,0:T(8,128)(2,1)S(1)}, bf16[2048,768]{1,0:T(8,128)(2,1)S(1)}, bf16[4,4,64,768]{3,2,1,0:T(8,128)(2,1)S(1)}, bf16[4,4,64,768]{3,2,1,0:T(8,128)(2,1)S(1)}) custom-call(s32[2]{0:T(128)S(1)} %pad_add_fusion.place, bf16[16,40,2048]{2,1,0:T(8,128)(2,1)} %all-to-all-done.received, ...), custom_call_target="tpu_custom_call" | custom-call | tf_op jit(solution)/shard_map/expert/pallas_call | solution.py:217
  66.6 2.1 %collective-permute-start = (bf16[4,4,64,768]{3,2,1,0:T(8,128)(2,1)S(1)}, bf16[4,4,64,768]{3,2,1,0:T(8,128)(2,1)S(1)}, u32[]{:S(2)}, u32[]{:S(2)}) collective-permute-start(bf16[4,4,64,768]{3,2,1,0:T(8,128)(2,1)S(1)} %get-tuple-element.28), channel_id=1, source_target_pairs={{0,16},{16,0},{32,48},{48,32},{64,80},{80,64},{96,112},{112,96},{1... | collective-permute-start | bytes 4718600 | tf_op jit(solution)/shard_map/ppermute | solution.py:363
  68.7 1.6 %returns.1 = bf16[16,72,1024]{2,1,0:T(8,128)(2,1)S(1)} custom-call(bf16[288,384]{1,0:T(8,128)(2,1)S(1)} %get-tuple-element.29.act, bf16[288,384]{1,0:T(8,128)(2,1)S(1)} %get-tuple-element.30.dh, bf16[2048,768]{1,0:T(8,128)(2,1)S(1)} %get-tuple-element.31.weights), custom_call_target="tpu_custom_call" | custom-call | flops 49999998976 | bytes 1000000 | tf_op jit(solution)/shard_map/returns/pallas_call | solution.py:262
  70.3 1.6 %collective-permute-done = bf16[4,4,64,768]{3,2,1,0:T(8,128)(2,1)S(1)} collective-permute-done((bf16[4,4,64,768]{3,2,1,0:T(8,128)(2,1)S(1)}, bf16[4,4,64,768]{3,2,1,0:T(8,128)(2,1)S(1)}, u32[]{:S(2)}, u32[]{:S(2)}) %collective-permute-start) | collective-permute-done | bytes 1572896 | tf_op jit(solution)/shard_map/ppermute | solution.py:363
  71.9 1.3 %fusion.1 = (bf16[4,64,768]{2,1,0:T(8,128)(2,1)}, bf16[4,64,768]{2,1,0:T(8,128)(2,1)}, bf16[4,64,768]{2,1,0:T(8,128)(2,1)}, f32[4,64,768]{2,1,0:T(8,128)S(1)}) fusion(bf16[4,4,64,768]{3,2,1,0:T(8,128)(2,1)S(1)} %collective-permute-done, bf16[4,4,64,768]{3,2,1,0:T(8,128)(2,1)S(1)} %get-tuple-element.27), kind=kLoop, calls=%fused_computation.6 | loop fusion | flops 2949120 | bytes 5111808 | tf_op jit(solution)/shard_map/convert_element_type | solution.py:386
  73.2 3.5 %collective-permute-start.1 = (bf16[4,64,768]{2,1,0:T(8,128)(2,1)}, bf16[4,64,768]{2,1,0:T(8,128)(2,1)S(1)}, u32[]{:S(2)}, u32[]{:S(2)}) collective-permute-start(bf16[4,64,768]{2,1,0:T(8,128)(2,1)} %get-tuple-element.48), channel_id=1, source_target_pairs={{0,64},{16,464},{32,96},{48,496},{64,128},{80,16},{96,160},{112,48... | collective-permute-start | bytes 1179656 | tf_op jit(solution)/shard_map/ppermute | solution.py:363
  76.7 6.9 %all-to-all-start.1 = ((bf16[16,72,1024]{2,1,0:T(8,128)(2,1)}), bf16[16,72,1024]{2,1,0:T(8,128)(2,1)S(1)}, u32[]{:S(2)}, u32[]{:S(2)}) async-start(bf16[16,72,1024]{2,1,0:T(8,128)(2,1)} %copy-done), calls=%async_computation.1 | async-start | bytes 4718592 | tf_op jit(solution)/shard_map/all_to_all | solution.py:393
  83.6 2.6 %collective-permute-start.2 = (bf16[4,64,768]{2,1,0:T(8,128)(2,1)}, bf16[4,64,768]{2,1,0:T(8,128)(2,1)S(1)}, u32[]{:S(2)}, u32[]{:S(2)}) collective-permute-start(bf16[4,64,768]{2,1,0:T(8,128)(2,1)} %get-tuple-element.46), channel_id=1, source_target_pairs={{0,32},{16,496},{32,64},{48,16},{64,96},{80,48},{96,128},{112,80},... | collective-permute-start | bytes 1179656 | tf_op jit(solution)/shard_map/ppermute | solution.py:363
  86.2 2.7 %collective-permute-start.3 = (bf16[4,64,768]{2,1,0:T(8,128)(2,1)}, bf16[4,64,768]{2,1,0:T(8,128)(2,1)S(1)}, u32[]{:S(2)}, u32[]{:S(2)}) collective-permute-start(bf16[4,64,768]{2,1,0:T(8,128)(2,1)} %get-tuple-element.47), channel_id=1, source_target_pairs={{0,480},{16,48},{32,0},{48,80},{64,32},{80,112},{96,64},{112,144},... | collective-permute-start | bytes 1179656 | tf_op jit(solution)/shard_map/ppermute | solution.py:363
  88.9 0.1 partial_sum.1
  88.9 0.0 copy-start.2
  89.0 0.0 copy-start.1
  89.0 5.8 %collective-permute-done.2 = bf16[4,64,768]{2,1,0:T(8,128)(2,1)S(1)} collective-permute-done((bf16[4,64,768]{2,1,0:T(8,128)(2,1)}, bf16[4,64,768]{2,1,0:T(8,128)(2,1)S(1)}, u32[]{:S(2)}, u32[]{:S(2)}) %collective-permute-start.2) | collective-permute-done | bytes 393248 | tf_op jit(solution)/shard_map/ppermute | solution.py:363
  94.8 3.2 %collective-permute-done.3 = bf16[4,64,768]{2,1,0:T(8,128)(2,1)S(1)} collective-permute-done((bf16[4,64,768]{2,1,0:T(8,128)(2,1)}, bf16[4,64,768]{2,1,0:T(8,128)(2,1)S(1)}, u32[]{:S(2)}, u32[]{:S(2)}) %collective-permute-start.3) | collective-permute-done | bytes 393248 | tf_op jit(solution)/shard_map/ppermute | solution.py:363
  98.0 0.1 add_convert_fusion
  98.2 7.4 %collective-permute-start.6 = (bf16[64,768]{1,0:T(8,128)(2,1)S(1)}, bf16[64,768]{1,0:T(8,128)(2,1)S(1)}, u32[]{:S(2)}, u32[]{:S(2)}) collective-permute-start(bf16[64,768]{1,0:T(8,128)(2,1)S(1)} %get-tuple-element.53), channel_id=1, source_target_pairs={{0,256},{16,272},{32,288},{48,304},{64,320},{80,336},{96,352},{112... | collective-permute-start | bytes 294920 | tf_op jit(solution)/shard_map/ppermute | solution.py:363
  105.5 4.8 %collective-permute-start.5 = (bf16[64,768]{1,0:T(8,128)(2,1)S(1)}, bf16[64,768]{1,0:T(8,128)(2,1)S(1)}, u32[]{:S(2)}, u32[]{:S(2)}) collective-permute-start(bf16[64,768]{1,0:T(8,128)(2,1)S(1)} %get-tuple-element.54), channel_id=1, source_target_pairs={{0,384},{16,144},{32,416},{48,176},{64,448},{80,208},{96,480},{112... | collective-permute-start | bytes 294920 | tf_op jit(solution)/shard_map/ppermute | solution.py:363
  110.4 4.4 %collective-permute-start.4 = (bf16[64,768]{1,0:T(8,128)(2,1)S(1)}, bf16[64,768]{1,0:T(8,128)(2,1)S(1)}, u32[]{:S(2)}, u32[]{:S(2)}) collective-permute-start(bf16[64,768]{1,0:T(8,128)(2,1)S(1)} %get-tuple-element.55), channel_id=1, source_target_pairs={{0,128},{16,400},{32,160},{48,432},{64,192},{80,464},{96,224},{112... | collective-permute-start | bytes 294920 | tf_op jit(solution)/shard_map/ppermute | solution.py:363
  114.8 0.3 tables.1
  115.1 7.0 %all-to-all-done.1.back = bf16[16,72,1024]{2,1,0:T(8,128)(2,1)S(1)} async-done(((bf16[16,72,1024]{2,1,0:T(8,128)(2,1)}), bf16[16,72,1024]{2,1,0:T(8,128)(2,1)S(1)}, u32[]{:S(2)}, u32[]{:S(2)}) %all-to-all-start.1) | async-done | bytes 2359328 | tf_op jit(solution)/shard_map/all_to_all | solution.py:393
  122.1 1.9 %combine.1 = (bf16[128,2048]{1,0:T(8,128)(2,1)}, bf16[128,2048]{1,0:T(8,128)(2,1)}) custom-call(bf16[384,256]{1,0:T(8,128)(2,1)S(1)} %get-tuple-element.34.in_body, bf16[2,384,128]{2,1,0:T(8,128)(2,1)S(1)} %get-tuple-element.35.in_over, f32[2,128]{1,0:T(2,128)S(1)} %bitcast.27, bf16[16,72,1024]{2,1,0:T(8,128)(2,1)S(1)} %all-to-all-done.1.back), custom_call_target="tpu_custom_call" | custom-call | tf_op jit(solution)/shard_map/combine/pallas_call | solution.py:331
  124.0 0.0 collective-permute-done.6
  124.0 0.0 collective-permute-done.5
  124.0 0.0 collective-permute-done.4
  124.0 0.7 fusion.4
  (8 shorter events, 0.1 us)
Async XLA Ops:
  4.6 7.8 %copy-start.3 = (bf16[72,768]{1,0:T(8,128)(2,1)S(1)}, bf16[72,768]{1,0:T(8,128)(2,1)}, u32[]{:S(2)}) copy-start(bf16[72,768]{1,0:T(8,128)(2,1)} %get-tuple-element.26) | copy-start | bytes 331780
  4.6 56.5 %all-to-all-start = ((bf16[16,40,2048]{2,1,0:T(8,128)(2,1)}), bf16[16,40,2048]{2,1,0:T(8,128)(2,1)}, u32[]{:S(2)}, u32[]{:S(2)}) async-start(bf16[16,40,2048]{2,1,0:T(8,128)(2,1)} %get-tuple-element.25), calls=%async_computation | async-start | bytes 5242880 | tf_op jit(solution)/shard_map/all_to_all | solution.py:368
  66.6 5.3 %collective-permute-start = (bf16[4,4,64,768]{3,2,1,0:T(8,128)(2,1)S(1)}, bf16[4,4,64,768]{3,2,1,0:T(8,128)(2,1)S(1)}, u32[]{:S(2)}, u32[]{:S(2)}) collective-permute-start(bf16[4,4,64,768]{3,2,1,0:T(8,128)(2,1)S(1)} %get-tuple-element.28), channel_id=1, source_target_pairs={{0,16},{16,0},{32,48},{48,32},{64,80},{80,64},{96,112},{112,96},{1... | collective-permute-start | bytes 4718600 | tf_op jit(solution)/shard_map/ppermute | solution.py:363
  70.3 2.9 %copy-start = (bf16[16,72,1024]{2,1,0:T(8,128)(2,1)}, bf16[16,72,1024]{2,1,0:T(8,128)(2,1)S(1)}, u32[]{:S(2)}) copy-start(bf16[16,72,1024]{2,1,0:T(8,128)(2,1)S(1)} %returns.1) | copy-start | bytes 7077892
  73.2 15.7 %collective-permute-start.1 = (bf16[4,64,768]{2,1,0:T(8,128)(2,1)}, bf16[4,64,768]{2,1,0:T(8,128)(2,1)S(1)}, u32[]{:S(2)}, u32[]{:S(2)}) collective-permute-start(bf16[4,64,768]{2,1,0:T(8,128)(2,1)} %get-tuple-element.48), channel_id=1, source_target_pairs={{0,64},{16,464},{32,96},{48,496},{64,128},{80,16},{96,160},{112,48... | collective-permute-start | bytes 1179656 | tf_op jit(solution)/shard_map/ppermute | solution.py:363
  76.7 45.5 %all-to-all-start.1 = ((bf16[16,72,1024]{2,1,0:T(8,128)(2,1)}), bf16[16,72,1024]{2,1,0:T(8,128)(2,1)S(1)}, u32[]{:S(2)}, u32[]{:S(2)}) async-start(bf16[16,72,1024]{2,1,0:T(8,128)(2,1)} %copy-done), calls=%async_computation.1 | async-start | bytes 4718592 | tf_op jit(solution)/shard_map/all_to_all | solution.py:393
  83.6 11.2 %collective-permute-start.2 = (bf16[4,64,768]{2,1,0:T(8,128)(2,1)}, bf16[4,64,768]{2,1,0:T(8,128)(2,1)S(1)}, u32[]{:S(2)}, u32[]{:S(2)}) collective-permute-start(bf16[4,64,768]{2,1,0:T(8,128)(2,1)} %get-tuple-element.46), channel_id=1, source_target_pairs={{0,32},{16,496},{32,64},{48,16},{64,96},{80,48},{96,128},{112,80},... | collective-permute-start | bytes 1179656 | tf_op jit(solution)/shard_map/ppermute | solution.py:363
  86.2 11.8 %collective-permute-start.3 = (bf16[4,64,768]{2,1,0:T(8,128)(2,1)}, bf16[4,64,768]{2,1,0:T(8,128)(2,1)S(1)}, u32[]{:S(2)}, u32[]{:S(2)}) collective-permute-start(bf16[4,64,768]{2,1,0:T(8,128)(2,1)} %get-tuple-element.47), channel_id=1, source_target_pairs={{0,480},{16,48},{32,0},{48,80},{64,32},{80,112},{96,64},{112,144},... | collective-permute-start | bytes 1179656 | tf_op jit(solution)/shard_map/ppermute | solution.py:363
  88.9 25.8 %copy-start.2 = (s32[128,2]{0,1:T(2,128)S(1)}, s32[128,2]{0,1:T(2,128)}, u32[]{:S(2)}) copy-start(s32[128,2]{0,1:T(2,128)} %param.7) | copy-start | bytes 3076
  89.0 33.2 %copy-start.1 = (f32[128,2]{0,1:T(2,128)S(1)}, f32[128,2]{0,1:T(2,128)}, u32[]{:S(2)}) copy-start(f32[128,2]{0,1:T(2,128)} %param.8) | copy-start | bytes 3076
  98.2 25.8 %collective-permute-start.6 = (bf16[64,768]{1,0:T(8,128)(2,1)S(1)}, bf16[64,768]{1,0:T(8,128)(2,1)S(1)}, u32[]{:S(2)}, u32[]{:S(2)}) collective-permute-start(bf16[64,768]{1,0:T(8,128)(2,1)S(1)} %get-tuple-element.53), channel_id=1, source_target_pairs={{0,256},{16,272},{32,288},{48,304},{64,320},{80,336},{96,352},{112... | collective-permute-start | bytes 294920 | tf_op jit(solution)/shard_map/ppermute | solution.py:363
  105.5 18.5 %collective-permute-start.5 = (bf16[64,768]{1,0:T(8,128)(2,1)S(1)}, bf16[64,768]{1,0:T(8,128)(2,1)S(1)}, u32[]{:S(2)}, u32[]{:S(2)}) collective-permute-start(bf16[64,768]{1,0:T(8,128)(2,1)S(1)} %get-tuple-element.54), channel_id=1, source_target_pairs={{0,384},{16,144},{32,416},{48,176},{64,448},{80,208},{96,480},{112... | collective-permute-start | bytes 294920 | tf_op jit(solution)/shard_map/ppermute | solution.py:363
  110.4 13.6 %collective-permute-start.4 = (bf16[64,768]{1,0:T(8,128)(2,1)S(1)}, bf16[64,768]{1,0:T(8,128)(2,1)S(1)}, u32[]{:S(2)}, u32[]{:S(2)}) collective-permute-start(bf16[64,768]{1,0:T(8,128)(2,1)S(1)} %get-tuple-element.55), channel_id=1, source_target_pairs={{0,128},{16,400},{32,160},{48,432},{64,192},{80,464},{96,224},{112... | collective-permute-start | bytes 294920 | tf_op jit(solution)/shard_map/ppermute | solution.py:363

commit v7 on v6

--- a/solution.py
+++ b/solution.py
@@ -60,8 +60,7 @@
     peak = jnp.max(jnp.max(jnp.abs(rows), axis=1, keepdims=True), axis=0, keepdims=True)
     power = jnp.floor(jnp.log2(16384.0 / jnp.maximum(peak, 2.0**-100)))
     factor = jnp.exp2(power).astype(BF16).astype(F32)
-    code = (rows * factor).astype(BF16)
-    return jnp.concatenate([code, jnp.broadcast_to(power, (NOTE, rows.shape[1])).astype(BF16)], axis=0)
+    return (rows * factor).astype(BF16), power
 
 
 def dispatch_kernel(
@@ -84,9 +83,11 @@
         load.start()
     for load in small:
         load.wait()
-    hidden = up.shape[2]
-    codes[:, :hidden] = coded(up_in[0])
-    codes[:, hidden:] = coded(down_in[0])
+    share, hidden = up.shape[1:]
+    codes[:share], up_power = coded(up_in[0])
+    codes[share : 2 * share], down_power = coded(down_in[0])
+    note = lax.broadcasted_iota(jnp.int32, (NOTE, hidden), 0) < NOTE // 2
+    codes[2 * share :] = jnp.where(note, up_power, down_power).astype(BF16)
     first, second, count = named_and_earlier(routes_in[...])
     held = jnp.where(first | second, count, -2)[:, None, :]
     one, two = slots_of_rows(BLOCK, number)
@@ -123,7 +124,7 @@
         out_specs=[anywhere, pl.BlockSpec(memory_space=pltpu.VMEM)],
         out_shape=[
             jax.ShapeDtypeStruct((EXPERTS, BLOCK, width), BF16),
-            jax.ShapeDtypeStruct((share + NOTE, 2 * hidden), BF16),
+            jax.ShapeDtypeStruct((2 * share + NOTE, hidden), BF16),
         ],
         scratch_shapes=[
             pltpu.VMEM(routes.shape, jnp.int32),
@@ -152,12 +153,15 @@
     place, received, codes, act_out, dh_out, weights, keep, give, x, g
 ):
     width = received.shape[2]
-    hidden = codes.shape[2] // 2
-    share = codes.shape[1] - NOTE
+    hidden = codes.shape[2]
+    share = (codes.shape[1] - NOTE) // 2
     body = EXPERTS * BODY
     rest = EXPERTS * REST
-    factor = jnp.exp2(-codes[:, share:, :].astype(F32)).astype(BF16)[:, :1, :]
-    weights[...] = (codes[:, :share, :] * factor).reshape(weights.shape)
+    factor = jnp.exp2(-codes[:, 2 * share :, :].astype(F32)).astype(BF16)
+    for n in range(2):
+        rows = codes[:, n * share : (n + 1) * share, :]
+        here = factor[:, n * NOTE // 2 : n * NOTE // 2 + 1, :]
+        weights[:, n * hidden : (n + 1) * hidden] = (rows * here).reshape(width, hidden)
     x[:body] = received[:, :BODY, :].reshape(body, width)
     g[:body] = received[:, BODY : 2 * BODY, :].reshape(body, width)
     eight = BLOCK - 2 * BODY
@@ -208,8 +212,8 @@
 
 def expert(place, received, codes):
     width = received.shape[2]
-    wide = codes.shape[2]
-    share = codes.shape[1] - NOTE
+    wide = 2 * codes.shape[2]
+    share = (codes.shape[1] - NOTE) // 2
     rows = EXPERTS * CAP
     whole = pl.BlockSpec(memory_space=pltpu.VMEM)
     chips = width // share // CORES

time: 125 us -> 124 us (level)
  no operation moved by 1% of the time
where the time goes in v7:
time: 124 us; the launch traced here: 123 us
  blocking collectives  47.3 us (38%)
  starting transfers between devices  41.6 us (34%)
  waiting for transfers between devices  17.6 us (14%)
  Pallas kernels  13.2 us (11%)
  other arithmetic  2.77 us (2%)
    all_gather x1, blocking collectives, local(): codes = lax.all_gather(codes.astype(jnp.float16), 'dp').astype(BF16)  47.3 us
    ppermute x7, starting transfers between devices, moved(): return lax.ppermute(array, 'dp', pairs)  27.5 us
    ppermute x7, waiting for transfers between devices, moved(): return lax.ppermute(array, 'dp', pairs)  11 us
    all_to_all x1, starting transfers between devices, local(): lax.all_to_all(send, 'expert', split_axis=0, concat_axis=0, tiled=True)  7.77 us
    all_to_all x1, waiting for transfers between devices, local(): lax.all_to_all(back, 'expert', split_axis=0, concat_axis=0, tiled=True)  6.53 us
    all_to_all x1, starting transfers between devices, local(): lax.all_to_all(back, 'expert', split_axis=0, concat_axis=0, tiled=True)  6.38 us
    pallas_call x1, Pallas kernels, expert(): pl.pallas_call(expert_kernel, in_specs=[pl.BlockSpec(memory_space=pltpu.S...  5.47 us
    pallas_call x1, Pallas kernels, dispatch(): pl.pallas_call(dispatch_kernel, in_specs=[anywhere] * 6, out_specs=[anywh...  3.92 us
  transfers between devices with their start and end apart: 9, of which 4 were waited for; matrix products, arithmetic and copies ran while one was open for 1% of the time, Pallas kernels for 3%

profile of v7, /device:TPU:1, one launch (start us, length us, event | category | flops | bytes accessed | tf_op | source)
XLA Modules:
  0.0 123.4 jit_solution(11046530724164086496)
XLA Ops:
  0.6 3.9 %dispatch.1 = (bf16[16,40,2048]{2,1,0:T(8,128)(2,1)}, bf16[136,384]{1,0:T(8,128)(2,1)}) custom-call(s32[2,128]{1,0:T(2,128)} %bitcast.28, f32[2,128]{1,0:T(2,128)} %bitcast.26, bf16[1,64,384]{2,1,0:T(8,128)(2,1)} %up.1, bf16[1,64,384]{2,1,0:T(8,128)(2,1)} %down.1, bf16[128,2048]{1,0:T(8,128)(2,1)} %tokens.1, bf16[128,2048]{1,0:T(8,128)(2,1)} %cotangent.1), custom_call_target="tpu_custom_call" | custom-call | tf_op jit(solution)/shard_map/dispatch/pallas_call | solution.py:121
  4.6 0.0 copy-start.3
  4.6 7.8 %all-to-all-start = ((bf16[16,40,2048]{2,1,0:T(8,128)(2,1)}), bf16[16,40,2048]{2,1,0:T(8,128)(2,1)}, u32[]{:S(2)}, u32[]{:S(2)}) async-start(bf16[16,40,2048]{2,1,0:T(8,128)(2,1)} %get-tuple-element.25), calls=%async_computation | async-start | bytes 5242880 | tf_op jit(solution)/shard_map/all_to_all | solution.py:372
  12.4 47.3 %all-gather.2 = f16[4352,384]{1,0:T(8,128)(2,1)S(1)} all-gather(f16[136,384]{1,0:T(8,128)(2,1)S(1)} %convert_element_type.95), channel_id=2, replica_groups=mesh['dp'=32,'expert'=16] {'dp'}, dimensions={0}, use_global_device_ids=true | all-gather | bytes 3446784 | tf_op jit(solution)/shard_map/all_gather | solution.py:371
  59.7 0.6 convert_element_type.124
  60.3 0.1 pad_add_fusion.place
  60.4 0.0 all-to-all-done.received
  60.4 5.5 %expert.1 = (bf16[288,384]{1,0:T(8,128)(2,1)S(1)}, bf16[288,384]{1,0:T(8,128)(2,1)S(1)}, bf16[2048,768]{1,0:T(8,128)(2,1)S(1)}, bf16[4,4,64,768]{3,2,1,0:T(8,128)(2,1)S(1)}, bf16[4,4,64,768]{3,2,1,0:T(8,128)(2,1)S(1)}) custom-call(s32[2]{0:T(128)S(1)} %pad_add_fusion.place, bf16[16,40,2048]{2,1,0:T(8,128)(2,1)} %all-to-all-done.received, ...), custom_call_target="tpu_custom_call" | custom-call | tf_op jit(solution)/shard_map/expert/pallas_call | solution.py:221
  65.9 2.1 %collective-permute-start = (bf16[4,4,64,768]{3,2,1,0:T(8,128)(2,1)S(1)}, bf16[4,4,64,768]{3,2,1,0:T(8,128)(2,1)S(1)}, u32[]{:S(2)}, u32[]{:S(2)}) collective-permute-start(bf16[4,4,64,768]{3,2,1,0:T(8,128)(2,1)S(1)} %get-tuple-element.28), channel_id=1, source_target_pairs={{0,16},{16,0},{32,48},{48,32},{64,80},{80,64},{96,112},{112,96},{1... | collective-permute-start | bytes 4718600 | tf_op jit(solution)/shard_map/ppermute | solution.py:367
  68.0 1.6 %returns.1 = bf16[16,72,1024]{2,1,0:T(8,128)(2,1)S(1)} custom-call(bf16[288,384]{1,0:T(8,128)(2,1)S(1)} %get-tuple-element.29.act, bf16[288,384]{1,0:T(8,128)(2,1)S(1)} %get-tuple-element.30.dh, bf16[2048,768]{1,0:T(8,128)(2,1)S(1)} %get-tuple-element.31.weights), custom_call_target="tpu_custom_call" | custom-call | flops 49999998976 | bytes 1000000 | tf_op jit(solution)/shard_map/returns/pallas_call | solution.py:266
  69.6 1.6 %collective-permute-done = bf16[4,4,64,768]{3,2,1,0:T(8,128)(2,1)S(1)} collective-permute-done((bf16[4,4,64,768]{3,2,1,0:T(8,128)(2,1)S(1)}, bf16[4,4,64,768]{3,2,1,0:T(8,128)(2,1)S(1)}, u32[]{:S(2)}, u32[]{:S(2)}) %collective-permute-start) | collective-permute-done | bytes 1572896 | tf_op jit(solution)/shard_map/ppermute | solution.py:367
  71.2 1.3 %fusion.1 = (bf16[4,64,768]{2,1,0:T(8,128)(2,1)}, bf16[4,64,768]{2,1,0:T(8,128)(2,1)}, bf16[4,64,768]{2,1,0:T(8,128)(2,1)}, f32[4,64,768]{2,1,0:T(8,128)S(1)}) fusion(bf16[4,4,64,768]{3,2,1,0:T(8,128)(2,1)S(1)} %collective-permute-done, bf16[4,4,64,768]{3,2,1,0:T(8,128)(2,1)S(1)} %get-tuple-element.27), kind=kLoop, calls=%fused_computation.6 | loop fusion | flops 2949120 | bytes 5111808 | tf_op jit(solution)/shard_map/convert_element_type | solution.py:390
  72.4 3.9 %collective-permute-start.1 = (bf16[4,64,768]{2,1,0:T(8,128)(2,1)}, bf16[4,64,768]{2,1,0:T(8,128)(2,1)S(1)}, u32[]{:S(2)}, u32[]{:S(2)}) collective-permute-start(bf16[4,64,768]{2,1,0:T(8,128)(2,1)} %get-tuple-element.48), channel_id=1, source_target_pairs={{0,64},{16,464},{32,96},{48,496},{64,128},{80,16},{96,160},{112,48... | collective-permute-start | bytes 1179656 | tf_op jit(solution)/shard_map/ppermute | solution.py:367
  76.4 6.4 %all-to-all-start.1 = ((bf16[16,72,1024]{2,1,0:T(8,128)(2,1)}), bf16[16,72,1024]{2,1,0:T(8,128)(2,1)S(1)}, u32[]{:S(2)}, u32[]{:S(2)}) async-start(bf16[16,72,1024]{2,1,0:T(8,128)(2,1)} %copy-done), calls=%async_computation.1 | async-start | bytes 4718592 | tf_op jit(solution)/shard_map/all_to_all | solution.py:397
  82.8 2.6 %collective-permute-start.2 = (bf16[4,64,768]{2,1,0:T(8,128)(2,1)}, bf16[4,64,768]{2,1,0:T(8,128)(2,1)S(1)}, u32[]{:S(2)}, u32[]{:S(2)}) collective-permute-start(bf16[4,64,768]{2,1,0:T(8,128)(2,1)} %get-tuple-element.46), channel_id=1, source_target_pairs={{0,32},{16,496},{32,64},{48,16},{64,96},{80,48},{96,128},{112,80},... | collective-permute-start | bytes 1179656 | tf_op jit(solution)/shard_map/ppermute | solution.py:367
  85.4 2.7 %collective-permute-start.3 = (bf16[4,64,768]{2,1,0:T(8,128)(2,1)}, bf16[4,64,768]{2,1,0:T(8,128)(2,1)S(1)}, u32[]{:S(2)}, u32[]{:S(2)}) collective-permute-start(bf16[4,64,768]{2,1,0:T(8,128)(2,1)} %get-tuple-element.47), channel_id=1, source_target_pairs={{0,480},{16,48},{32,0},{48,80},{64,32},{80,112},{96,64},{112,144},... | collective-permute-start | bytes 1179656 | tf_op jit(solution)/shard_map/ppermute | solution.py:367
  88.1 0.1 partial_sum.1
  88.2 0.0 copy-start.2
  88.2 0.0 copy-start.1
  88.2 5.5 %collective-permute-done.2 = bf16[4,64,768]{2,1,0:T(8,128)(2,1)S(1)} collective-permute-done((bf16[4,64,768]{2,1,0:T(8,128)(2,1)}, bf16[4,64,768]{2,1,0:T(8,128)(2,1)S(1)}, u32[]{:S(2)}, u32[]{:S(2)}) %collective-permute-start.2) | collective-permute-done | bytes 393248 | tf_op jit(solution)/shard_map/ppermute | solution.py:367
  93.7 3.9 %collective-permute-done.3 = bf16[4,64,768]{2,1,0:T(8,128)(2,1)S(1)} collective-permute-done((bf16[4,64,768]{2,1,0:T(8,128)(2,1)}, bf16[4,64,768]{2,1,0:T(8,128)(2,1)S(1)}, u32[]{:S(2)}, u32[]{:S(2)}) %collective-permute-start.3) | collective-permute-done | bytes 393248 | tf_op jit(solution)/shard_map/ppermute | solution.py:367
  97.6 0.1 add_convert_fusion
  97.7 7.0 %collective-permute-start.6 = (bf16[64,768]{1,0:T(8,128)(2,1)S(1)}, bf16[64,768]{1,0:T(8,128)(2,1)S(1)}, u32[]{:S(2)}, u32[]{:S(2)}) collective-permute-start(bf16[64,768]{1,0:T(8,128)(2,1)S(1)} %get-tuple-element.53), channel_id=1, source_target_pairs={{0,256},{16,272},{32,288},{48,304},{64,320},{80,336},{96,352},{112... | collective-permute-start | bytes 294920 | tf_op jit(solution)/shard_map/ppermute | solution.py:367
  104.8 4.8 %collective-permute-start.5 = (bf16[64,768]{1,0:T(8,128)(2,1)S(1)}, bf16[64,768]{1,0:T(8,128)(2,1)S(1)}, u32[]{:S(2)}, u32[]{:S(2)}) collective-permute-start(bf16[64,768]{1,0:T(8,128)(2,1)S(1)} %get-tuple-element.54), channel_id=1, source_target_pairs={{0,384},{16,144},{32,416},{48,176},{64,448},{80,208},{96,480},{112... | collective-permute-start | bytes 294920 | tf_op jit(solution)/shard_map/ppermute | solution.py:367
  109.6 4.4 %collective-permute-start.4 = (bf16[64,768]{1,0:T(8,128)(2,1)S(1)}, bf16[64,768]{1,0:T(8,128)(2,1)S(1)}, u32[]{:S(2)}, u32[]{:S(2)}) collective-permute-start(bf16[64,768]{1,0:T(8,128)(2,1)S(1)} %get-tuple-element.55), channel_id=1, source_target_pairs={{0,128},{16,400},{32,160},{48,432},{64,192},{80,464},{96,224},{112... | collective-permute-start | bytes 294920 | tf_op jit(solution)/shard_map/ppermute | solution.py:367
  114.0 0.3 tables.1
  114.3 6.5 %all-to-all-done.1.back = bf16[16,72,1024]{2,1,0:T(8,128)(2,1)S(1)} async-done(((bf16[16,72,1024]{2,1,0:T(8,128)(2,1)}), bf16[16,72,1024]{2,1,0:T(8,128)(2,1)S(1)}, u32[]{:S(2)}, u32[]{:S(2)}) %all-to-all-start.1) | async-done | bytes 2359328 | tf_op jit(solution)/shard_map/all_to_all | solution.py:397
  120.8 1.9 %combine.1 = (bf16[128,2048]{1,0:T(8,128)(2,1)}, bf16[128,2048]{1,0:T(8,128)(2,1)}) custom-call(bf16[384,256]{1,0:T(8,128)(2,1)S(1)} %get-tuple-element.34.in_body, bf16[2,384,128]{2,1,0:T(8,128)(2,1)S(1)} %get-tuple-element.35.in_over, f32[2,128]{1,0:T(2,128)S(1)} %bitcast.27, bf16[16,72,1024]{2,1,0:T(8,128)(2,1)S(1)} %all-to-all-done.1.back), custom_call_target="tpu_custom_call" | custom-call | tf_op jit(solution)/shard_map/combine/pallas_call | solution.py:335
  122.7 0.0 collective-permute-done.6
  122.7 0.0 collective-permute-done.5
  122.7 0.0 collective-permute-done.4
  122.7 0.7 fusion.4
  (8 shorter events, 0.1 us)
Async XLA Ops:
  4.6 7.8 %copy-start.3 = (bf16[136,384]{1,0:T(8,128)(2,1)S(1)}, bf16[136,384]{1,0:T(8,128)(2,1)}, u32[]{:S(2)}) copy-start(bf16[136,384]{1,0:T(8,128)(2,1)} %get-tuple-element.26) | copy-start | bytes 313348
  4.6 55.8 %all-to-all-start = ((bf16[16,40,2048]{2,1,0:T(8,128)(2,1)}), bf16[16,40,2048]{2,1,0:T(8,128)(2,1)}, u32[]{:S(2)}, u32[]{:S(2)}) async-start(bf16[16,40,2048]{2,1,0:T(8,128)(2,1)} %get-tuple-element.25), calls=%async_computation | async-start | bytes 5242880 | tf_op jit(solution)/shard_map/all_to_all | solution.py:372
  65.9 5.3 %collective-permute-start = (bf16[4,4,64,768]{3,2,1,0:T(8,128)(2,1)S(1)}, bf16[4,4,64,768]{3,2,1,0:T(8,128)(2,1)S(1)}, u32[]{:S(2)}, u32[]{:S(2)}) collective-permute-start(bf16[4,4,64,768]{3,2,1,0:T(8,128)(2,1)S(1)} %get-tuple-element.28), channel_id=1, source_target_pairs={{0,16},{16,0},{32,48},{48,32},{64,80},{80,64},{96,112},{112,96},{1... | collective-permute-start | bytes 4718600 | tf_op jit(solution)/shard_map/ppermute | solution.py:367
  69.6 2.9 %copy-start = (bf16[16,72,1024]{2,1,0:T(8,128)(2,1)}, bf16[16,72,1024]{2,1,0:T(8,128)(2,1)S(1)}, u32[]{:S(2)}) copy-start(bf16[16,72,1024]{2,1,0:T(8,128)(2,1)S(1)} %returns.1) | copy-start | bytes 7077892
  72.4 15.6 %collective-permute-start.1 = (bf16[4,64,768]{2,1,0:T(8,128)(2,1)}, bf16[4,64,768]{2,1,0:T(8,128)(2,1)S(1)}, u32[]{:S(2)}, u32[]{:S(2)}) collective-permute-start(bf16[4,64,768]{2,1,0:T(8,128)(2,1)} %get-tuple-element.48), channel_id=1, source_target_pairs={{0,64},{16,464},{32,96},{48,496},{64,128},{80,16},{96,160},{112,48... | collective-permute-start | bytes 1179656 | tf_op jit(solution)/shard_map/ppermute | solution.py:367
  76.4 44.4 %all-to-all-start.1 = ((bf16[16,72,1024]{2,1,0:T(8,128)(2,1)}), bf16[16,72,1024]{2,1,0:T(8,128)(2,1)S(1)}, u32[]{:S(2)}, u32[]{:S(2)}) async-start(bf16[16,72,1024]{2,1,0:T(8,128)(2,1)} %copy-done), calls=%async_computation.1 | async-start | bytes 4718592 | tf_op jit(solution)/shard_map/all_to_all | solution.py:397
  82.8 10.9 %collective-permute-start.2 = (bf16[4,64,768]{2,1,0:T(8,128)(2,1)}, bf16[4,64,768]{2,1,0:T(8,128)(2,1)S(1)}, u32[]{:S(2)}, u32[]{:S(2)}) collective-permute-start(bf16[4,64,768]{2,1,0:T(8,128)(2,1)} %get-tuple-element.46), channel_id=1, source_target_pairs={{0,32},{16,496},{32,64},{48,16},{64,96},{80,48},{96,128},{112,80},... | collective-permute-start | bytes 1179656 | tf_op jit(solution)/shard_map/ppermute | solution.py:367
  85.4 12.2 %collective-permute-start.3 = (bf16[4,64,768]{2,1,0:T(8,128)(2,1)}, bf16[4,64,768]{2,1,0:T(8,128)(2,1)S(1)}, u32[]{:S(2)}, u32[]{:S(2)}) collective-permute-start(bf16[4,64,768]{2,1,0:T(8,128)(2,1)} %get-tuple-element.47), channel_id=1, source_target_pairs={{0,480},{16,48},{32,0},{48,80},{64,32},{80,112},{96,64},{112,144},... | collective-permute-start | bytes 1179656 | tf_op jit(solution)/shard_map/ppermute | solution.py:367
  88.2 25.8 %copy-start.2 = (s32[128,2]{0,1:T(2,128)S(1)}, s32[128,2]{0,1:T(2,128)}, u32[]{:S(2)}) copy-start(s32[128,2]{0,1:T(2,128)} %param.7) | copy-start | bytes 3076
  88.2 32.7 %copy-start.1 = (f32[128,2]{0,1:T(2,128)S(1)}, f32[128,2]{0,1:T(2,128)}, u32[]{:S(2)}) copy-start(f32[128,2]{0,1:T(2,128)} %param.8) | copy-start | bytes 3076
  97.7 25.0 %collective-permute-start.6 = (bf16[64,768]{1,0:T(8,128)(2,1)S(1)}, bf16[64,768]{1,0:T(8,128)(2,1)S(1)}, u32[]{:S(2)}, u32[]{:S(2)}) collective-permute-start(bf16[64,768]{1,0:T(8,128)(2,1)S(1)} %get-tuple-element.53), channel_id=1, source_target_pairs={{0,256},{16,272},{32,288},{48,304},{64,320},{80,336},{96,352},{112... | collective-permute-start | bytes 294920 | tf_op jit(solution)/shard_map/ppermute | solution.py:367
  104.8 17.9 %collective-permute-start.5 = (bf16[64,768]{1,0:T(8,128)(2,1)S(1)}, bf16[64,768]{1,0:T(8,128)(2,1)S(1)}, u32[]{:S(2)}, u32[]{:S(2)}) collective-permute-start(bf16[64,768]{1,0:T(8,128)(2,1)S(1)} %get-tuple-element.54), channel_id=1, source_target_pairs={{0,384},{16,144},{32,416},{48,176},{64,448},{80,208},{96,480},{112... | collective-permute-start | bytes 294920 | tf_op jit(solution)/shard_map/ppermute | solution.py:367
  109.6 13.1 %collective-permute-start.4 = (bf16[64,768]{1,0:T(8,128)(2,1)S(1)}, bf16[64,768]{1,0:T(8,128)(2,1)S(1)}, u32[]{:S(2)}, u32[]{:S(2)}) collective-permute-start(bf16[64,768]{1,0:T(8,128)(2,1)S(1)} %get-tuple-element.55), channel_id=1, source_target_pairs={{0,128},{16,400},{32,160},{48,432},{64,192},{80,464},{96,224},{112... | collective-permute-start | bytes 294920 | tf_op jit(solution)/shard_map/ppermute | solution.py:367

commit v8 on v7

--- a/solution.py
+++ b/solution.py
@@ -149,19 +149,34 @@
     return jnp.where(chosen(row) == column, 1.0, 0.0).astype(BF16)
 
 
-def expert_kernel(
-    place, received, codes, act_out, dh_out, weights, keep, give, x, g
-):
-    width = received.shape[2]
-    hidden = codes.shape[2]
+def decode_kernel(codes, weights):
+    width, hidden = weights.shape[0], codes.shape[2]
     share = (codes.shape[1] - NOTE) // 2
-    body = EXPERTS * BODY
-    rest = EXPERTS * REST
     factor = jnp.exp2(-codes[:, 2 * share :, :].astype(F32)).astype(BF16)
     for n in range(2):
         rows = codes[:, n * share : (n + 1) * share, :]
         here = factor[:, n * NOTE // 2 : n * NOTE // 2 + 1, :]
         weights[:, n * hidden : (n + 1) * hidden] = (rows * here).reshape(width, hidden)
+
+
+def decode(codes):
+    devices, rows, hidden = codes.shape
+    return pl.pallas_call(
+        decode_kernel,
+        out_shape=jax.ShapeDtypeStruct((devices * (rows - NOTE) // 2, 2 * hidden), BF16),
+        compiler_params=pltpu.CompilerParams(vmem_limit_bytes=LARGE),
+        name="decode",
+    )(codes)
+
+
+def expert_kernel(
+    place, received, weights, act_out, dh_out, keep, give, x, g
+):
+    width = received.shape[2]
+    hidden = weights.shape[1] // 2
+    share = keep.shape[2]
+    body = EXPERTS * BODY
+    rest = EXPERTS * REST
     x[:body] = received[:, :BODY, :].reshape(body, width)
     g[:body] = received[:, BODY : 2 * BODY, :].reshape(body, width)
     eight = BLOCK - 2 * BODY
@@ -210,10 +225,8 @@
         pl.when(mine == core)(functools.partial(parts_of, core))
 
 
-def expert(place, received, codes):
-    width = received.shape[2]
-    wide = 2 * codes.shape[2]
-    share = (codes.shape[1] - NOTE) // 2
+def expert(place, received, weights, share):
+    width, wide = weights.shape
     rows = EXPERTS * CAP
     whole = pl.BlockSpec(memory_space=pltpu.VMEM)
     chips = width // share // CORES
@@ -221,11 +234,10 @@
     return pl.pallas_call(
         expert_kernel,
         in_specs=[pl.BlockSpec(memory_space=pltpu.SMEM), whole, whole],
-        out_specs=[whole] * 5,
+        out_specs=[whole] * 4,
         out_shape=[
             jax.ShapeDtypeStruct((rows, wide // 2), BF16),
             jax.ShapeDtypeStruct((rows, wide // 2), BF16),
-            jax.ShapeDtypeStruct((width, wide), BF16),
             jax.ShapeDtypeStruct((near, chips // near, share, wide), BF16),
             jax.ShapeDtypeStruct((near, chips // near, share, wide), BF16),
         ],
@@ -235,7 +247,7 @@
         ],
         compiler_params=pltpu.CompilerParams(vmem_limit_bytes=LARGE),
         name="expert",
-    )(place, received, codes)
+    )(place, received, weights)
 
 
 def return_kernel(act, dh, weights, back):
@@ -372,7 +384,8 @@
     received = lax.all_to_all(send, "expert", split_axis=0, concat_axis=0, tiled=True)
     me = lax.axis_index("dp").astype(jnp.int32)
     place = jnp.stack([me // CORES, me % CORES])
-    act, dh, weights, keep, give = expert(place, received, codes)
+    weights = decode(codes)
+    act, dh, keep, give = expert(place, received, weights, up_weight.shape[1])
     got = moved(give, None)
 
     def total(*arrays):

time: 124 us -> 124 us (level)
  no operation moved by 1% of the time
where the time goes in v8:
time: 124 us
  blocking collectives  47.3 us (38%)
  starting transfers between devices  41.6 us (34%)
  waiting for transfers between devices  17.4 us (14%)
  Pallas kernels  13.5 us (11%)
  other arithmetic  2.77 us (2%)
    all_gather x1, blocking collectives, local(): codes = lax.all_gather(codes.astype(jnp.float16), 'dp').astype(BF16)  47.3 us
    ppermute x7, starting transfers between devices, moved(): return lax.ppermute(array, 'dp', pairs)  27.1 us
    ppermute x7, waiting for transfers between devices, moved(): return lax.ppermute(array, 'dp', pairs)  11 us
    all_to_all x1, starting transfers between devices, local(): lax.all_to_all(send, 'expert', split_axis=0, concat_axis=0, tiled=True)  7.77 us
    all_to_all x1, starting transfers between devices, local(): lax.all_to_all(back, 'expert', split_axis=0, concat_axis=0, tiled=True)  6.75 us
    all_to_all x1, waiting for transfers between devices, local(): lax.all_to_all(back, 'expert', split_axis=0, concat_axis=0, tiled=True)  6.38 us
    pallas_call x1, Pallas kernels, expert(): pl.pallas_call(expert_kernel, in_specs=[pl.BlockSpec(memory_space=pltpu.S...  5.43 us
    pallas_call x1, Pallas kernels, dispatch(): pl.pallas_call(dispatch_kernel, in_specs=[anywhere] * 6, out_specs=[anywh...  3.92 us
  transfers between devices with their start and end apart: 9, of which 4 were waited for; matrix products, arithmetic and copies ran while one was open for 1% of the time, Pallas kernels for 3%

profile of v8, /device:TPU:1, one launch (start us, length us, event | category | flops | bytes accessed | tf_op | source)
XLA Modules:
  0.0 123.6 jit_solution(10167130744399153678)
XLA Ops:
  0.6 3.9 %dispatch.1 = (bf16[16,40,2048]{2,1,0:T(8,128)(2,1)}, bf16[136,384]{1,0:T(8,128)(2,1)}) custom-call(s32[2,128]{1,0:T(2,128)} %bitcast.28, f32[2,128]{1,0:T(2,128)} %bitcast.26, bf16[1,64,384]{2,1,0:T(8,128)(2,1)} %up.1, bf16[1,64,384]{2,1,0:T(8,128)(2,1)} %down.1, bf16[128,2048]{1,0:T(8,128)(2,1)} %tokens.1, bf16[128,2048]{1,0:T(8,128)(2,1)} %cotangent.1), custom_call_target="tpu_custom_call" | custom-call | tf_op jit(solution)/shard_map/dispatch/pallas_call | solution.py:121
  4.6 0.0 copy-start.3
  4.6 7.8 %all-to-all-start = ((bf16[16,40,2048]{2,1,0:T(8,128)(2,1)}), bf16[16,40,2048]{2,1,0:T(8,128)(2,1)}, u32[]{:S(2)}, u32[]{:S(2)}) async-start(bf16[16,40,2048]{2,1,0:T(8,128)(2,1)} %get-tuple-element.24), calls=%async_computation | async-start | bytes 5242880 | tf_op jit(solution)/shard_map/all_to_all | solution.py:384
  12.4 47.3 %all-gather.2 = f16[4352,384]{1,0:T(8,128)(2,1)S(1)} all-gather(f16[136,384]{1,0:T(8,128)(2,1)S(1)} %convert_element_type.95), channel_id=2, replica_groups=mesh['dp'=32,'expert'=16] {'dp'}, dimensions={0}, use_global_device_ids=true | all-gather | bytes 3446784 | tf_op jit(solution)/shard_map/all_gather | solution.py:383
  59.7 0.6 convert_element_type.124
  60.3 0.4 decode.1.weights
  60.7 0.1 pad_add_fusion.place
  60.8 0.0 all-to-all-done.received
  60.8 5.4 %expert.1 = (bf16[288,384]{1,0:T(8,128)(2,1)S(1)}, bf16[288,384]{1,0:T(8,128)(2,1)S(1)}, bf16[4,4,64,768]{3,2,1,0:T(8,128)(2,1)S(1)}, bf16[4,4,64,768]{3,2,1,0:T(8,128)(2,1)S(1)}) custom-call(s32[2]{0:T(128)S(1)} %pad_add_fusion.place, bf16[16,40,2048]{2,1,0:T(8,128)(2,1)} %all-to-all-done.received, bf16[2048,768]{1,0:T(8,128)(2,1)S(1)} %decode.1.weights), custom_call_target="tpu_custom_call" | custom-call | tf_op jit(solution)/shard_map/expert/pallas_call | solution.py:234
  66.2 2.1 %collective-permute-start = (bf16[4,4,64,768]{3,2,1,0:T(8,128)(2,1)S(1)}, bf16[4,4,64,768]{3,2,1,0:T(8,128)(2,1)S(1)}, u32[]{:S(2)}, u32[]{:S(2)}) collective-permute-start(bf16[4,4,64,768]{3,2,1,0:T(8,128)(2,1)S(1)} %get-tuple-element.27), channel_id=1, source_target_pairs={{0,16},{16,0},{32,48},{48,32},{64,80},{80,64},{96,112},{112,96},{1... | collective-permute-start | bytes 4718600 | tf_op jit(solution)/shard_map/ppermute | solution.py:379
  68.3 1.6 %returns.1 = bf16[16,72,1024]{2,1,0:T(8,128)(2,1)S(1)} custom-call(bf16[288,384]{1,0:T(8,128)(2,1)S(1)} %get-tuple-element.28.act, bf16[288,384]{1,0:T(8,128)(2,1)S(1)} %get-tuple-element.29.dh, bf16[2048,768]{1,0:T(8,128)(2,1)S(1)} %decode.1.weights), custom_call_target="tpu_custom_call" | custom-call | flops 49999998976 | bytes 1000000 | tf_op jit(solution)/shard_map/returns/pallas_call | solution.py:278
  69.9 1.6 %collective-permute-done = bf16[4,4,64,768]{3,2,1,0:T(8,128)(2,1)S(1)} collective-permute-done((bf16[4,4,64,768]{3,2,1,0:T(8,128)(2,1)S(1)}, bf16[4,4,64,768]{3,2,1,0:T(8,128)(2,1)S(1)}, u32[]{:S(2)}, u32[]{:S(2)}) %collective-permute-start) | collective-permute-done | bytes 1572896 | tf_op jit(solution)/shard_map/ppermute | solution.py:379
  71.5 1.3 %fusion.1 = (bf16[4,64,768]{2,1,0:T(8,128)(2,1)}, bf16[4,64,768]{2,1,0:T(8,128)(2,1)}, bf16[4,64,768]{2,1,0:T(8,128)(2,1)}, f32[4,64,768]{2,1,0:T(8,128)S(1)}) fusion(bf16[4,4,64,768]{3,2,1,0:T(8,128)(2,1)S(1)} %collective-permute-done, bf16[4,4,64,768]{3,2,1,0:T(8,128)(2,1)S(1)} %get-tuple-element.26), kind=kLoop, calls=%fused_computation.6 | loop fusion | flops 2949120 | bytes 5111808 | tf_op jit(solution)/shard_map/convert_element_type | solution.py:403
  72.8 3.6 %collective-permute-start.1 = (bf16[4,64,768]{2,1,0:T(8,128)(2,1)}, bf16[4,64,768]{2,1,0:T(8,128)(2,1)S(1)}, u32[]{:S(2)}, u32[]{:S(2)}) collective-permute-start(bf16[4,64,768]{2,1,0:T(8,128)(2,1)} %get-tuple-element.46), channel_id=1, source_target_pairs={{0,64},{16,464},{32,96},{48,496},{64,128},{80,16},{96,160},{112,48... | collective-permute-start | bytes 1179656 | tf_op jit(solution)/shard_map/ppermute | solution.py:379
  76.3 6.8 %all-to-all-start.1 = ((bf16[16,72,1024]{2,1,0:T(8,128)(2,1)}), bf16[16,72,1024]{2,1,0:T(8,128)(2,1)S(1)}, u32[]{:S(2)}, u32[]{:S(2)}) async-start(bf16[16,72,1024]{2,1,0:T(8,128)(2,1)} %copy-done), calls=%async_computation.1 | async-start | bytes 4718592 | tf_op jit(solution)/shard_map/all_to_all | solution.py:410
  83.1 2.6 %collective-permute-start.2 = (bf16[4,64,768]{2,1,0:T(8,128)(2,1)}, bf16[4,64,768]{2,1,0:T(8,128)(2,1)S(1)}, u32[]{:S(2)}, u32[]{:S(2)}) collective-permute-start(bf16[4,64,768]{2,1,0:T(8,128)(2,1)} %get-tuple-element.44), channel_id=1, source_target_pairs={{0,32},{16,496},{32,64},{48,16},{64,96},{80,48},{96,128},{112,80},... | collective-permute-start | bytes 1179656 | tf_op jit(solution)/shard_map/ppermute | solution.py:379
  85.7 2.7 %collective-permute-start.3 = (bf16[4,64,768]{2,1,0:T(8,128)(2,1)}, bf16[4,64,768]{2,1,0:T(8,128)(2,1)S(1)}, u32[]{:S(2)}, u32[]{:S(2)}) collective-permute-start(bf16[4,64,768]{2,1,0:T(8,128)(2,1)} %get-tuple-element.45), channel_id=1, source_target_pairs={{0,480},{16,48},{32,0},{48,80},{64,32},{80,112},{96,64},{112,144},... | collective-permute-start | bytes 1179656 | tf_op jit(solution)/shard_map/ppermute | solution.py:379
  88.4 0.0 collective-permute-done.1.two
  88.4 0.1 partial_sum.1
  88.5 0.0 copy-start.2
  88.5 0.0 copy-start.1
  88.5 5.5 %collective-permute-done.2 = bf16[4,64,768]{2,1,0:T(8,128)(2,1)S(1)} collective-permute-done((bf16[4,64,768]{2,1,0:T(8,128)(2,1)}, bf16[4,64,768]{2,1,0:T(8,128)(2,1)S(1)}, u32[]{:S(2)}, u32[]{:S(2)}) %collective-permute-start.2) | collective-permute-done | bytes 393248 | tf_op jit(solution)/shard_map/ppermute | solution.py:379
  94.0 3.9 %collective-permute-done.3 = bf16[4,64,768]{2,1,0:T(8,128)(2,1)S(1)} collective-permute-done((bf16[4,64,768]{2,1,0:T(8,128)(2,1)}, bf16[4,64,768]{2,1,0:T(8,128)(2,1)S(1)}, u32[]{:S(2)}, u32[]{:S(2)}) %collective-permute-start.3) | collective-permute-done | bytes 393248 | tf_op jit(solution)/shard_map/ppermute | solution.py:379
  97.9 0.1 add_convert_fusion
  98.1 7.0 %collective-permute-start.6 = (bf16[64,768]{1,0:T(8,128)(2,1)S(1)}, bf16[64,768]{1,0:T(8,128)(2,1)S(1)}, u32[]{:S(2)}, u32[]{:S(2)}) collective-permute-start(bf16[64,768]{1,0:T(8,128)(2,1)S(1)} %get-tuple-element.51), channel_id=1, source_target_pairs={{0,256},{16,272},{32,288},{48,304},{64,320},{80,336},{96,352},{112... | collective-permute-start | bytes 294920 | tf_op jit(solution)/shard_map/ppermute | solution.py:379
  105.1 4.8 %collective-permute-start.5 = (bf16[64,768]{1,0:T(8,128)(2,1)S(1)}, bf16[64,768]{1,0:T(8,128)(2,1)S(1)}, u32[]{:S(2)}, u32[]{:S(2)}) collective-permute-start(bf16[64,768]{1,0:T(8,128)(2,1)S(1)} %get-tuple-element.52), channel_id=1, source_target_pairs={{0,384},{16,144},{32,416},{48,176},{64,448},{80,208},{96,480},{112... | collective-permute-start | bytes 294920 | tf_op jit(solution)/shard_map/ppermute | solution.py:379
  109.9 4.4 %collective-permute-start.4 = (bf16[64,768]{1,0:T(8,128)(2,1)S(1)}, bf16[64,768]{1,0:T(8,128)(2,1)S(1)}, u32[]{:S(2)}, u32[]{:S(2)}) collective-permute-start(bf16[64,768]{1,0:T(8,128)(2,1)S(1)} %get-tuple-element.53), channel_id=1, source_target_pairs={{0,128},{16,400},{32,160},{48,432},{64,192},{80,464},{96,224},{112... | collective-permute-start | bytes 294920 | tf_op jit(solution)/shard_map/ppermute | solution.py:379
  114.3 0.3 tables.1
  114.6 6.4 %all-to-all-done.1.back = bf16[16,72,1024]{2,1,0:T(8,128)(2,1)S(1)} async-done(((bf16[16,72,1024]{2,1,0:T(8,128)(2,1)}), bf16[16,72,1024]{2,1,0:T(8,128)(2,1)S(1)}, u32[]{:S(2)}, u32[]{:S(2)}) %all-to-all-start.1) | async-done | bytes 2359328 | tf_op jit(solution)/shard_map/all_to_all | solution.py:410
  121.0 1.9 %combine.1 = (bf16[128,2048]{1,0:T(8,128)(2,1)}, bf16[128,2048]{1,0:T(8,128)(2,1)}) custom-call(bf16[384,256]{1,0:T(8,128)(2,1)S(1)} %get-tuple-element.32.in_body, bf16[2,384,128]{2,1,0:T(8,128)(2,1)S(1)} %get-tuple-element.33.in_over, f32[2,128]{1,0:T(2,128)S(1)} %bitcast.27, bf16[16,72,1024]{2,1,0:T(8,128)(2,1)S(1)} %all-to-all-done.1.back), custom_call_target="tpu_custom_call" | custom-call | tf_op jit(solution)/shard_map/combine/pallas_call | solution.py:347
  122.9 0.0 collective-permute-done.6
  122.9 0.7 fusion.4
  (9 shorter events, 0.1 us)
Async XLA Ops:
  4.6 7.8 %copy-start.3 = (bf16[136,384]{1,0:T(8,128)(2,1)S(1)}, bf16[136,384]{1,0:T(8,128)(2,1)}, u32[]{:S(2)}) copy-start(bf16[136,384]{1,0:T(8,128)(2,1)} %get-tuple-element.25) | copy-start | bytes 313348
  4.6 56.2 %all-to-all-start = ((bf16[16,40,2048]{2,1,0:T(8,128)(2,1)}), bf16[16,40,2048]{2,1,0:T(8,128)(2,1)}, u32[]{:S(2)}, u32[]{:S(2)}) async-start(bf16[16,40,2048]{2,1,0:T(8,128)(2,1)} %get-tuple-element.24), calls=%async_computation | async-start | bytes 5242880 | tf_op jit(solution)/shard_map/all_to_all | solution.py:384
  66.2 5.3 %collective-permute-start = (bf16[4,4,64,768]{3,2,1,0:T(8,128)(2,1)S(1)}, bf16[4,4,64,768]{3,2,1,0:T(8,128)(2,1)S(1)}, u32[]{:S(2)}, u32[]{:S(2)}) collective-permute-start(bf16[4,4,64,768]{3,2,1,0:T(8,128)(2,1)S(1)} %get-tuple-element.27), channel_id=1, source_target_pairs={{0,16},{16,0},{32,48},{48,32},{64,80},{80,64},{96,112},{112,96},{1... | collective-permute-start | bytes 4718600 | tf_op jit(solution)/shard_map/ppermute | solution.py:379
  69.9 2.9 %copy-start = (bf16[16,72,1024]{2,1,0:T(8,128)(2,1)}, bf16[16,72,1024]{2,1,0:T(8,128)(2,1)S(1)}, u32[]{:S(2)}) copy-start(bf16[16,72,1024]{2,1,0:T(8,128)(2,1)S(1)} %returns.1) | copy-start | bytes 7077892
  72.8 15.6 %collective-permute-start.1 = (bf16[4,64,768]{2,1,0:T(8,128)(2,1)}, bf16[4,64,768]{2,1,0:T(8,128)(2,1)S(1)}, u32[]{:S(2)}, u32[]{:S(2)}) collective-permute-start(bf16[4,64,768]{2,1,0:T(8,128)(2,1)} %get-tuple-element.46), channel_id=1, source_target_pairs={{0,64},{16,464},{32,96},{48,496},{64,128},{80,16},{96,160},{112,48... | collective-permute-start | bytes 1179656 | tf_op jit(solution)/shard_map/ppermute | solution.py:379
  76.3 44.7 %all-to-all-start.1 = ((bf16[16,72,1024]{2,1,0:T(8,128)(2,1)}), bf16[16,72,1024]{2,1,0:T(8,128)(2,1)S(1)}, u32[]{:S(2)}, u32[]{:S(2)}) async-start(bf16[16,72,1024]{2,1,0:T(8,128)(2,1)} %copy-done), calls=%async_computation.1 | async-start | bytes 4718592 | tf_op jit(solution)/shard_map/all_to_all | solution.py:410
  83.1 10.9 %collective-permute-start.2 = (bf16[4,64,768]{2,1,0:T(8,128)(2,1)}, bf16[4,64,768]{2,1,0:T(8,128)(2,1)S(1)}, u32[]{:S(2)}, u32[]{:S(2)}) collective-permute-start(bf16[4,64,768]{2,1,0:T(8,128)(2,1)} %get-tuple-element.44), channel_id=1, source_target_pairs={{0,32},{16,496},{32,64},{48,16},{64,96},{80,48},{96,128},{112,80},... | collective-permute-start | bytes 1179656 | tf_op jit(solution)/shard_map/ppermute | solution.py:379
  85.7 12.2 %collective-permute-start.3 = (bf16[4,64,768]{2,1,0:T(8,128)(2,1)}, bf16[4,64,768]{2,1,0:T(8,128)(2,1)S(1)}, u32[]{:S(2)}, u32[]{:S(2)}) collective-permute-start(bf16[4,64,768]{2,1,0:T(8,128)(2,1)} %get-tuple-element.45), channel_id=1, source_target_pairs={{0,480},{16,48},{32,0},{48,80},{64,32},{80,112},{96,64},{112,144},... | collective-permute-start | bytes 1179656 | tf_op jit(solution)/shard_map/ppermute | solution.py:379
  88.5 25.8 %copy-start.2 = (s32[128,2]{0,1:T(2,128)S(1)}, s32[128,2]{0,1:T(2,128)}, u32[]{:S(2)}) copy-start(s32[128,2]{0,1:T(2,128)} %param.7) | copy-start | bytes 3076
  88.5 32.5 %copy-start.1 = (f32[128,2]{0,1:T(2,128)S(1)}, f32[128,2]{0,1:T(2,128)}, u32[]{:S(2)}) copy-start(f32[128,2]{0,1:T(2,128)} %param.8) | copy-start | bytes 3076
  98.1 24.8 %collective-permute-start.6 = (bf16[64,768]{1,0:T(8,128)(2,1)S(1)}, bf16[64,768]{1,0:T(8,128)(2,1)S(1)}, u32[]{:S(2)}, u32[]{:S(2)}) collective-permute-start(bf16[64,768]{1,0:T(8,128)(2,1)S(1)} %get-tuple-element.51), channel_id=1, source_target_pairs={{0,256},{16,272},{32,288},{48,304},{64,320},{80,336},{96,352},{112... | collective-permute-start | bytes 294920 | tf_op jit(solution)/shard_map/ppermute | solution.py:379
  105.1 17.8 %collective-permute-start.5 = (bf16[64,768]{1,0:T(8,128)(2,1)S(1)}, bf16[64,768]{1,0:T(8,128)(2,1)S(1)}, u32[]{:S(2)}, u32[]{:S(2)}) collective-permute-start(bf16[64,768]{1,0:T(8,128)(2,1)S(1)} %get-tuple-element.52), channel_id=1, source_target_pairs={{0,384},{16,144},{32,416},{48,176},{64,448},{80,208},{96,480},{112... | collective-permute-start | bytes 294920 | tf_op jit(solution)/shard_map/ppermute | solution.py:379
  109.9 13.0 %collective-permute-start.4 = (bf16[64,768]{1,0:T(8,128)(2,1)S(1)}, bf16[64,768]{1,0:T(8,128)(2,1)S(1)}, u32[]{:S(2)}, u32[]{:S(2)}) collective-permute-start(bf16[64,768]{1,0:T(8,128)(2,1)S(1)} %get-tuple-element.53), channel_id=1, source_target_pairs={{0,128},{16,400},{32,160},{48,432},{64,192},{80,464},{96,224},{112... | collective-permute-start | bytes 294920 | tf_op jit(solution)/shard_map/ppermute | solution.py:379
